TPU v7x, 32 devices: a whole 2x2x4 slice. The times are simulated.
32 devices in a mesh: fsdp: 4 (over y, x), ctx: 8 (over z, core).
Axes of the slice: x: 2, y: 2, z: 4, core: 2. Of those that a mesh axis runs over, the one named last changes fastest.
Arguments:
- hidden_in: bfloat16 [2, 8192, 2048], P(None, ('fsdp', 'ctx')), may hold values from -6 to 6
- segment_ids: int32 [2, 8192], P(None, ('fsdp', 'ctx')), may hold values from 0 to 2, as said below
- positions: int32 [2, 8192], P(None, ('fsdp', 'ctx')), may hold values from 0 to 1535, as said below
- norm1_gain: bfloat16 [2048], P('fsdp'), may hold values from 0.5 to 1.5
- norm1_bias: bfloat16 [2048], P('fsdp'), may hold values from -3 to 3
- query_weight: bfloat16 [2048, 2048], P('fsdp'), may hold values from -0.125 to 0.125
- query_bias: bfloat16 [2048], P('fsdp'), may hold values from -4 to 4
- keyval_weight: bfloat16 [2048, 256], P('fsdp'), may hold values from -0.125 to 0.125
- value_bias: bfloat16 [128], P('fsdp'), may hold values from -0.75 to 0.75
- out_weight: bfloat16 [2048, 2048], P('fsdp'), may hold values from -1.5 to 1.5
- out_bias: bfloat16 [2048], P('fsdp'), may hold values from -3 to 3
- norm2_gain: bfloat16 [2048], P('fsdp'), may hold values from 0.5 to 1.5
- norm2_bias: bfloat16 [2048], P('fsdp'), may hold values from -3 to 3
- fc_weight: bfloat16 [2048, 8192], P('fsdp'), may hold values from -0.125 to 0.125
- fc_bias: bfloat16 [8192], P('fsdp'), may hold values from -4 to 4
- proj_weight: bfloat16 [8192, 2048], P('fsdp'), may hold values from -0.0625 to 0.0625
- proj_bias: bfloat16 [2048], P('fsdp'), may hold values from -3 to 3
- out_grad: bfloat16 [2, 8192, 2048], P(None, ('fsdp', 'ctx')), may hold values from -6 to 6
Outputs:
- hidden_out: bfloat16 [2, 8192, 2048], P(None, ('fsdp', 'ctx'))
- hidden_grad: float32 [2, 8192, 2048], P(None, ('fsdp', 'ctx'))
- norm1_gain_grad: float32 [2048], P('fsdp')
- norm1_bias_grad: float32 [2048], P('fsdp')
- query_weight_grad: float32 [2048, 2048], P('fsdp')
- query_bias_grad: float32 [2048], P('fsdp')
- keyval_weight_grad: float32 [2048, 256], P('fsdp')
- value_bias_grad: float32 [128], P('fsdp')
- out_weight_grad: float32 [2048, 2048], P('fsdp')
- out_bias_grad: float32 [2048], P('fsdp')
- norm2_gain_grad: float32 [2048], P('fsdp')
- norm2_bias_grad: float32 [2048], P('fsdp')
- fc_weight_grad: float32 [2048, 8192], P('fsdp')
- fc_bias_grad: float32 [8192], P('fsdp')
- proj_weight_grad: float32 [8192, 2048], P('fsdp')
- proj_bias_grad: float32 [2048], P('fsdp')
Inputs may be any that keep to these rules, and one draw needn't show every extreme that they name: `segment_ids`: in each group of 2048 consecutive tokens of a micro-batch, segment 0 holds positions 0 to 1023 once each and each segment k of 1 to 2 holds positions 1024 to 1535 once each. Tokens come in aligned runs of 64 consecutive positions of one segment; a group's first run is positions 0 to 63 of the prompt and its last run is the prompt's last 64 positions; the other runs are in any order. `positions`: as stated for segment_ids.
All inputs are finite; a program needn't handle non-finite values.
Results may differ from a plain program's by a relative error of at most 0.015.
Values may be sent and summed in bfloat16 or wider, within the bound.
A program may use at most 448 MiB of HBM per device.

v0:
```python
import math

import jax
import jax.numpy as jnp
from jax import lax
from jax.sharding import PartitionSpec as P

D = 2048
HEADS = 16
HD = 128


def layer_norm(values, gain, shift):
    center = jnp.mean(values, axis=-1, keepdims=True)
    shifted = values - center
    spread = jnp.mean(shifted * shifted, axis=-1, keepdims=True)
    return shifted * lax.rsqrt(spread + 1e-05) * gain + shift


def gelu_tanh(values):
    return jax.nn.gelu(values, approximate=True)


def fetch_attention(
    norm1_gain,
    norm1_bias,
    query_weight,
    query_bias,
    keyval_weight,
    value_bias,
    out_weight,
    out_bias,
):
    return (
        lax.all_gather(norm1_gain, "fsdp", axis=0, tiled=True),
        lax.all_gather(norm1_bias, "fsdp", axis=0, tiled=True),
        lax.all_gather(query_weight, "fsdp", axis=0, tiled=True),
        lax.all_gather(query_bias, "fsdp", axis=0, tiled=True),
        lax.all_gather(keyval_weight, "fsdp", axis=0, tiled=True),
        lax.all_gather(value_bias, "fsdp", axis=0, tiled=True),
        lax.all_gather(out_weight, "fsdp", axis=0, tiled=True),
        lax.all_gather(out_bias, "fsdp", axis=0, tiled=True),
    )


def fetch_feedforward(norm2_gain, norm2_bias, fc_weight, fc_bias, proj_weight, proj_bias):
    return (
        lax.all_gather(norm2_gain, "fsdp", axis=0, tiled=True),
        lax.all_gather(norm2_bias, "fsdp", axis=0, tiled=True),
        lax.all_gather(fc_weight, "fsdp", axis=0, tiled=True),
        lax.all_gather(fc_bias, "fsdp", axis=0, tiled=True),
        lax.all_gather(proj_weight, "fsdp", axis=0, tiled=True),
        lax.all_gather(proj_bias, "fsdp", axis=0, tiled=True),
    )


def sum_attention(terms):
    return (
        lax.psum_scatter(terms[0], ("fsdp", "ctx"), scatter_dimension=0, tiled=True),
        lax.psum_scatter(terms[1], ("fsdp", "ctx"), scatter_dimension=0, tiled=True),
        lax.psum_scatter(terms[2], ("fsdp", "ctx"), scatter_dimension=0, tiled=True),
        lax.psum_scatter(terms[3], ("fsdp", "ctx"), scatter_dimension=0, tiled=True),
        lax.psum_scatter(terms[4], ("fsdp", "ctx"), scatter_dimension=0, tiled=True),
        lax.psum_scatter(terms[5], ("fsdp", "ctx"), scatter_dimension=0, tiled=True),
        lax.psum_scatter(terms[6], ("fsdp", "ctx"), scatter_dimension=0, tiled=True),
        lax.psum_scatter(terms[7], ("fsdp", "ctx"), scatter_dimension=0, tiled=True),
    )


def sum_feedforward(terms):
    return (
        lax.psum_scatter(terms[0], ("fsdp", "ctx"), scatter_dimension=0, tiled=True),
        lax.psum_scatter(terms[1], ("fsdp", "ctx"), scatter_dimension=0, tiled=True),
        lax.psum_scatter(terms[2], ("fsdp", "ctx"), scatter_dimension=0, tiled=True),
        lax.psum_scatter(terms[3], ("fsdp", "ctx"), scatter_dimension=0, tiled=True),
        lax.psum_scatter(terms[4], ("fsdp", "ctx"), scatter_dimension=0, tiled=True),
        lax.psum_scatter(terms[5], ("fsdp", "ctx"), scatter_dimension=0, tiled=True),
    )


def attend_forward(queries, keys, values, visible, head_block, scale):
    pieces = []
    lse_parts = []
    for start in range(0, HEADS, head_block):
        query_block = queries[:, start : start + head_block]
        scores = (
            jnp.einsum("qhd,kd->hqk", query_block, keys, preferred_element_type=jnp.float32) * scale
        )
        scores = jnp.where(visible[None], scores, -1e30)
        peak = jnp.max(scores, axis=-1, keepdims=True)
        expo = jnp.exp(scores - peak)
        total = jnp.sum(expo, axis=-1, keepdims=True)
        probs = expo / total
        lse_parts.append(peak[..., 0] + jnp.log(total[..., 0]))
        pieces.append(
            jnp.einsum(
                "hqk,kd->qhd",
                probs.astype(jnp.bfloat16),
                values,
                preferred_element_type=jnp.float32,
            )
        )
    return (jnp.concatenate(pieces, axis=1), jnp.concatenate(lse_parts, axis=0))


def attend_backward(queries, keys, values, visible, lse_rows, grad_mixed, head_block, scale):
    query_grads = []
    key_grad = jnp.zeros((keys.shape[0], HD), jnp.float32)
    value_grad = jnp.zeros((keys.shape[0], HD), jnp.float32)
    for start in range(0, HEADS, head_block):
        query_block = queries[:, start : start + head_block]
        grad_block = grad_mixed[:, start : start + head_block]
        scores = (
            jnp.einsum("qhd,kd->hqk", query_block, keys, preferred_element_type=jnp.float32) * scale
        )
        scores = jnp.where(visible[None], scores, -1e30)
        probs = jnp.exp(scores - lse_rows[start : start + head_block][..., None])
        grad_probs = jnp.einsum(
            "qhd,kd->hqk", grad_block, values, preferred_element_type=jnp.float32
        )
        inner = jnp.sum(probs * grad_probs, axis=-1, keepdims=True)
        grad_scores = (probs * (grad_probs - inner)).astype(jnp.bfloat16)
        query_grads.append(
            jnp.einsum("hqk,kd->qhd", grad_scores, keys, preferred_element_type=jnp.float32) * scale
        )
        key_grad = (
            key_grad
            + jnp.einsum(
                "hqk,qhd->kd", grad_scores, query_block, preferred_element_type=jnp.float32
            )
            * scale
        )
        value_grad = value_grad + jnp.einsum(
            "hqk,qhd->kd",
            probs.astype(jnp.bfloat16),
            grad_block,
            preferred_element_type=jnp.float32,
        )
    return (jnp.concatenate(query_grads, axis=1), key_grad, value_grad)


def joined(pieces):
    return jnp.concatenate(pieces, axis=0)


def per_device(
    hidden_in,
    segment_ids,
    positions,
    norm1_gain,
    norm1_bias,
    query_weight,
    query_bias,
    keyval_weight,
    value_bias,
    out_weight,
    out_bias,
    norm2_gain,
    norm2_bias,
    fc_weight,
    fc_bias,
    proj_weight,
    proj_bias,
    out_grad,
):
    micro_count = hidden_in.shape[0]
    tok_rows = hidden_in.shape[1]
    scale = 1.0 / math.sqrt(HD)
    head_block = 1
    while head_block * tok_rows < 512 and head_block < HEADS:
        head_block = head_block * 2
    seg_group, pos_group = (
        lax.all_gather(segment_ids, "ctx", axis=1, tiled=True),
        lax.all_gather(positions, "ctx", axis=1, tiled=True),
    )
    attn_fixed = fetch_attention(
        norm1_gain,
        norm1_bias,
        query_weight,
        query_bias,
        keyval_weight,
        value_bias,
        out_weight,
        out_bias,
    )
    ffn_fixed = fetch_feedforward(
        norm2_gain, norm2_bias, fc_weight, fc_bias, proj_weight, proj_bias
    )
    results = []
    input_grads = []
    kept_active = []
    kept_cot = []
    kept_normed2 = []
    kept_before = []
    kept_mixed = []
    kept_branch = []
    kept_normed1 = []
    kept_queries = []
    kept_keyvals = []
    small_sums = None
    for micro_index in range(micro_count):
        gain_one, shift_one, w_query, b_query, w_keyval, b_value, w_out, b_out = attn_fixed
        gain_one = gain_one.astype(jnp.float32)
        shift_one = shift_one.astype(jnp.float32)
        hidden = hidden_in[micro_index].astype(jnp.float32)
        normed1 = layer_norm(hidden, gain_one, shift_one).astype(jnp.bfloat16)
        queries = (
            jnp.dot(normed1, w_query, preferred_element_type=jnp.float32)
            + b_query.astype(jnp.float32)
        ).astype(jnp.bfloat16)
        kv_bias = jnp.concatenate([jnp.zeros((HD,), jnp.float32), b_value.astype(jnp.float32)])
        keyvals = (jnp.dot(normed1, w_keyval, preferred_element_type=jnp.float32) + kv_bias).astype(
            jnp.bfloat16
        )
        group_kv = lax.all_gather(keyvals, "ctx", axis=0, tiled=True)
        keys_all = group_kv[:, :HD]
        values_all = group_kv[:, HD:]
        seg_here = segment_ids[micro_index]
        pos_here = positions[micro_index]
        seg_all = seg_group[micro_index]
        pos_all = pos_group[micro_index]
        visible = (pos_all[None, :] <= pos_here[:, None]) & (
            (seg_all[None, :] == 0) | (seg_all[None, :] == seg_here[:, None])
        )
        head_queries = queries.reshape(tok_rows, HEADS, HD)
        attn_out, lse_rows = attend_forward(
            head_queries, keys_all, values_all, visible, head_block, scale
        )
        mixed = attn_out.reshape(tok_rows, D).astype(jnp.bfloat16)
        middle = (
            hidden
            + jnp.dot(mixed, w_out, preferred_element_type=jnp.float32)
            + b_out.astype(jnp.float32)
        )
        gain_two, shift_two, w_fc, b_fc, w_proj, b_proj = ffn_fixed
        gain_two = gain_two.astype(jnp.float32)
        shift_two = shift_two.astype(jnp.float32)
        normed2 = layer_norm(middle, gain_two, shift_two).astype(jnp.bfloat16)
        before = jnp.dot(normed2, w_fc, preferred_element_type=jnp.float32) + b_fc.astype(
            jnp.float32
        )
        active = gelu_tanh(before).astype(jnp.bfloat16)
        result = (
            middle
            + jnp.dot(active, w_proj, preferred_element_type=jnp.float32)
            + b_proj.astype(jnp.float32)
        )
        results.append(result.astype(jnp.bfloat16))
        cotangent = out_grad[micro_index]
        d_active = jnp.einsum("td,fd->tf", cotangent, w_proj, preferred_element_type=jnp.float32)
        gelu_pull = jax.vjp(gelu_tanh, before)[1]
        d_before = gelu_pull(d_active)[0].astype(jnp.bfloat16)
        d_normed2 = jnp.einsum("tf,df->td", d_before, w_fc, preferred_element_type=jnp.float32)
        norm_pull = jax.vjp(layer_norm, middle, gain_two, shift_two)[1]
        d_middle_norm, gain_two_grad, shift_two_grad = norm_pull(d_normed2)
        d_middle = cotangent.astype(jnp.float32) + d_middle_norm
        d_branch = d_middle.astype(jnp.bfloat16)
        d_mixed = jnp.einsum(
            "te,de->td", d_branch, w_out, preferred_element_type=jnp.float32
        ).astype(jnp.bfloat16)
        grad_queries, key_grad, value_grad = attend_backward(
            head_queries,
            keys_all,
            values_all,
            visible,
            lse_rows,
            d_mixed.reshape(tok_rows, HEADS, HD),
            head_block,
            scale,
        )
        kv_terms = jnp.concatenate([key_grad, value_grad], axis=1)
        d_keyvals = lax.psum_scatter(
            kv_terms.astype(jnp.bfloat16), "ctx", scatter_dimension=0, tiled=True
        )
        d_queries = grad_queries.reshape(tok_rows, D).astype(jnp.bfloat16)
        d_normed1 = jnp.einsum(
            "te,de->td", d_queries, w_query, preferred_element_type=jnp.float32
        ) + jnp.einsum("te,de->td", d_keyvals, w_keyval, preferred_element_type=jnp.float32)
        first_pull = jax.vjp(layer_norm, hidden, gain_one, shift_one)[1]
        d_hidden_norm, gain_one_grad, shift_one_grad = first_pull(d_normed1)
        input_grads.append(d_middle + d_hidden_norm)
        small_terms = (gain_one_grad, shift_one_grad, gain_two_grad, shift_two_grad)
        if small_sums is None:
            small_sums = small_terms
        else:
            small_sums = jax.tree.map(jnp.add, small_sums, small_terms)
        kept_active.append(active)
        kept_cot.append(cotangent)
        kept_normed2.append(normed2)
        kept_before.append(d_before)
        kept_mixed.append(mixed)
        kept_branch.append(d_branch)
        kept_normed1.append(normed1)
        kept_queries.append(d_queries)
        kept_keyvals.append(d_keyvals)
    all_cot = joined(kept_cot)
    all_before = joined(kept_before)
    all_branch = joined(kept_branch)
    all_queries = joined(kept_queries)
    all_keyvals = joined(kept_keyvals)
    all_normed1 = joined(kept_normed1)
    proj_w_grad = jnp.einsum(
        "tf,td->fd", joined(kept_active), all_cot, preferred_element_type=jnp.float32
    )
    proj_b_grad = jnp.sum(all_cot.astype(jnp.float32), axis=0)
    fc_w_grad = jnp.einsum(
        "td,tf->df", joined(kept_normed2), all_before, preferred_element_type=jnp.float32
    )
    fc_b_grad = jnp.sum(all_before.astype(jnp.float32), axis=0)
    ffn_total = sum_feedforward(
        (small_sums[2], small_sums[3], fc_w_grad, fc_b_grad, proj_w_grad, proj_b_grad)
    )
    out_w_grad = jnp.einsum(
        "td,te->de", joined(kept_mixed), all_branch, preferred_element_type=jnp.float32
    )
    out_b_grad = jnp.sum(all_branch.astype(jnp.float32), axis=0)
    query_w_grad = jnp.einsum(
        "td,te->de", all_normed1, all_queries, preferred_element_type=jnp.float32
    )
    query_b_grad = jnp.sum(all_queries.astype(jnp.float32), axis=0)
    keyval_w_grad = jnp.einsum(
        "td,te->de", all_normed1, all_keyvals, preferred_element_type=jnp.float32
    )
    value_b_grad = jnp.sum(all_keyvals[:, HD:].astype(jnp.float32), axis=0)
    attn_total = sum_attention(
        (
            small_sums[0],
            small_sums[1],
            query_w_grad,
            query_b_grad,
            keyval_w_grad,
            value_b_grad,
            out_w_grad,
            out_b_grad,
        )
    )
    grads = (
        lax.all_gather(attn_total[0].astype(jnp.bfloat16), "ctx", axis=0, tiled=True).astype(
            jnp.float32
        ),
        lax.all_gather(attn_total[1].astype(jnp.bfloat16), "ctx", axis=0, tiled=True).astype(
            jnp.float32
        ),
        lax.all_gather(attn_total[2].astype(jnp.bfloat16), "ctx", axis=0, tiled=True).astype(
            jnp.float32
        ),
        lax.all_gather(attn_total[3].astype(jnp.bfloat16), "ctx", axis=0, tiled=True).astype(
            jnp.float32
        ),
        lax.all_gather(attn_total[4].astype(jnp.bfloat16), "ctx", axis=0, tiled=True).astype(
            jnp.float32
        ),
        lax.all_gather(attn_total[5].astype(jnp.bfloat16), "ctx", axis=0, tiled=True).astype(
            jnp.float32
        ),
        lax.all_gather(attn_total[6].astype(jnp.bfloat16), "ctx", axis=0, tiled=True).astype(
            jnp.float32
        ),
        lax.all_gather(attn_total[7].astype(jnp.bfloat16), "ctx", axis=0, tiled=True).astype(
            jnp.float32
        ),
        lax.all_gather(ffn_total[0].astype(jnp.bfloat16), "ctx", axis=0, tiled=True).astype(
            jnp.float32
        ),
        lax.all_gather(ffn_total[1].astype(jnp.bfloat16), "ctx", axis=0, tiled=True).astype(
            jnp.float32
        ),
        lax.all_gather(ffn_total[2].astype(jnp.bfloat16), "ctx", axis=0, tiled=True).astype(
            jnp.float32
        ),
        lax.all_gather(ffn_total[3].astype(jnp.bfloat16), "ctx", axis=0, tiled=True).astype(
            jnp.float32
        ),
        lax.all_gather(ffn_total[4].astype(jnp.bfloat16), "ctx", axis=0, tiled=True).astype(
            jnp.float32
        ),
        lax.all_gather(ffn_total[5].astype(jnp.bfloat16), "ctx", axis=0, tiled=True).astype(
            jnp.float32
        ),
    )
    return (
        jnp.stack(results, axis=0),
        jnp.stack(input_grads, axis=0),
        grads[0],
        grads[1],
        grads[2],
        grads[3],
        grads[4],
        grads[5],
        grads[6],
        grads[7],
        grads[8],
        grads[9],
        grads[10],
        grads[11],
        grads[12],
        grads[13],
    )


def solution(mesh):
    placed = (
        P(None, ("fsdp", "ctx"), None),
        P(None, ("fsdp", "ctx")),
        P(None, ("fsdp", "ctx")),
        P("fsdp"),
        P("fsdp"),
        P("fsdp", None),
        P("fsdp"),
        P("fsdp", None),
        P("fsdp"),
        P("fsdp", None),
        P("fsdp"),
        P("fsdp"),
        P("fsdp"),
        P("fsdp", None),
        P("fsdp"),
        P("fsdp", None),
        P("fsdp"),
        P(None, ("fsdp", "ctx"), None),
    )
    return jax.shard_map(
        per_device,
        mesh=mesh,
        in_specs=placed,
        out_specs=(
            P(None, ("fsdp", "ctx"), None),
            P(None, ("fsdp", "ctx"), None),
            P("fsdp"),
            P("fsdp"),
            P("fsdp", None),
            P("fsdp"),
            P("fsdp", None),
            P("fsdp"),
            P("fsdp", None),
            P("fsdp"),
            P("fsdp"),
            P("fsdp"),
            P("fsdp", None),
            P("fsdp"),
            P("fsdp", None),
            P("fsdp"),
        ),
        check_vma=False,
    )
```

profile of v0, /device:TPU:1, one launch (start us, length us, event | category | flops | bytes accessed | tf_op | source)
XLA Modules:
  0.0 3267.5 jit_solution(11865605644637766781)
XLA Ops:
  10.1 6.9 all-gather.1
  17.0 6.4 all-gather
  26.2 7.0 all-reduce.1
  46.4 5.7 all-gather.5
  52.7 6.1 all-gather.4
  58.8 6.3 all-gather.3
  65.2 6.1 all-gather.2
  71.3 6.1 all_gather.110
  78.1 26.7 all_gather.102
  104.8 12.7 all_gather.101
  123.2 5.4 all-gather.24.cloned.1.call-done
  128.6 5.9 fusion.227
  139.0 14.3 all-gather.32.cloned.1.call-done
  190.9 51.0 %all-gather.26.cloned.1.call-done = bf16[2048,2048]{1,0:T(8,128)(2,1)} async-done(((bf16[512,2048]{1,0:T(8,128)(2,1)}), bf16[2048,2048]{1,0:T(8,128)(2,1)}) %all-gather.26.cloned.1.call-update) | async-done | bytes 8388624 | tf_op jit(solution)/shard_map/all_gather | solution.py:41
  241.9 6.2 fusion.450
  252.1 14.3 all-gather.22.cloned.1.call-done
  315.7 249.0 %all-gather.28.cloned.1.call-done = bf16[2048,8192]{1,0:T(8,128)(2,1)} async-done(((bf16[512,8192]{1,0:T(8,128)(2,1)}), bf16[2048,8192]{1,0:T(8,128)(2,1)}) %all-gather.28.cloned.1.call-update) | async-done | bytes 33554448 | tf_op jit(solution)/shard_map/all_gather | solution.py:50
  564.7 21.6 multiply_convert_fusion.1
  586.3 21.8 multiply_convert_fusion
  608.1 255.7 %all-gather.30.cloned.1.call-done = bf16[8192,2048]{1,0:T(8,128)(2,1)} async-done(((bf16[2048,2048]{1,0:T(8,128)(2,1)}), bf16[8192,2048]{1,0:T(8,128)(2,1)}) %all-gather.30.cloned.1.call-update) | async-done | bytes 33554448 | tf_op jit(solution)/shard_map/all_gather | solution.py:52
  863.8 20.6 fusion.6
  884.4 20.8 fusion.13
  905.2 17.1 fusion.452
  922.3 19.6 multiply_reduce_fusion.1
  1060.4 8.6 fusion.228
  1070.8 9.7 fusion.185
  1082.1 29.5 fusion.18
  1114.7 31.9 fusion.14
  1150.8 126.8 %reduce-scatter.12.cloned.1.call-done = f32[64,2048]{1,0:T(8,128)} async-done(((f32[2048,2048]{1,0:T(8,128)}), f32[64,2048]{1,0:T(8,128)}) %reduce-scatter.12.cloned.1.call-update) | async-done | bytes 524304 | tf_op jit(solution)/shard_map/reduce_scatter | solution.py:61
  1279.5 185.4 %reduce-scatter.16.cloned.1.call-done = f32[64,2048]{1,0:T(8,128)} async-done(((f32[2048,2048]{1,0:T(8,128)}), f32[64,2048]{1,0:T(8,128)}) %reduce-scatter.16.cloned.1.call-update) | async-done | bytes 524304 | tf_op jit(solution)/shard_map/reduce_scatter | solution.py:65
  1466.8 707.4 %reduce-scatter.18.cloned.1.call-done = f32[64,8192]{1,0:T(8,128)} async-done(((f32[2048,8192]{1,0:T(8,128)}), f32[64,8192]{1,0:T(8,128)}) %reduce-scatter.18.cloned.1.call-update) | async-done | bytes 2097168 | tf_op jit(solution)/shard_map/reduce_scatter | solution.py:74
  2176.9 705.6 %reduce-scatter.20.cloned.1.call-done = f32[256,2048]{1,0:T(8,128)} async-done(((f32[8192,2048]{1,0:T(8,128)}), f32[256,2048]{1,0:T(8,128)}) %reduce-scatter.20.cloned.1.call-update) | async-done | bytes 2097168 | tf_op jit(solution)/shard_map/reduce_scatter | solution.py:76
  2887.3 6.2 all-gather.6
  2897.5 16.5 fusion.120
  2914.0 16.7 fusion.119
  2935.9 5.9 fusion.453
  2941.7 5.9 fusion.451
  2952.9 44.2 %all-reduce.19 = (bf16[2048]{0:T(1024)(128)(2,1)S(1)}, bf16[2048]{0:T(1024)(128)(2,1)S(1)}, bf16[2048]{0:T(1024)(128)(2,1)S(1)}, bf16[128]{0:T(256)(128)(2,1)S(1...) all-reduce(f32[2048]{0:T(1024)S(1)} %add.515, ...), channel_id=4, replica_groups=mesh['fsdp'=4,'ctx'=8] {'fsdp','ctx'}, use_global_device_ids=true, to_apply=%region_68.69.clone | all-reduce | flops 22656 | bytes 135936
  2999.4 13.9 all-reduce.20
  3018.0 9.6 all-gather.7
  3028.2 5.2 add_bitcast_fusion.1
  3036.8 15.1 all_gather.118
  3052.8 4.1 convert_element_type.456
  3056.9 25.9 all-gather.36.cloned.1.call-done
  3086.9 79.6 %all-gather.38.cloned.1.call-done = bf16[512,8192]{1,0:T(8,128)(2,1)} async-done(((bf16[64,8192]{1,0:T(8,128)(2,1)}), bf16[512,8192]{1,0:T(8,128)(2,1)}) %all-gather.38.cloned.1.call-update) | async-done | bytes 8388624 | tf_op jit(solution)/shard_map/all_gather | solution.py:368
  3166.5 12.5 convert_element_type.475
  3179.0 69.6 %all-gather.40.cloned.1.call-done = bf16[2048,2048]{1,0:T(8,128)(2,1)} async-done(((bf16[256,2048]{1,0:T(8,128)(2,1)}), bf16[2048,2048]{1,0:T(8,128)(2,1)}) %all-gather.40.cloned.1.call-update) | async-done | bytes 8388624 | tf_op jit(solution)/shard_map/all_gather | solution.py:374
  3248.7 11.7 convert_element_type.480
  (799 shorter events, 286.8 us)
Async XLA Ops:
  7.2 27.9 copy-start
  7.2 31.9 all-gather.20.cloned.1.call-start
  7.9 120.7 %all-gather.24.cloned.1.call-start = ((), (), s32[]{:S(2)}) async-start(), calls=%async_computation.9 | async-start | bytes 10485760 | tf_op jit(solution)/shard_map/all_gather | solution.py:37
  8.7 144.6 %all-gather.32.cloned.1.call-start = ((), (), s32[]{:S(2)}) async-start(), calls=%async_computation.13 | async-start | bytes 1179648 | tf_op jit(solution)/shard_map/all_gather | solution.py:215
  41.9 200.1 %all-gather.26.cloned.1.call-start = ((), (), s32[]{:S(2)}) async-start(), calls=%async_computation.10 | async-start | bytes 10485760 | tf_op jit(solution)/shard_map/all_gather | solution.py:41
  42.4 224.0 %all-gather.22.cloned.1.call-start = ((), (), s32[]{:S(2)}) async-start(), calls=%async_computation.8 | async-start | bytes 1179648 | tf_op jit(solution)/shard_map/all_gather | solution.py:215
  44.8 519.9 %all-gather.28.cloned.1.call-start = ((), (), s32[]{:S(2)}) async-start(), calls=%async_computation.11 | async-start | bytes 41943040 | tf_op jit(solution)/shard_map/all_gather | solution.py:50
  45.5 25.8 copy-start.231
  45.5 32.6 copy-start.229
  45.5 59.3 %copy-start.230 = (s32[2,256]{1,0:T(2,128)S(1)}, s32[2,256]{1,0:T(2,128)}, u32[]{:S(2)}) copy-start(s32[2,256]{1,0:T(2,128)} %param.20) | copy-start | bytes 6148
  45.5 83.1 %copy-start.112 = (bf16[256,2048]{1,0:T(8,128)(2,1)S(1)}, bf16[256,2048]{1,0:T(8,128)(2,1)}, u32[]{:S(2)}) copy-start(bf16[256,2048]{1,0:T(8,128)(2,1)} %get-tuple-element.61) | copy-start | bytes 3145732
  45.5 818.3 %all-gather.30.cloned.1.call-start = ((), (), s32[]{:S(2)}) async-start(), calls=%async_computation.12 | async-start | bytes 41943040 | tf_op jit(solution)/shard_map/all_gather | solution.py:52
  46.3 1100.4 %reduce-scatter.8.cloned.1.call-start = ((), (), s32[]{:S(2)}) async-start(), calls=%async_computation.14 | async-start | bytes 1179648 | tf_op jit(solution)/shard_map/reduce_scatter | solution.py:272
  139.0 36.4 %copy-start.118 = (bf16[256,2,128]{2,1,0:T(2,128)(2,1)}, bf16[256,2,128]{2,1,0:T(2,128)(2,1)S(1)}, u32[]{:S(2)}) copy-start(bf16[256,2,128]{2,1,0:T(2,128)(2,1)S(1)} %get-tuple-element.98) | copy-start | bytes 393220
  155.3 34.1 %copy-start.10 = (f32[2,256,2048]{1,2,0:T(8,128)}, f32[2,256,2048]{1,2,0:T(8,128)S(1)}, u32[]{:S(2)}) copy-start(f32[2,256,2048]{1,2,0:T(8,128)S(1)} %get-tuple-element.129) | copy-start | bytes 12582916
  155.3 34.1 %copy-start.193 = (f32[2,256]{1,0:T(2,128)}, f32[2,256]{1,0:T(2,128)S(1)}, u32[]{:S(2)}) copy-start(f32[2,256]{1,0:T(2,128)S(1)} %get-tuple-element.128) | copy-start | bytes 6148
  155.9 33.5 %copy-start.195 = (f32[2,256]{1,0:T(2,128)}, f32[2,256]{1,0:T(2,128)S(1)}, u32[]{:S(2)}) copy-start(f32[2,256]{1,0:T(2,128)S(1)} %fusion.82) | copy-start | bytes 6148
  158.1 29.7 copy-start.14
  158.1 29.7 copy-start.197
  158.7 29.1 copy-start.199
  161.4 24.8 copy-start.18
  252.1 36.5 %copy-start.120 = (bf16[256,2,128]{2,1,0:T(2,128)(2,1)}, bf16[256,2,128]{2,1,0:T(2,128)(2,1)S(1)}, u32[]{:S(2)}) copy-start(bf16[256,2,128]{2,1,0:T(2,128)(2,1)S(1)} %get-tuple-element.90) | copy-start | bytes 393220
  268.4 30.5 copy-start.12
  271.2 26.7 copy-start.16
  304.7 260.0 %copy-start.161 = (f32[8192]{0:T(1024)S(1)}, f32[8192]{0:T(1024)}, u32[]{:S(2)}) copy-start(f32[8192]{0:T(1024)} %convert_element_type.388) | copy-start | bytes 98308
  315.6 270.7 %copy-start.83 = (bf16[256,2048]{1,0:T(8,128)(2,1)}, bf16[256,2048]{1,0:T(8,128)(2,1)S(1)}, u32[]{:S(2)}) copy-start(bf16[256,2048]{1,0:T(8,128)(2,1)S(1)} %get-tuple-element.99) | copy-start | bytes 3145732
  315.6 270.7 %copy-start.85 = (bf16[256,2048]{1,0:T(8,128)(2,1)}, bf16[256,2048]{1,0:T(8,128)(2,1)S(1)}, u32[]{:S(2)}) copy-start(bf16[256,2048]{1,0:T(8,128)(2,1)S(1)} %get-tuple-element.100) | copy-start | bytes 3145732
  586.3 277.5 %copy-start.46 = (bf16[2,256,2048]{2,1,0:T(8,128)(2,1)S(1)}, bf16[2,256,2048]{2,1,0:T(8,128)(2,1)}, u32[]{:S(2)}) copy-start(bf16[2,256,2048]{2,1,0:T(8,128)(2,1)} %param.35) | copy-start | bytes 6291460
  905.2 42.8 %slice-start.2 = ((s8[8388608]{0:T(1024)(128)(4,1)}), s8[4194304]{0:T(1024)(128)(4,1)S(1)}, s32[]{:S(2)}) async-start(s8[8388608]{0:T(1024)(128)(4,1)} %bitcast.810), calls=%async_computation.27 | async-start | bytes 8388608
  922.3 25.7 slice-start.3
  1028.4 119.4 %reduce-scatter.10.cloned.1.call-start = ((), (), s32[]{:S(2)}) async-start(), calls=%async_computation.15 | async-start | bytes 1179648 | tf_op jit(solution)/shard_map/reduce_scatter | solution.py:272
  1045.9 231.7 %reduce-scatter.12.cloned.1.call-start = ((), (), s32[]{:S(2)}) async-start(), calls=%async_computation.16 | async-start | bytes 17301504 | tf_op jit(solution)/shard_map/reduce_scatter | solution.py:61
  1069.0 395.9 %reduce-scatter.16.cloned.1.call-start = ((), (), s32[]{:S(2)}) async-start(), calls=%async_computation.19 | async-start | bytes 17301504 | tf_op jit(solution)/shard_map/reduce_scatter | solution.py:65
  1080.6 1093.6 %reduce-scatter.18.cloned.1.call-start = ((), (), s32[]{:S(2)}) async-start(), calls=%async_computation.21 | async-start | bytes 69206016 | tf_op jit(solution)/shard_map/reduce_scatter | solution.py:74
  1111.6 1770.8 %reduce-scatter.20.cloned.1.call-start = ((), (), s32[]{:S(2)}) async-start(), calls=%async_computation.23 | async-start | bytes 69206016 | tf_op jit(solution)/shard_map/reduce_scatter | solution.py:76
  1146.6 1889.4 %reduce-scatter.14.cloned.1.call-start = ((), (), s32[]{:S(2)}) async-start(), calls=%async_computation.18 | async-start | bytes 2162688 | tf_op jit(solution)/shard_map/reduce_scatter | solution.py:63
  1150.8 1902.0 %all-gather.34.cloned.1.call-start = ((), (), s32[]{:S(2)}) async-start(), calls=%async_computation.17 | async-start | bytes 2359296 | tf_op jit(solution)/shard_map/all_gather | solution.py:344
  1279.4 1803.4 %all-gather.36.cloned.1.call-start = ((), (), s32[]{:S(2)}) async-start(), calls=%async_computation.20 | async-start | bytes 2359296 | tf_op jit(solution)/shard_map/all_gather | solution.py:356
  1466.7 1418.5 %copy-start.238 = (u32[32]{0:T(128)S(1)}, u32[32]{0:T(128)}, u32[]{:S(2)}) copy-start(u32[32]{0:T(128)} %constant.59) | copy-start | bytes 388
  1466.7 1420.6 %copy-start.236 = (bf16[512]{0:T(512)(128)(2,1)S(1)}, bf16[512]{0:T(512)(128)(2,1)}, u32[]{:S(2)}) copy-start(bf16[512]{0:T(512)(128)(2,1)} %param.34) | copy-start | bytes 3076
  1466.7 1699.8 %all-gather.38.cloned.1.call-start = ((), (), s32[]{:S(2)}) async-start(), calls=%async_computation.22 | async-start | bytes 9437184 | tf_op jit(solution)/shard_map/all_gather | solution.py:368
  2176.8 718.6 %copy-start.227 = (f32[2048]{0:T(1024)S(1)}, f32[2048]{0:T(1024)}, u32[]{:S(2)}) copy-start(f32[2048]{0:T(1024)} %get-tuple-element.22) | copy-start | bytes 24580
  2176.8 718.6 %copy-start.228 = (f32[2048]{0:T(1024)S(1)}, f32[2048]{0:T(1024)}, u32[]{:S(2)}) copy-start(f32[2048]{0:T(1024)} %get-tuple-element.109) | copy-start | bytes 24580
  2176.8 718.6 %copy-start.225 = (f32[2048]{0:T(1024)S(1)}, f32[2048]{0:T(1024)}, u32[]{:S(2)}) copy-start(f32[2048]{0:T(1024)} %get-tuple-element.30) | copy-start | bytes 24580
  2176.8 718.7 %copy-start.226 = (f32[2048]{0:T(1024)S(1)}, f32[2048]{0:T(1024)}, u32[]{:S(2)}) copy-start(f32[2048]{0:T(1024)} %get-tuple-element.107) | copy-start | bytes 24580
  2176.8 1071.8 %all-gather.40.cloned.1.call-start = ((), (), s32[]{:S(2)}) async-start(), calls=%async_computation.24 | async-start | bytes 9437184 | tf_op jit(solution)/shard_map/all_gather | solution.py:374
  2950.7 77.5 %copy-start.186 = (f32[256]{0:T(256)S(1)}, f32[256]{0:T(256)}, u32[]{:S(2)}) copy-start(f32[256]{0:T(256)} %copy-done.185) | copy-start | bytes 3076
  2950.7 77.5 %copy-start.188 = (f32[256]{0:T(256)S(1)}, f32[256]{0:T(256)}, u32[]{:S(2)}) copy-start(f32[256]{0:T(256)} %copy-done.187) | copy-start | bytes 3076
  (213 other events, 950.8 us)
Sparse Core Ops, SparseCore 0:
  9.9 28.8 all-gather.19
  40.6 87.9 all-gather.23
  130.8 22.4 all-gather.31
  155.0 86.9 all-gather.25
  244.0 22.4 all-gather.21
  268.1 296.5 all-gather.27
  566.5 297.2 all-gather.29
  1028.5 29.1 reduce-scatter.7
  1059.9 30.5 reduce-scatter.9
  1093.2 184.3 reduce-scatter.11
  1280.5 184.3 reduce-scatter.15
  1467.1 706.9 reduce-scatter.17
  2176.5 705.9 reduce-scatter.19
  2884.6 133.0 reduce-scatter.13
  3019.2 33.0 all-gather.33
  3054.4 28.3 all-gather.35
  3084.9 81.5 all-gather.37
  3168.1 80.5 all-gather.39
where the time goes:
time: 3270 us
  waiting for transfers between devices  2490 us (76%)
  matrix products  398 us (12%)
  blocking collectives  179 us (5%)
  other arithmetic  118 us (4%)
  local copies, waits for them, and re-layouts  57.3 us (2%)
    reduce_scatter x1, waiting for transfers between devices, sum_feedforward(): lax.psum_scatter(terms[2], ('fsdp', 'ctx'), scatter_dimension=0, tiled=True)  707 us
    reduce_scatter x1, waiting for transfers between devices, sum_feedforward(): lax.psum_scatter(terms[4], ('fsdp', 'ctx'), scatter_dimension=0, tiled=True)  706 us
    all_gather x1, waiting for transfers between devices, fetch_feedforward(): lax.all_gather(proj_weight, 'fsdp', axis=0, tiled=True)  256 us
    all_gather x1, waiting for transfers between devices, fetch_feedforward(): lax.all_gather(fc_weight, 'fsdp', axis=0, tiled=True)  249 us
    reduce_scatter x1, waiting for transfers between devices, sum_attention(): lax.psum_scatter(terms[6], ('fsdp', 'ctx'), scatter_dimension=0, tiled=True)  185 us
    reduce_scatter x1, waiting for transfers between devices, sum_attention(): lax.psum_scatter(terms[2], ('fsdp', 'ctx'), scatter_dimension=0, tiled=True)  127 us
    all_gather x1, waiting for transfers between devices, per_device(): lax.all_gather(ffn_total[2].astype(jnp.bfloat16), 'ctx', axis=0, tiled=True)  79.6 us
    all_gather x1, waiting for transfers between devices, per_device(): lax.all_gather(ffn_total[4].astype(jnp.bfloat16), 'ctx', axis=0, tiled=True)  69.6 us
  transfers between devices with their start and end apart: 18, of which 13 were waited for; matrix products, arithmetic and copies ran while one was open for 11% of the time, Pallas kernels for 0%

commit v1 on v0

v1 whole, which is shorter than its diff:
```python
import math

import jax
import jax.numpy as jnp
from jax import lax
from jax.sharding import PartitionSpec as P

D = 2048
HEADS = 16
HD = 128
QUAD = 4
F32 = jnp.float32
BF16 = jnp.bfloat16


def layer_norm(values, gain, shift):
    center = jnp.mean(values, axis=-1, keepdims=True)
    shifted = values - center
    spread = jnp.mean(shifted * shifted, axis=-1, keepdims=True)
    return shifted * lax.rsqrt(spread + 1e-05) * gain + shift


def layer_norm_back(values, gain, d_out):
    center = jnp.mean(values, axis=-1, keepdims=True)
    shifted = values - center
    spread = jnp.mean(shifted * shifted, axis=-1, keepdims=True)
    r = lax.rsqrt(spread + 1e-05)
    xhat = shifted * r
    e = d_out * gain
    d_values = r * (
        e - jnp.mean(e, axis=-1, keepdims=True) - xhat * jnp.mean(e * xhat, axis=-1, keepdims=True)
    )
    return d_values, jnp.sum(d_out * xhat, axis=0), jnp.sum(d_out, axis=0)


def gelu_and_slope(u):
    a = math.sqrt(2.0 / math.pi)
    t = jnp.tanh(a * (u + 0.044715 * u * u * u))
    half = 0.5 * (1.0 + t)
    slope = half + 0.5 * u * (1.0 - t * t) * a * (1.0 + 3.0 * 0.044715 * u * u)
    return u * half, slope


def dot(a, b):
    return jnp.dot(a, b, preferred_element_type=F32)


def dot_t(a, b):
    return lax.dot_general(a, b, (((1,), (1,)), ((), ())), preferred_element_type=F32)


def t_dot(a, b):
    return lax.dot_general(a, b, (((0,), (0,)), ((), ())), preferred_element_type=F32)


def swap_f(x, bit, size):
    return lax.ppermute(x, "fsdp", [(i, i ^ bit) for i in range(size)])


def swap_k(x, bit, size):
    return lax.ppermute(x, "ctx", [(i, i ^ bit) for i in range(size)])


def bits_of(size):
    out = []
    bit = 1
    while bit < size:
        out.append(bit)
        bit *= 2
    return out


def gather_f(piece, f, size):
    rows, n = piece.shape
    half = rows // 2
    orders = (bits_of(size), bits_of(size)[::-1])
    out = jnp.zeros((size, 2, half, n), piece.dtype)
    for h, order in enumerate(orders):
        held = {0: piece[h * half : (h + 1) * half]}
        for bit in order:
            for d in list(held):
                held[d ^ bit] = swap_f(held[d], bit, size)
        for d, part in held.items():
            out = lax.dynamic_update_slice(out, part[None, None], (f ^ d, h, 0, 0))
    return out.reshape(size * rows, n)


def reduce_f(term, size):
    outs = []
    for h, order in enumerate((bits_of(size), bits_of(size)[::-1])):
        sums = {d: (lambda d=d, h=h: term(d, h)) for d in range(size)}
        extra = {d: [] for d in range(size)}

        def value(d):
            total = sums[d]()
            for e in extra[d]:
                total = total + e.astype(F32)
            return total

        left = set(range(size))
        for bit in order:
            for d in sorted(left, reverse=True):
                if d & bit:
                    extra[d ^ bit].append(swap_f(value(d).astype(BF16), bit, size))
                    left.discard(d)
        outs.append(value(0))
    return jnp.concatenate(outs, axis=1)


def attend_forward(queries, keys, values, visible, head_block, scale):
    pieces = []
    lse_parts = []
    for start in range(0, HEADS, head_block):
        query_block = queries[:, start : start + head_block]
        scores = (
            jnp.einsum("qhd,kd->hqk", query_block, keys, preferred_element_type=F32) * scale
        )
        scores = jnp.where(visible[None], scores, -1e30)
        peak = jnp.max(scores, axis=-1, keepdims=True)
        expo = jnp.exp(scores - peak)
        total = jnp.sum(expo, axis=-1, keepdims=True)
        probs = expo / total
        lse_parts.append(peak[..., 0] + jnp.log(total[..., 0]))
        pieces.append(
            jnp.einsum("hqk,kd->qhd", probs.astype(BF16), values, preferred_element_type=F32)
        )
    return (jnp.concatenate(pieces, axis=1), jnp.concatenate(lse_parts, axis=0))


def attend_backward(queries, keys, values, visible, lse_rows, grad_mixed, head_block, scale):
    query_grads = []
    key_grad = jnp.zeros((keys.shape[0], HD), F32)
    value_grad = jnp.zeros((keys.shape[0], HD), F32)
    for start in range(0, HEADS, head_block):
        query_block = queries[:, start : start + head_block]
        grad_block = grad_mixed[:, start : start + head_block]
        scores = (
            jnp.einsum("qhd,kd->hqk", query_block, keys, preferred_element_type=F32) * scale
        )
        scores = jnp.where(visible[None], scores, -1e30)
        probs = jnp.exp(scores - lse_rows[start : start + head_block][..., None])
        grad_probs = jnp.einsum("qhd,kd->hqk", grad_block, values, preferred_element_type=F32)
        inner = jnp.sum(probs * grad_probs, axis=-1, keepdims=True)
        grad_scores = (probs * (grad_probs - inner)).astype(BF16)
        query_grads.append(
            jnp.einsum("hqk,kd->qhd", grad_scores, keys, preferred_element_type=F32) * scale
        )
        key_grad = (
            key_grad
            + jnp.einsum("hqk,qhd->kd", grad_scores, query_block, preferred_element_type=F32)
            * scale
        )
        value_grad = value_grad + jnp.einsum(
            "hqk,qhd->kd", probs.astype(BF16), grad_block, preferred_element_type=F32
        )
    return (jnp.concatenate(query_grads, axis=1), key_grad, value_grad)


def build(F, C):
    Z = C // 2

    def per_device(
        hidden_in,
        segment_ids,
        positions,
        norm1_gain,
        norm1_bias,
        query_weight,
        query_bias,
        keyval_weight,
        value_bias,
        out_weight,
        out_bias,
        norm2_gain,
        norm2_bias,
        fc_weight,
        fc_bias,
        proj_weight,
        proj_bias,
        out_grad,
    ):
        micros, rows = hidden_in.shape[:2]
        tok = micros * rows
        scale = 1.0 / math.sqrt(HD)
        head_block = 1
        while head_block * rows < 512 and head_block < HEADS:
            head_block = head_block * 2
        f = lax.axis_index("fsdp")
        k = lax.axis_index("ctx")
        core = k % 2
        quad = k % QUAD
        zi = k // 2
        hsh = D // F
        width = fc_weight.shape[1] // F // QUAD

        def pick_core(a, b):
            return jnp.where(core == 0, a, b)

        def in_order(own, other):
            return pick_core(
                jnp.concatenate([own, other], axis=1), jnp.concatenate([other, own], axis=1)
            )

        def halves(x):
            w = x.shape[1] // 2
            return pick_core(x[:, :w], x[:, w:]), pick_core(x[:, w:], x[:, :w])

        def after(x, *deps):
            return lax.optimization_barrier((x,) + deps)[0]

        def swk(x, bit):
            return swap_k(x, bit, C)

        def gather_ctx(x):
            held = {0: x}
            for bit in bits_of(C)[1:][::-1] + [1]:
                for d in list(held):
                    held[d ^ bit] = swk(held[d], bit)
            return [held[d] for d in range(C)]

        def gather_quad(x):
            a = swk(x, 1)
            b = swk(x, 2)
            c = swk(b, 1)
            return [x, a, b, c]

        names = (
            norm1_gain, norm1_bias, query_bias, out_bias, norm2_gain, norm2_bias, proj_bias,
            fc_bias, value_bias,
        )
        sizes = [v.shape[0] for v in names]
        packed = jnp.concatenate(names)
        pad = -packed.shape[0] % 1024
        packed = jnp.pad(packed, (0, pad)).reshape(-1, 128)
        vec = jnp.zeros((F,) + packed.shape, BF16)
        for d in range(F):
            part = packed if d == 0 else swap_f(packed, d, F)
            vec = lax.dynamic_update_slice(vec, part[None], (f ^ d, 0, 0))
        vec = vec.reshape(F, -1).astype(F32)
        full = []
        at = 0
        for size in sizes:
            full.append(vec[:, at : at + size])
            at += size
        gain_one, shift_one, b_query, b_out, gain_two, shift_two, b_proj = [
            v.reshape(-1) for v in full[:7]
        ]
        b_value = full[8].reshape(-1)
        b_fc = lax.dynamic_slice(
            full[7].reshape(F, QUAD, width), (0, quad, 0), (F, 1, width)
        ).reshape(-1)
        kv_bias = jnp.concatenate([jnp.zeros((HD,), F32), b_value])

        places = jnp.concatenate([segment_ids, positions], axis=0)
        places = jnp.stack(gather_ctx(places), axis=1)
        seg_all = places[:micros].reshape(micros, -1)
        pos_all = places[micros:].reshape(micros, -1)

        w_keyval = gather_f(keyval_weight, f, F)
        wq_piece = halves(query_weight)[0]
        wq_own = gather_f(after(wq_piece, w_keyval), f, F)
        wq_other = swk(wq_own, 1)
        wo_piece = halves(out_weight)[0]
        wo_own = gather_f(after(wo_piece, wq_own), f, F)
        wo_other = swk(wo_own, 1)

        fc_view = fc_weight.reshape(hsh, F, QUAD, width)
        fc_piece = fc_view[:, :, 0]
        for i in range(1, QUAD):
            fc_piece = jnp.where(quad == i, fc_view[:, :, i], fc_piece)
        fc_piece = fc_piece.reshape(hsh, F * width)
        proj_piece = lax.dynamic_slice(proj_weight, (quad * width, 0), (width, D))
        w_fc = gather_f(after(fc_piece, wo_own), f, F)
        w_proj = gather_f(after(proj_piece, w_fc), f, F)

        hidden = hidden_in.reshape(tok, D).astype(F32)
        normed1 = layer_norm(hidden, gain_one, shift_one).astype(BF16)
        keyvals = (dot(normed1, w_keyval) + kv_bias).astype(BF16)
        group_kv = jnp.stack(gather_ctx(keyvals.reshape(micros, rows, 2 * HD)), axis=1)
        group_kv = group_kv.reshape(micros, C * rows, 2 * HD)
        queries = (in_order(dot(normed1, wq_own), dot(normed1, wq_other)) + b_query).astype(BF16)
        queries = queries.reshape(micros, rows, HEADS, HD)
        visible = [
            (pos_all[m][None, :] <= positions[m][:, None])
            & ((seg_all[m][None, :] == 0) | (seg_all[m][None, :] == segment_ids[m][:, None]))
            for m in range(micros)
        ]
        mixed = []
        lse = []
        middle = []
        normed2_blocks = []
        for m in range(micros):
            out, lse_rows = attend_forward(
                queries[m], group_kv[m, :, :HD], group_kv[m, :, HD:], visible[m], head_block, scale
            )
            mix = out.reshape(rows, D).astype(BF16)
            mixed.append(mix)
            lse.append(lse_rows)
            mid = (
                hidden[m * rows : (m + 1) * rows]
                + in_order(dot(mix, wo_own), dot(mix, wo_other))
                + b_out
            )
            middle.append(mid)
            normed2_blocks.append(gather_quad(layer_norm(mid, gain_two, shift_two).astype(BF16)))
        mixed = jnp.concatenate(mixed, axis=0)
        middle = jnp.concatenate(middle, axis=0)
        normed2 = jnp.concatenate(
            [normed2_blocks[m][d] for d in range(QUAD) for m in range(micros)], axis=0
        )
        cot_own = out_grad.reshape(tok, D)
        cot = jnp.concatenate(gather_quad(cot_own), axis=0)

        active, slope = gelu_and_slope(dot(normed2, w_fc) + b_fc)
        active = active.astype(BF16)
        slope = slope.astype(BF16)

        def cols(x, d):
            w = x.shape[1] // F
            return lax.dynamic_slice(x, (0, (f ^ d) * w), (x.shape[0], w))

        def weight_grad(left, right):
            w = right.shape[1] // 2
            return reduce_f(lambda d, h: t_dot(cols(left, d), right[:, h * w : (h + 1) * w]), F)

        proj_grad = weight_grad(active, cot)

        def reduce_quad(term):
            outs = []
            for m in range(micros):
                r2 = swk(term(3, m).astype(BF16), 1)
                r0 = swk(term(1, m).astype(BF16), 1)
                z0 = swk((term(2, m) + r2.astype(F32)).astype(BF16), 2)
                outs.append(term(0, m) + r0.astype(F32) + z0.astype(F32))
            return outs

        def block(x, d, m):
            at = d * tok + m * rows
            return x[at : at + rows]

        d_before = (dot_t(cot, w_proj) * slope.astype(F32)).astype(BF16)
        d_normed2 = reduce_quad(lambda d, m: dot_t(block(d_before, d, m), w_fc))
        fc_grad = weight_grad(normed2, d_before)
        fc_b_grad = jnp.sum(d_before.astype(F32), axis=0)
        ffn = reduce_quad(lambda d, m: dot(block(active, d, m), w_proj))
        result = middle + jnp.concatenate(ffn, axis=0) + b_proj
        hidden_out = result.astype(BF16).reshape(micros, rows, D)

        d_middle, gain_two_grad, shift_two_grad = layer_norm_back(
            middle, gain_two, jnp.concatenate(d_normed2, axis=0)
        )
        d_middle = cot_own.astype(F32) + d_middle
        d_branch = d_middle.astype(BF16)
        branch_own, branch_other = halves(d_branch)
        d_mixed = (dot_t(branch_own, wo_own) + dot_t(branch_other, wo_other)).astype(BF16)
        branch_pair = jnp.concatenate([branch_own, swk(branch_other, 1)], axis=0)
        mixed_pair = jnp.concatenate([mixed, swk(mixed, 1)], axis=0)
        normed1_pair = jnp.concatenate([normed1, swk(normed1, 1)], axis=0)
        out_w_grad = weight_grad(mixed_pair, branch_pair)
        d_mixed = d_mixed.reshape(micros, rows, HEADS, HD)
        d_queries = []
        d_keyvals = []
        for m in range(micros):
            grad_queries, key_grad, value_grad = attend_backward(
                queries[m],
                group_kv[m, :, :HD],
                group_kv[m, :, HD:],
                visible[m],
                lse[m],
                d_mixed[m],
                head_block,
                scale,
            )
            d_queries.append(grad_queries.reshape(rows, D).astype(BF16))
            terms = jnp.concatenate([key_grad, value_grad], axis=1).reshape(C, rows, 2 * HD)
            terms = {d: terms[d] for d in range(C)}
            for bit in [1] + bits_of(C)[1:][::-1]:
                sent = [d for d in terms if d & bit]
                got = swk(jnp.stack([terms[d] for d in sent]).astype(BF16), bit)
                for i, d in enumerate(sent):
                    terms[d ^ bit] = terms[d ^ bit] + got[i].astype(F32)
                    del terms[d]
            d_keyvals.append(terms[0].astype(BF16))
        d_queries = jnp.concatenate(d_queries, axis=0)
        d_keyvals = jnp.concatenate(d_keyvals, axis=0)
        dq_own, dq_other = halves(d_queries)
        dq_pair = jnp.concatenate([dq_own, swk(dq_other, 1)], axis=0)
        query_w_grad = weight_grad(normed1_pair, dq_pair)
        keyval_w_grad = weight_grad(normed1, d_keyvals)
        d_normed1 = (
            dot_t(dq_own, wq_own) + dot_t(dq_other, wq_other) + dot_t(d_keyvals, w_keyval)
        )
        d_hidden, gain_one_grad, shift_one_grad = layer_norm_back(hidden, gain_one, d_normed1)
        hidden_grad = (d_middle + d_hidden).reshape(micros, rows, D)

        def sum_z(x):
            part = x.shape[0] // Z
            blocks = x.astype(BF16).reshape(Z, part, x.shape[1])

            def one(d):
                return lax.dynamic_slice(blocks, (zi ^ d, 0, 0), (1,) + blocks.shape[1:])[0]

            total = one(0).astype(F32)
            for d in range(1, Z):
                total = total + swk(one(d), 2 * d).astype(F32)
            total = total.astype(BF16)
            out = jnp.zeros(blocks.shape, BF16)
            for d in range(Z):
                got = total if d == 0 else swk(total, 2 * d)
                out = lax.dynamic_update_slice(out, got[None], (zi ^ d, 0, 0))
            own = out.reshape(x.shape)
            return in_order(own, swk(own, 1)).astype(F32)

        def sum_quads(x):
            for bit in bits_of(C)[2:]:
                x = x + swk(x.astype(BF16), bit).astype(F32)
            parts = gather_quad(x.astype(BF16))
            out = jnp.zeros((QUAD,) + x.shape, BF16)
            for d in range(QUAD):
                out = lax.dynamic_update_slice(out, parts[d][None], (quad ^ d, 0, 0))
            return out

        proj_out = sum_quads(proj_grad).reshape(QUAD * width, D).astype(F32)
        fc_parts = sum_quads(fc_grad)
        fc_out = jnp.concatenate(
            [
                fc_parts[i][:, j * width : (j + 1) * width]
                for j in range(F)
                for i in range(QUAD)
            ],
            axis=1,
        ).astype(F32)
        out_out = sum_z(out_w_grad)
        query_out = sum_z(query_w_grad)
        kv_sum = keyval_w_grad
        for bit in bits_of(C):
            kv_sum = kv_sum + swk(kv_sum.astype(BF16), bit).astype(F32)

        fc_b_full = lax.dynamic_update_slice(
            jnp.zeros((F, QUAD, width), F32), fc_b_grad.reshape(F, 1, width), (0, quad, 0)
        )

        def sum_vectors(vectors):
            sizes = [v.size // F for v in vectors]
            packed = jnp.concatenate([v.reshape(F, -1) for v in vectors], axis=1)
            packed = jnp.pad(packed, ((0, 0), (0, -packed.shape[1] % 1024)))
            packed = packed.reshape(F, -1, 128)

            def one(d):
                return lax.dynamic_slice(packed, (f ^ d, 0, 0), (1,) + packed.shape[1:])[0]

            total = one(0)
            for d in range(1, F):
                total = total + swap_f(one(d), d, F)
            for bit in bits_of(C):
                total = total + swk(total, bit)
            total = total.reshape(-1)
            outs = []
            at = 0
            for size in sizes:
                outs.append(total[at : at + size])
                at += size
            return outs

        def column_sum(x):
            return jnp.sum(x.astype(F32), axis=0)

        g2, s2, bp, bo, bf = sum_vectors(
            [gain_two_grad, shift_two_grad, column_sum(cot_own), column_sum(d_branch), fc_b_full]
        )
        g1, s1, bq, bv = sum_vectors(
            [
                gain_one_grad,
                shift_one_grad,
                column_sum(d_queries),
                column_sum(d_keyvals[:, HD:]),
            ]
        )
        return (
            hidden_out, hidden_grad, g1, s1, query_out, bq, kv_sum, bv, out_out, bo, g2, s2,
            fc_out, bf, proj_out, bp,
        )

    return per_device


def solution(mesh):
    tokens = P(None, ("fsdp", "ctx"), None)
    places = P(None, ("fsdp", "ctx"))
    vec = P("fsdp")
    mat = P("fsdp", None)
    grads = (vec, vec, mat, vec, mat, vec, mat, vec, vec, vec, mat, vec, mat, vec)
    return jax.shard_map(
        build(mesh.shape["fsdp"], mesh.shape["ctx"]),
        mesh=mesh,
        in_specs=(tokens, places, places) + grads + (tokens,),
        out_specs=(tokens, tokens) + grads,
        check_vma=False,
    )
```

time: 3270 us -> 1540 us (0.47)
  waiting for transfers between devices: 2490 us -> 485 us
  starting transfers between devices: 1.31 us -> 200 us
  blocking collectives: 179 us -> 0 us
  local copies, waits for them, and re-layouts: 57.3 us -> 188 us
  other arithmetic: 118 us -> 191 us
  matrix products: 398 us -> 468 us
    reduce_scatter x7 -> x0, waiting for transfers between devices: 1730 us -> none  [the longest x1 707 us: sum_feedforward(): lax.psum_scatter(terms[2], ('fsdp', 'ctx'), scatter_dimension=0, tiled=True)]
    all_gather x11 -> x0, waiting for transfers between devices: 765 us -> none  [the longest x1 256 us: fetch_feedforward(): lax.all_gather(proj_weight, 'fsdp', axis=0, tiled=True)]
    ppermute x0 -> x147, waiting for transfers between devices: none -> 485 us  [the longest x78 354 us: swap_k(): return lax.ppermute(x, 'ctx', [(i, i ^ bit) for i in range(size)])]
    ppermute x0 -> x147, starting transfers between devices: none -> 200 us  [the longest x78 144 us: swap_k(): return lax.ppermute(x, 'ctx', [(i, i ^ bit) for i in range(size)])]
    all_gather x12 -> x0, blocking collectives: 114 us -> none  [the longest x1 26.7 us: per_device(): lax.all_gather(segment_ids, 'ctx', axis=1, tiled=True)]
    unnamed x3 -> x0, blocking collectives: 65.1 us -> none
    dot_general x105 -> x150, matrix products: 379 us -> 441 us  [the longest x14 120 us: dot_t(): lax.dot_general(a, b, (((1,), (1,)), ((), ())), preferred_element_type=F32)]
    dynamic_update_slice x0 -> x57, local copies, waits for them, and re-layouts: none -> 48.4 us  [the longest x40 33.2 us: gather_f(): out = lax.dynamic_update_slice(out, part[None, None], (f ^ d, h, 0, 0))]
  transfers between devices with their start and end apart: 18 -> 147, of which waited for: 13 -> 54; matrix products, arithmetic and copies ran while one was open for 11% -> 52% of each run, Pallas kernels for 0% -> 0%
where the time goes in v1:
time: 1540 us
  waiting for transfers between devices  485 us (31%)
  matrix products  468 us (30%)
  starting transfers between devices  200 us (13%)
  other arithmetic  191 us (12%)
  local copies, waits for them, and re-layouts  188 us (12%)
    ppermute x78, waiting for transfers between devices, swap_k(): return lax.ppermute(x, 'ctx', [(i, i ^ bit) for i in range(size)])  354 us
    ppermute x78, starting transfers between devices, swap_k(): return lax.ppermute(x, 'ctx', [(i, i ^ bit) for i in range(size)])  144 us
    ppermute x69, waiting for transfers between devices, swap_f(): return lax.ppermute(x, 'fsdp', [(i, i ^ bit) for i in range(size)])  131 us
    dot_general x14, matrix products, dot_t(): lax.dot_general(a, b, (((1,), (1,)), ((), ())), preferred_element_type=F32)  120 us
    dot_general x40, matrix products, t_dot(): lax.dot_general(a, b, (((0,), (0,)), ((), ())), preferred_element_type=F32)  110 us
    dot_general x16, matrix products, dot(): return jnp.dot(a, b, preferred_element_type=F32)  84.8 us
    unnamed x619, local copies, waits for them, and re-layouts  83.2 us
    ppermute x69, starting transfers between devices, swap_f(): return lax.ppermute(x, 'fsdp', [(i, i ^ bit) for i in range(size)])  55.7 us
  transfers between devices with their start and end apart: 147, of which 54 were waited for; matrix products, arithmetic and copies ran while one was open for 52% of the time, Pallas kernels for 0%

profile of v1, /device:TPU:1, one launch (start us, length us, event | category | flops | bytes accessed | tf_op | source)
XLA Modules:
  0.0 1536.5 jit_solution(2174714809913777624)
XLA Ops:
  27.3 11.9 copy.431
  97.6 6.2 collective-permute-start.9
  108.2 10.3 collective-permute-done.25
  142.6 7.5 collective-permute-start.13
  153.9 9.8 collective-permute-done.32
  165.7 8.6 collective-permute-start.11
  191.8 8.3 collective-permute-done.43
  201.8 9.9 collective-permute-start.29
  242.1 7.0 pad_maximum_fusion
  365.7 12.2 collective-permute-done.51
  392.0 10.3 collective-permute-done.39
  405.0 19.7 %collective-permute-done.40 = bf16[256,2048]{1,0:T(8,128)(2,1)} collective-permute-done((bf16[256,2048]{1,0:T(8,128)(2,1)}, bf16[256,2048]{1,0:T(8,128)(2,1)}, u32[]{:S(2)}, u32[]{:S(2)}) %collective-permute-start.40) | collective-permute-done | bytes 1048608 | tf_op jit(solution)/shard_map/ppermute | solution.py:61
  440.1 29.0 %multiply_convert_fusion.1 = (bf16[2048,2048]{1,0:T(8,128)(2,1)}, f32[2048,2048]{1,0:T(8,128)}) fusion(f32[2048]{0:T(1024)S(1)} %bitcast.1302, bf16[2048,2048]{1,0:T(8,128)(2,1)S(1)} %constant_dynamic-update-slice_fusion.9, bf16[2048,2048]{1,0:T(8,128)(2,1)} %bitcast.129), kind=kOutput, calls=%fused_computation.10 | convolution fusion | flops 17221812224 | bytes 41951232 | tf_op jit(solution)/shard_map/dot_general | solution.py:45
  469.1 38.2 %convert_reduce_fusion = (f32[2048]{0:T(1024)S(1)}, bf16[2048,2048]{1,0:T(8,128)(2,1)}) fusion(f32[2048,2048]{1,0:T(8,128)} %get-tuple-element.247, f32[2048]{0:T(1024)S(1)} %bitcast.1303, bf16[2048,2048]{1,0:T(8,128)(2,1)} %bitcast.1204, bf16[512,2048]{1,0:T(8,128)(2,1)} %collective-permute-done.63, bf16[512,2048]{1,0:T(8,128)(2,1)} %collective-permute-done.62, ...), kind=kOutput, calls=%fused_computation.8 | convolution fusion | flops 17314084864 | bytes 41959424 | tf_op jit(solution)/shard_map/dot_general | solution.py:49
  507.3 7.1 convolution_convert_fusion
  520.5 7.2 convolution_convert_fusion.2
  527.6 6.2 convolution_convert_fusion.3
  584.5 6.4 fusion.131
  591.5 6.6 fusion.130
  608.5 14.8 collective-permute-done.131
  635.2 12.0 collective-permute-done.141
  657.5 13.0 collective-permute-done.69
  670.5 7.0 fusion.689
  679.1 13.9 collective-permute-done.66
  693.0 6.9 fusion.688
  923.9 13.0 collective-permute-done.60
  942.2 17.1 %collective-permute-done.57 = bf16[256,2048]{1,0:T(8,128)(2,1)S(1)} collective-permute-done((bf16[256,2048]{1,0:T(8,128)(2,1)S(1)}, bf16[256,2048]{1,0:T(8,128)(2,1)S(1)}, u32[]{:S(2)}, u32[]{:S(2)}) %collective-permute-start.57) | collective-permute-done | bytes 1048608 | tf_op jit(solution)/shard_map/ppermute | solution.py:61
  966.0 6.7 fusion.697
  975.1 6.5 collective-permute-done.142
  999.4 6.9 fusion.698
  1028.5 16.0 %collective-permute-done.74 = bf16[2,256,256]{1,2,0:T(8,128)(2,1)S(1)} collective-permute-done((bf16[2,256,256]{1,2,0:T(8,128)(2,1)S(1)}, bf16[2,256,256]{1,2,0:T(8,128)(2,1)S(1)}, u32[]{:S(2)}, u32[]{:S(2)}) %collective-permute-start.74) | collective-permute-done | bytes 262176 | tf_op jit(solution)/shard_map/ppermute | solution.py:61
  1062.6 7.3 multiply_reduce_fusion.1
  1084.0 37.2 %collective-permute-done.80 = f32[16,128]{1,0:T(8,128)S(1)} collective-permute-done((f32[16,128]{1,0:T(8,128)S(1)}, f32[16,128]{1,0:T(8,128)S(1)}, u32[]{:S(2)}, u32[]{:S(2)}) %collective-permute-start.80) | collective-permute-done | bytes 8224 | tf_op jit(solution)/shard_map/ppermute | solution.py:61
  1142.7 6.7 collective-permute-done.102
  1153.8 11.2 collective-permute-start.103
  1173.1 7.8 collective-permute-done.109
  1182.1 9.7 collective-permute-done.112
  1213.9 6.9 collective-permute-done.108
  1236.7 14.8 collective-permute-done.92
  1253.9 67.1 %collective-permute-done.91 = bf16[128,1024]{1,0:T(8,128)(2,1)S(1)} collective-permute-done((bf16[128,1024]{1,0:T(8,128)(2,1)S(1)}, bf16[128,1024]{1,0:T(8,128)(2,1)S(1)}, u32[]{:S(2)}, u32[]{:S(2)}) %collective-permute-start.91) | collective-permute-done | bytes 262176 | tf_op jit(solution)/shard_map/ppermute | solution.py:61
  1345.6 20.4 %collective-permute-done.94 = bf16[128,1024]{1,0:T(8,128)(2,1)S(1)} collective-permute-done((bf16[128,1024]{1,0:T(8,128)(2,1)S(1)}, bf16[128,1024]{1,0:T(8,128)(2,1)S(1)}, u32[]{:S(2)}, u32[]{:S(2)}) %collective-permute-start.94) | collective-permute-done | bytes 262176 | tf_op jit(solution)/shard_map/ppermute | solution.py:61
  1366.0 7.0 collective-permute-start.118
  1374.1 15.9 %collective-permute-done.118 = bf16[128,1024]{1,0:T(8,128)(2,1)S(1)} collective-permute-done((bf16[128,1024]{1,0:T(8,128)(2,1)S(1)}, bf16[128,1024]{1,0:T(8,128)(2,1)S(1)}, u32[]{:S(2)}, u32[]{:S(2)}) %collective-permute-start.118) | collective-permute-done | bytes 262176 | tf_op jit(solution)/shard_map/ppermute | solution.py:61
  1410.2 24.6 %collective-permute-done.135 = bf16[512,2048]{1,0:T(8,128)(2,1)} collective-permute-done((bf16[512,2048]{1,0:T(8,128)(2,1)}, bf16[512,2048]{1,0:T(8,128)(2,1)}, u32[]{:S(2)}, u32[]{:S(2)}) %collective-permute-start.135) | collective-permute-done | bytes 2097184 | tf_op jit(solution)/shard_map/ppermute | solution.py:61
  1434.8 6.7 collective-permute-start.136
  1441.5 38.2 %collective-permute-done.145 = bf16[512,2048]{1,0:T(8,128)(2,1)} collective-permute-done((bf16[512,2048]{1,0:T(8,128)(2,1)}, bf16[512,2048]{1,0:T(8,128)(2,1)}, u32[]{:S(2)}, u32[]{:S(2)}) %collective-permute-start.145) | collective-permute-done | bytes 2097184 | tf_op jit(solution)/shard_map/ppermute | solution.py:61
  1511.5 11.7 convert_element_type.894
  1524.7 11.7 bitcast_convert_fusion
  (1308 shorter events, 870.5 us)
Async XLA Ops:
  8.6 60.0 %collective-permute-start = (bf16[48,128]{1,0:T(8,128)(2,1)S(1)}, bf16[48,128]{1,0:T(8,128)(2,1)S(1)}, u32[]{:S(2)}, u32[]{:S(2)}) collective-permute-start(bf16[48,128]{1,0:T(8,128)(2,1)S(1)} %pad_bitcast_fusion), channel_id=1, source_target_pairs={{0,8},{8,0},{16,24},{24,16},{1,9},{9,1},{17,25},{25,17},{2,10},{10... | collective-permute-start | bytes 36872 | tf_op jit(solution)/shard_map/ppermute | solution.py:57
  10.7 58.2 %collective-permute-start.1 = (bf16[48,128]{1,0:T(8,128)(2,1)S(1)}, bf16[48,128]{1,0:T(8,128)(2,1)S(1)}, u32[]{:S(2)}, u32[]{:S(2)}) collective-permute-start(bf16[48,128]{1,0:T(8,128)(2,1)S(1)} %pad_bitcast_fusion), channel_id=1, source_target_pairs={{0,16},{8,24},{16,0},{24,8},{1,17},{9,25},{17,1},{25,9},{2,18},{10... | collective-permute-start | bytes 36872 | tf_op jit(solution)/shard_map/ppermute | solution.py:57
  11.9 58.2 %collective-permute-start.2 = (bf16[48,128]{1,0:T(8,128)(2,1)S(1)}, bf16[48,128]{1,0:T(8,128)(2,1)S(1)}, u32[]{:S(2)}, u32[]{:S(2)}) collective-permute-start(bf16[48,128]{1,0:T(8,128)(2,1)S(1)} %pad_bitcast_fusion), channel_id=1, source_target_pairs={{0,24},{8,16},{16,8},{24,0},{1,25},{9,17},{17,9},{25,1},{2,26},{10... | collective-permute-start | bytes 36872 | tf_op jit(solution)/shard_map/ppermute | solution.py:57
  13.2 38.3 %collective-permute-start.16 = (s32[4,256]{1,0:T(4,128)}, s32[4,256]{1,0:T(4,128)}, u32[]{:S(2)}, u32[]{:S(2)}) collective-permute-start(s32[4,256]{1,0:T(4,128)} %pad_add_fusion), channel_id=1, source_target_pairs={{0,1},{1,0},{2,3},{3,2},{4,5},{5,4},{6,7},{7,6},{8,9},{9,8},{10,11... | collective-permute-start | bytes 12296 | tf_op jit(solution)/shard_map/ppermute | solution.py:61
  14.5 39.4 %collective-permute-start.17 = (s32[4,256]{1,0:T(4,128)}, s32[4,256]{1,0:T(4,128)}, u32[]{:S(2)}, u32[]{:S(2)}) collective-permute-start(s32[4,256]{1,0:T(4,128)} %pad_add_fusion), channel_id=1, source_target_pairs={{0,2},{1,3},{2,0},{3,1},{4,6},{5,7},{6,4},{7,5},{8,10},{9,11},{10,... | collective-permute-start | bytes 12296 | tf_op jit(solution)/shard_map/ppermute | solution.py:61
  70.1 116.0 %collective-permute-start.62 = (bf16[512,2048]{1,0:T(8,128)(2,1)}, bf16[512,2048]{1,0:T(8,128)(2,1)}, u32[]{:S(2)}, u32[]{:S(2)}) collective-permute-start(bf16[512,2048]{1,0:T(8,128)(2,1)} %bitcast.141), channel_id=1, source_target_pairs={{0,2},{1,3},{2,0},{3,1},{4,6},{5,7},{6,4},{7,5},{8,10},{9,11},{10,... | collective-permute-start | bytes 6291464 | tf_op jit(solution)/shard_map/ppermute | solution.py:61
  142.6 39.4 %collective-permute-start.13 = (bf16[2,256,256]{2,1,0:T(8,128)(2,1)S(1)}, bf16[2,256,256]{2,1,0:T(8,128)(2,1)S(1)}, u32[]{:S(2)}, u32[]{:S(2)}) collective-permute-start(bf16[2,256,256]{2,1,0:T(8,128)(2,1)S(1)} %collective-permute-done.12), channel_id=1, source_target_pairs={{0,1},{1,0},{2,3},{3,2},{4,5},{5,4},{6,7},{7,6},{8,9},{9,8},{10,11... | collective-permute-start | bytes 786440 | tf_op jit(solution)/shard_map/ppermute | solution.py:61
  182.0 58.2 %collective-permute-start.61 = (bf16[512,2048]{1,0:T(8,128)(2,1)}, bf16[512,2048]{1,0:T(8,128)(2,1)}, u32[]{:S(2)}, u32[]{:S(2)}) collective-permute-start(bf16[512,2048]{1,0:T(8,128)(2,1)} %bitcast.141), channel_id=1, source_target_pairs={{0,1},{1,0},{2,3},{3,2},{4,5},{5,4},{6,7},{7,6},{8,9},{9,8},{10,11... | collective-permute-start | bytes 6291464 | tf_op jit(solution)/shard_map/ppermute | solution.py:61
  186.1 56.0 %collective-permute-start.63 = (bf16[512,2048]{1,0:T(8,128)(2,1)}, bf16[512,2048]{1,0:T(8,128)(2,1)}, u32[]{:S(2)}, u32[]{:S(2)}) collective-permute-start(bf16[512,2048]{1,0:T(8,128)(2,1)} %collective-permute-done.62), channel_id=1, source_target_pairs={{0,1},{1,0},{2,3},{3,2},{4,5},{5,4},{6,7},{7,6},{8,9},{9,8},{10,11... | collective-permute-start | bytes 6291464 | tf_op jit(solution)/shard_map/ppermute | solution.py:61
  190.4 37.8 %collective-permute-start.46 = (bf16[256,2048]{0,1:T(8,128)(2,1)}, bf16[256,2048]{0,1:T(8,128)(2,1)}, u32[]{:S(2)}, u32[]{:S(2)}) collective-permute-start(bf16[256,2048]{0,1:T(8,128)(2,1)} %get-tuple-element.124), channel_id=1, source_target_pairs={{0,16},{8,24},{16,0},{24,8},{1,17},{9,25},{17,1},{25,9},{2,18},{10... | collective-permute-start | bytes 3145736 | tf_op jit(solution)/shard_map/ppermute | solution.py:57
  201.8 65.5 %collective-permute-start.29 = (bf16[2048,1024]{1,0:T(8,128)(2,1)}, bf16[2048,1024]{1,0:T(8,128)(2,1)}, u32[]{:S(2)}, u32[]{:S(2)}) collective-permute-start(bf16[2048,1024]{1,0:T(8,128)(2,1)} %bitcast.50), channel_id=1, source_target_pairs={{0,1},{1,0},{2,3},{3,2},{4,5},{5,4},{6,7},{7,6},{8,9},{9,8},{10,11... | collective-permute-start | bytes 12582920 | tf_op jit(solution)/shard_map/ppermute | solution.py:61
  240.2 113.6 %collective-permute-start.36 = (bf16[2048,1024]{1,0:T(8,128)(2,1)}, bf16[2048,1024]{1,0:T(8,128)(2,1)}, u32[]{:S(2)}, u32[]{:S(2)}) collective-permute-start(bf16[2048,1024]{1,0:T(8,128)(2,1)} %bitcast.1224), channel_id=1, source_target_pairs={{0,1},{1,0},{2,3},{3,2},{4,5},{5,4},{6,7},{7,6},{8,9},{9,8},{10,11... | collective-permute-start | bytes 12582920 | tf_op jit(solution)/shard_map/ppermute | solution.py:61
  264.7 85.0 %collective-permute-start.49 = (bf16[256,2048]{1,0:T(8,128)(2,1)S(1)}, bf16[256,2048]{1,0:T(8,128)(2,1)S(1)}, u32[]{:S(2)}, u32[]{:S(2)}) collective-permute-start(bf16[256,2048]{1,0:T(8,128)(2,1)S(1)} %get-tuple-element.123), channel_id=1, source_target_pairs={{0,8},{8,0},{16,24},{24,16},{1,9},{9,1},{17,25},{25,17},{2,10},{10... | collective-permute-start | bytes 3145736 | tf_op jit(solution)/shard_map/ppermute | solution.py:57
  264.7 88.3 %collective-permute-start.50 = (bf16[256,2048]{1,0:T(8,128)(2,1)S(1)}, bf16[256,2048]{1,0:T(8,128)(2,1)S(1)}, u32[]{:S(2)}, u32[]{:S(2)}) collective-permute-start(bf16[256,2048]{1,0:T(8,128)(2,1)S(1)} %get-tuple-element.123), channel_id=1, source_target_pairs={{0,16},{8,24},{16,0},{24,8},{1,17},{9,25},{17,1},{25,9},{2,18},{10... | collective-permute-start | bytes 3145736 | tf_op jit(solution)/shard_map/ppermute | solution.py:57
  265.0 88.1 %collective-permute-start.52 = (bf16[256,2048]{1,0:T(8,128)(2,1)}, bf16[256,2048]{1,0:T(8,128)(2,1)}, u32[]{:S(2)}, u32[]{:S(2)}) collective-permute-start(bf16[256,2048]{1,0:T(8,128)(2,1)} %get-tuple-element.122), channel_id=1, source_target_pairs={{0,16},{8,24},{16,0},{24,8},{1,17},{9,25},{17,1},{25,9},{2,18},{10... | collective-permute-start | bytes 3145736 | tf_op jit(solution)/shard_map/ppermute | solution.py:57
  267.3 116.1 %collective-permute-start.53 = (bf16[256,2048]{1,0:T(8,128)(2,1)}, bf16[256,2048]{1,0:T(8,128)(2,1)}, u32[]{:S(2)}, u32[]{:S(2)}) collective-permute-start(bf16[256,2048]{1,0:T(8,128)(2,1)} %get-tuple-element.122), channel_id=1, source_target_pairs={{0,8},{8,0},{16,24},{24,16},{1,9},{9,1},{17,25},{25,17},{2,10},{10... | collective-permute-start | bytes 3145736 | tf_op jit(solution)/shard_map/ppermute | solution.py:57
  349.7 84.7 %collective-permute-start.106 = (bf16[512,2048]{0,1:T(8,128)(2,1)S(1)}, bf16[512,2048]{0,1:T(8,128)(2,1)}, u32[]{:S(2)}, u32[]{:S(2)}) collective-permute-start(bf16[512,2048]{0,1:T(8,128)(2,1)S(1)} %pad_maximum_fusion.10), channel_id=1, source_target_pairs={{0,1},{1,0},{2,3},{3,2},{4,5},{5,4},{6,7},{7,6},{8,9},{9,8},{10,11... | collective-permute-start | bytes 6291464 | tf_op jit(solution)/shard_map/ppermute | solution.py:61
  383.4 41.3 %collective-permute-start.40 = (bf16[256,2048]{1,0:T(8,128)(2,1)}, bf16[256,2048]{1,0:T(8,128)(2,1)}, u32[]{:S(2)}, u32[]{:S(2)}) collective-permute-start(bf16[256,2048]{1,0:T(8,128)(2,1)} %get-tuple-element.94), channel_id=1, source_target_pairs={{0,2},{1,3},{2,0},{3,1},{4,6},{5,7},{6,4},{7,5},{8,10},{9,11},{10,... | collective-permute-start | bytes 3145736 | tf_op jit(solution)/shard_map/ppermute | solution.py:61
  386.1 42.6 %collective-permute-start.38 = (bf16[256,2048]{1,0:T(8,128)(2,1)}, bf16[256,2048]{1,0:T(8,128)(2,1)S(1)}, u32[]{:S(2)}, u32[]{:S(2)}) collective-permute-start(bf16[256,2048]{1,0:T(8,128)(2,1)} %get-tuple-element.94), channel_id=1, source_target_pairs={{0,1},{1,0},{2,3},{3,2},{4,5},{5,4},{6,7},{7,6},{8,9},{9,8},{10,11... | collective-permute-start | bytes 3145736 | tf_op jit(solution)/shard_map/ppermute | solution.py:61
  392.0 736.4 %collective-permute-start.82 = (bf16[512,2048]{1,0:T(8,128)(2,1)}, bf16[512,2048]{1,0:T(8,128)(2,1)}, u32[]{:S(2)}, u32[]{:S(2)}) collective-permute-start(bf16[512,2048]{1,0:T(8,128)(2,1)} %add_convert_fusion.4), channel_id=1, source_target_pairs={{0,1},{1,0},{2,3},{3,2},{4,5},{5,4},{6,7},{7,6},{8,9},{9,8},{10,11... | collective-permute-start | bytes 6291464 | tf_op jit(solution)/shard_map/ppermute | solution.py:61
  583.3 73.4 %collective-permute-start.67 = (bf16[256,2048]{1,0:T(8,128)(2,1)S(1)}, bf16[256,2048]{1,0:T(8,128)(2,1)}, u32[]{:S(2)}, u32[]{:S(2)}) collective-permute-start(bf16[256,2048]{1,0:T(8,128)(2,1)S(1)} %convolution_convert_fusion.1), channel_id=1, source_target_pairs={{0,1},{1,0},{2,3},{3,2},{4,5},{5,4},{6,7},{7,6},{8,9},{9,8},{10,11... | collective-permute-start | bytes 3145736 | tf_op jit(solution)/shard_map/ppermute | solution.py:61
  583.3 94.2 %collective-permute-start.64 = (bf16[256,2048]{1,0:T(8,128)(2,1)S(1)}, bf16[256,2048]{1,0:T(8,128)(2,1)S(1)}, u32[]{:S(2)}, u32[]{:S(2)}) collective-permute-start(bf16[256,2048]{1,0:T(8,128)(2,1)S(1)} %convolution_convert_fusion.3), channel_id=1, source_target_pairs={{0,1},{1,0},{2,3},{3,2},{4,5},{5,4},{6,7},{7,6},{8,9},{9,8},{10,11... | collective-permute-start | bytes 3145736 | tf_op jit(solution)/shard_map/ppermute | solution.py:61
  652.8 40.2 %collective-permute-start.66 = (bf16[256,2048]{1,0:T(8,128)(2,1)S(1)}, bf16[256,2048]{1,0:T(8,128)(2,1)S(1)}, u32[]{:S(2)}, u32[]{:S(2)}) collective-permute-start(bf16[256,2048]{1,0:T(8,128)(2,1)S(1)} %fusion.130), channel_id=1, source_target_pairs={{0,2},{1,3},{2,0},{3,1},{4,6},{5,7},{6,4},{7,5},{8,10},{9,11},{10,... | collective-permute-start | bytes 3145736 | tf_op jit(solution)/shard_map/ppermute | solution.py:61
  656.7 247.1 %collective-permute-start.130 = (bf16[512,1024]{1,0:T(8,128)(2,1)}, bf16[512,1024]{1,0:T(8,128)(2,1)}, u32[]{:S(2)}, u32[]{:S(2)}) collective-permute-start(bf16[512,1024]{1,0:T(8,128)(2,1)} %fusion.246), channel_id=1, source_target_pairs={{0,16},{8,24},{16,0},{24,8},{1,17},{9,25},{17,1},{25,9},{2,18},{10... | collective-permute-start | bytes 3145736 | tf_op jit(solution)/shard_map/ppermute | solution.py:57
  670.5 242.2 %collective-permute-start.127 = (bf16[512,1024]{1,0:T(8,128)(2,1)}, bf16[512,1024]{1,0:T(8,128)(2,1)}, u32[]{:S(2)}, u32[]{:S(2)}) collective-permute-start(bf16[512,1024]{1,0:T(8,128)(2,1)} %fusion.236), channel_id=1, source_target_pairs={{0,8},{8,0},{16,24},{24,16},{1,9},{9,1},{17,25},{25,17},{2,10},{10... | collective-permute-start | bytes 3145736 | tf_op jit(solution)/shard_map/ppermute | solution.py:57
  677.6 229.0 %collective-permute-start.132 = (bf16[512,1024]{1,0:T(8,128)(2,1)}, bf16[512,1024]{1,0:T(8,128)(2,1)}, u32[]{:S(2)}, u32[]{:S(2)}) collective-permute-start(bf16[512,1024]{1,0:T(8,128)(2,1)} %add_convert_fusion.8), channel_id=1, source_target_pairs={{0,8},{8,0},{16,24},{24,16},{1,9},{9,1},{17,25},{25,17},{2,10},{10... | collective-permute-start | bytes 3145736 | tf_op jit(solution)/shard_map/ppermute | solution.py:57
  693.0 220.4 %collective-permute-start.129 = (bf16[512,1024]{1,0:T(8,128)(2,1)}, bf16[512,1024]{1,0:T(8,128)(2,1)}, u32[]{:S(2)}, u32[]{:S(2)}) collective-permute-start(bf16[512,1024]{1,0:T(8,128)(2,1)} %add_convert_fusion.9), channel_id=1, source_target_pairs={{0,16},{8,24},{16,0},{24,8},{1,17},{9,25},{17,1},{25,9},{2,18},{10... | collective-permute-start | bytes 3145736 | tf_op jit(solution)/shard_map/ppermute | solution.py:57
  913.4 45.9 %collective-permute-start.57 = (bf16[256,2048]{1,0:T(8,128)(2,1)S(1)}, bf16[256,2048]{1,0:T(8,128)(2,1)S(1)}, u32[]{:S(2)}, u32[]{:S(2)}) collective-permute-start(bf16[256,2048]{1,0:T(8,128)(2,1)S(1)} %copy-done.245), channel_id=1, source_target_pairs={{0,2},{1,3},{2,0},{3,1},{4,6},{5,7},{6,4},{7,5},{8,10},{9,11},{10,... | collective-permute-start | bytes 3145736 | tf_op jit(solution)/shard_map/ppermute | solution.py:61
  922.4 50.8 %collective-permute-start.140 = (bf16[512,1024]{1,0:T(8,128)(2,1)S(1)}, bf16[512,1024]{1,0:T(8,128)(2,1)}, u32[]{:S(2)}, u32[]{:S(2)}) collective-permute-start(bf16[512,1024]{1,0:T(8,128)(2,1)S(1)} %copy-done.240), channel_id=1, source_target_pairs={{0,16},{8,24},{16,0},{24,8},{1,17},{9,25},{17,1},{25,9},{2,18},{10... | collective-permute-start | bytes 3145736 | tf_op jit(solution)/shard_map/ppermute | solution.py:57
  936.9 50.7 %collective-permute-start.137 = (bf16[512,1024]{1,0:T(8,128)(2,1)S(1)}, bf16[512,1024]{1,0:T(8,128)(2,1)}, u32[]{:S(2)}, u32[]{:S(2)}) collective-permute-start(bf16[512,1024]{1,0:T(8,128)(2,1)S(1)} %copy-done.239), channel_id=1, source_target_pairs={{0,8},{8,0},{16,24},{24,16},{1,9},{9,1},{17,25},{25,17},{2,10},{10... | collective-permute-start | bytes 3145736 | tf_op jit(solution)/shard_map/ppermute | solution.py:57
  941.1 40.4 %collective-permute-start.142 = (bf16[512,1024]{1,0:T(8,128)(2,1)S(1)}, bf16[512,1024]{1,0:T(8,128)(2,1)}, u32[]{:S(2)}, u32[]{:S(2)}) collective-permute-start(bf16[512,1024]{1,0:T(8,128)(2,1)S(1)} %copy-done.244), channel_id=1, source_target_pairs={{0,8},{8,0},{16,24},{24,16},{1,9},{9,1},{17,25},{25,17},{2,10},{10... | collective-permute-start | bytes 3145736 | tf_op jit(solution)/shard_map/ppermute | solution.py:57
  973.3 149.5 %collective-permute-start.83 = (bf16[512,1024]{1,0:T(8,128)(2,1)}, bf16[512,1024]{1,0:T(8,128)(2,1)}, u32[]{:S(2)}, u32[]{:S(2)}) collective-permute-start(bf16[512,1024]{1,0:T(8,128)(2,1)} %get-tuple-element.116), channel_id=1, source_target_pairs={{0,1},{1,0},{2,3},{3,2},{4,5},{5,4},{6,7},{7,6},{8,9},{9,8},{10,11... | collective-permute-start | bytes 3145736 | tf_op jit(solution)/shard_map/ppermute | solution.py:61
  1007.2 117.4 %collective-permute-start.107 = (bf16[512,1024]{1,0:T(8,128)(2,1)}, bf16[512,1024]{1,0:T(8,128)(2,1)}, u32[]{:S(2)}, u32[]{:S(2)}) collective-permute-start(bf16[512,1024]{1,0:T(8,128)(2,1)} %get-tuple-element.121), channel_id=1, source_target_pairs={{0,1},{1,0},{2,3},{3,2},{4,5},{5,4},{6,7},{7,6},{8,9},{9,8},{10,11... | collective-permute-start | bytes 3145736 | tf_op jit(solution)/shard_map/ppermute | solution.py:61
  1078.1 145.3 %collective-permute-start.133 = (bf16[512,2048]{1,0:T(8,128)(2,1)}, bf16[512,2048]{1,0:T(8,128)(2,1)S(1)}, u32[]{:S(2)}, u32[]{:S(2)}) collective-permute-start(bf16[512,2048]{1,0:T(8,128)(2,1)} %fusion.75), channel_id=1, source_target_pairs={{0,4},{1,5},{2,6},{3,7},{4,0},{5,1},{6,2},{7,3},{8,12},{9,13},{10,... | collective-permute-start | bytes 6291464 | tf_op jit(solution)/shard_map/ppermute | solution.py:61
  1083.3 37.9 %collective-permute-start.80 = (f32[16,128]{1,0:T(8,128)S(1)}, f32[16,128]{1,0:T(8,128)S(1)}, u32[]{:S(2)}, u32[]{:S(2)}) collective-permute-start(f32[16,128]{1,0:T(8,128)S(1)} %add.893), channel_id=1, source_target_pairs={{0,2},{1,3},{2,0},{3,1},{4,6},{5,7},{6,4},{7,5},{8,10},{9,11},{10,... | collective-permute-start | bytes 24584 | tf_op jit(solution)/shard_map/ppermute | solution.py:61
  1141.8 57.9 %collective-permute-start.84 = (bf16[512,512]{1,0:T(8,128)(2,1)S(1)}, bf16[512,512]{1,0:T(8,128)(2,1)S(1)}, u32[]{:S(2)}, u32[]{:S(2)}) collective-permute-start(bf16[512,512]{1,0:T(8,128)(2,1)S(1)} %convolution_convert_fusion.15), channel_id=1, source_target_pairs={{0,8},{8,0},{16,24},{24,16},{1,9},{9,1},{17,25},{25,17},{2,10},{10... | collective-permute-start | bytes 1572872 | tf_op jit(solution)/shard_map/ppermute | solution.py:57
  1199.7 124.2 %collective-permute-start.143 = (bf16[512,2048]{1,0:T(8,128)(2,1)}, bf16[512,2048]{1,0:T(8,128)(2,1)}, u32[]{:S(2)}, u32[]{:S(2)}) collective-permute-start(bf16[512,2048]{1,0:T(8,128)(2,1)} %fusion.74), channel_id=1, source_target_pairs={{0,4},{1,5},{2,6},{3,7},{4,0},{5,1},{6,2},{7,3},{8,12},{9,13},{10,... | collective-permute-start | bytes 6291464 | tf_op jit(solution)/shard_map/ppermute | solution.py:61
  1209.5 180.5 %collective-permute-start.81 = (f32[16,128]{1,0:T(8,128)S(1)}, f32[16,128]{1,0:T(8,128)S(1)}, u32[]{:S(2)}, u32[]{:S(2)}) collective-permute-start(f32[16,128]{1,0:T(8,128)S(1)} %add.894), channel_id=1, source_target_pairs={{0,4},{1,5},{2,6},{3,7},{4,0},{5,1},{6,2},{7,3},{8,12},{9,13},{10,... | collective-permute-start | bytes 24584 | tf_op jit(solution)/shard_map/ppermute | solution.py:61
  1232.3 88.7 %collective-permute-start.91 = (bf16[128,1024]{1,0:T(8,128)(2,1)S(1)}, bf16[128,1024]{1,0:T(8,128)(2,1)S(1)}, u32[]{:S(2)}, u32[]{:S(2)}) collective-permute-start(bf16[128,1024]{1,0:T(8,128)(2,1)S(1)} %copy-done.196), channel_id=1, source_target_pairs={{0,4},{1,5},{2,6},{3,7},{4,0},{5,1},{6,2},{7,3},{8,12},{9,13},{10,... | collective-permute-start | bytes 786440 | tf_op jit(solution)/shard_map/ppermute | solution.py:61
  1233.4 87.7 %collective-permute-start.90 = (bf16[128,1024]{1,0:T(8,128)(2,1)S(1)}, bf16[128,1024]{1,0:T(8,128)(2,1)S(1)}, u32[]{:S(2)}, u32[]{:S(2)}) collective-permute-start(bf16[128,1024]{1,0:T(8,128)(2,1)S(1)} %copy-done.195), channel_id=1, source_target_pairs={{0,2},{1,3},{2,0},{3,1},{4,6},{5,7},{6,4},{7,5},{8,10},{9,11},{10,... | collective-permute-start | bytes 786440 | tf_op jit(solution)/shard_map/ppermute | solution.py:61
  1251.5 78.7 %collective-permute-start.116 = (bf16[128,1024]{1,0:T(8,128)(2,1)S(1)}, bf16[128,1024]{1,0:T(8,128)(2,1)S(1)}, u32[]{:S(2)}, u32[]{:S(2)}) collective-permute-start(bf16[128,1024]{1,0:T(8,128)(2,1)S(1)} %get-tuple-element.132), channel_id=1, source_target_pairs={{0,6},{1,7},{2,4},{3,5},{4,2},{5,3},{6,0},{7,1},{8,14},{9,15},{10,... | collective-permute-start | bytes 786440 | tf_op jit(solution)/shard_map/ppermute | solution.py:61
  1330.2 64.6 %collective-permute-start.105 = (bf16[512,256]{0,1:T(8,128)(2,1)S(1)}, bf16[512,256]{0,1:T(8,128)(2,1)S(1)}, u32[]{:S(2)}, u32[]{:S(2)}) collective-permute-start(bf16[512,256]{0,1:T(8,128)(2,1)S(1)} %fusion.452), channel_id=1, source_target_pairs={{0,4},{1,5},{2,6},{3,7},{4,0},{5,1},{6,2},{7,3},{8,12},{9,13},{10,... | collective-permute-start | bytes 786440 | tf_op jit(solution)/shard_map/ppermute | solution.py:61
  1337.9 145.4 %collective-permute-start.134 = (bf16[512,2048]{1,0:T(8,128)(2,1)}, bf16[512,2048]{1,0:T(8,128)(2,1)}, u32[]{:S(2)}, u32[]{:S(2)}) collective-permute-start(bf16[512,2048]{1,0:T(8,128)(2,1)} %get-tuple-element.84), channel_id=1, source_target_pairs={{0,1},{1,0},{2,3},{3,2},{4,5},{5,4},{6,7},{7,6},{8,9},{9,8},{10,11... | collective-permute-start | bytes 6291464 | tf_op jit(solution)/shard_map/ppermute | solution.py:61
  1390.0 44.8 %collective-permute-start.135 = (bf16[512,2048]{1,0:T(8,128)(2,1)}, bf16[512,2048]{1,0:T(8,128)(2,1)}, u32[]{:S(2)}, u32[]{:S(2)}) collective-permute-start(bf16[512,2048]{1,0:T(8,128)(2,1)} %get-tuple-element.84), channel_id=1, source_target_pairs={{0,2},{1,3},{2,0},{3,1},{4,6},{5,7},{6,4},{7,5},{8,10},{9,11},{10,... | collective-permute-start | bytes 6291464 | tf_op jit(solution)/shard_map/ppermute | solution.py:61
  1390.0 89.7 %collective-permute-start.145 = (bf16[512,2048]{1,0:T(8,128)(2,1)}, bf16[512,2048]{1,0:T(8,128)(2,1)}, u32[]{:S(2)}, u32[]{:S(2)}) collective-permute-start(bf16[512,2048]{1,0:T(8,128)(2,1)} %get-tuple-element.82), channel_id=1, source_target_pairs={{0,2},{1,3},{2,0},{3,1},{4,6},{5,7},{6,4},{7,5},{8,10},{9,11},{10,... | collective-permute-start | bytes 6291464 | tf_op jit(solution)/shard_map/ppermute | solution.py:61
  1397.9 91.7 %collective-permute-start.144 = (bf16[512,2048]{1,0:T(8,128)(2,1)}, bf16[512,2048]{1,0:T(8,128)(2,1)}, u32[]{:S(2)}, u32[]{:S(2)}) collective-permute-start(bf16[512,2048]{1,0:T(8,128)(2,1)} %get-tuple-element.82), channel_id=1, source_target_pairs={{0,1},{1,0},{2,3},{3,2},{4,5},{5,4},{6,7},{7,6},{8,9},{9,8},{10,11... | collective-permute-start | bytes 6291464 | tf_op jit(solution)/shard_map/ppermute | solution.py:61
  1434.8 61.9 %collective-permute-start.136 = (bf16[512,2048]{1,0:T(8,128)(2,1)}, bf16[512,2048]{1,0:T(8,128)(2,1)S(1)}, u32[]{:S(2)}, u32[]{:S(2)}) collective-permute-start(bf16[512,2048]{1,0:T(8,128)(2,1)} %collective-permute-done.135), channel_id=1, source_target_pairs={{0,1},{1,0},{2,3},{3,2},{4,5},{5,4},{6,7},{7,6},{8,9},{9,8},{10,11... | collective-permute-start | bytes 6291464 | tf_op jit(solution)/shard_map/ppermute | solution.py:61
  1479.7 43.5 %collective-permute-start.146 = (bf16[512,2048]{1,0:T(8,128)(2,1)}, bf16[512,2048]{1,0:T(8,128)(2,1)S(1)}, u32[]{:S(2)}, u32[]{:S(2)}) collective-permute-start(bf16[512,2048]{1,0:T(8,128)(2,1)} %collective-permute-done.145), channel_id=1, source_target_pairs={{0,1},{1,0},{2,3},{3,2},{4,5},{5,4},{6,7},{7,6},{8,9},{9,8},{10,11... | collective-permute-start | bytes 6291464 | tf_op jit(solution)/shard_map/ppermute | solution.py:61
  (375 other events, 5156.9 us)

commit v2 on v1

v2 whole, which is shorter than its diff:
```python
import functools
import math

import jax
import jax.numpy as jnp
from jax import lax
from jax.experimental import pallas as pl
from jax.experimental.pallas import tpu as pltpu
from jax.sharding import PartitionSpec as P

D = 2048
HEADS = 16
HD = 128
QUAD = 4
F32 = jnp.float32
BF16 = jnp.bfloat16


def layer_norm(values, gain, shift):
    center = jnp.mean(values, axis=-1, keepdims=True)
    shifted = values - center
    spread = jnp.mean(shifted * shifted, axis=-1, keepdims=True)
    return shifted * lax.rsqrt(spread + 1e-05) * gain + shift


def layer_norm_back(values, gain, d_out):
    center = jnp.mean(values, axis=-1, keepdims=True)
    shifted = values - center
    spread = jnp.mean(shifted * shifted, axis=-1, keepdims=True)
    r = lax.rsqrt(spread + 1e-05)
    xhat = shifted * r
    e = d_out * gain
    d_values = r * (
        e - jnp.mean(e, axis=-1, keepdims=True) - xhat * jnp.mean(e * xhat, axis=-1, keepdims=True)
    )
    return d_values, jnp.sum(d_out * xhat, axis=0), jnp.sum(d_out, axis=0)


def gelu_and_slope(u):
    a = math.sqrt(2.0 / math.pi)
    t = jnp.tanh(a * (u + 0.044715 * u * u * u))
    half = 0.5 * (1.0 + t)
    slope = half + 0.5 * u * (1.0 - t * t) * a * (1.0 + 3.0 * 0.044715 * u * u)
    return u * half, slope


def dot(a, b):
    return jnp.dot(a, b, preferred_element_type=F32)


def dot_t(a, b):
    return lax.dot_general(a, b, (((1,), (1,)), ((), ())), preferred_element_type=F32)


def t_dot(a, b):
    return lax.dot_general(a, b, (((0,), (0,)), ((), ())), preferred_element_type=F32)


def swap_f(x, bit, size):
    return lax.ppermute(x, "fsdp", [(i, i ^ bit) for i in range(size)])


def swap_k(x, bit, size):
    return lax.ppermute(x, "ctx", [(i, i ^ bit) for i in range(size)])


def bits_of(size):
    out = []
    bit = 1
    while bit < size:
        out.append(bit)
        bit *= 2
    return out


def flip(index, d):
    bit = 1
    while bit <= d:
        if d & bit:
            index = index + bit * (1 - 2 * ((index // bit) % 2))
        bit *= 2
    return index


def head_kernel(
    F, C, vec_ref, place_ref, wkv_ref, wq_ref, vec_out, place_out, wkv_out, wq_out, send, recv, local
):
    f = lax.axis_index("fsdp")
    k = lax.axis_index("ctx")
    core = k % 2
    barrier = pltpu.get_barrier_semaphore()
    partners = [{"fsdp": flip(f, bit)} for bit in bits_of(F)]
    partners += [{"ctx": flip(k, bit)} for bit in bits_of(C)]
    for partner in partners:
        pl.semaphore_signal(barrier, inc=1, device_id=partner, device_id_type=pl.DeviceIdType.MESH)
    pl.semaphore_wait(barrier, len(partners))

    count = [0]
    started = []

    def remote(src, dst, partner):
        n = count[0]
        count[0] += 1
        copy = pltpu.make_async_remote_copy(
            src_ref=src,
            dst_ref=dst,
            send_sem=send.at[n],
            recv_sem=recv.at[n],
            device_id=partner,
            device_id_type=pl.DeviceIdType.MESH,
        )
        copy.start()
        started.append(copy)
        return copy

    own_copies = []

    def keep(src, dst):
        copy = pltpu.make_async_copy(src, dst, local.at[len(own_copies)])
        copy.start()
        own_copies.append(copy)

    def tree(own, place, order, me, axis, handed=None):
        come = {}

        def sends(d, position):
            for p in range(position, len(order)):
                src = own if d == 0 else place(d, d)
                copy = remote(src, place(d ^ order[p], d), {axis: flip(me, order[p])})
                come[d ^ order[p]] = (copy, p + 1)

        sends(0, 0)
        yield
        done = {0}
        while len(done) < len(come) + 1:
            for d in list(come):
                if d in done:
                    continue
                copy, position = come[d]
                copy.wait_recv()
                done.add(d)
                sends(d, position)
                if handed is not None:
                    handed(place(d, d))
                yield

    vec_rows = vec_ref.shape[0]
    trees = [
        tree(vec_ref, lambda d, e: vec_out.at[flip(f, e)], bits_of(F), f, "fsdp"),
    ]
    keep(vec_ref, vec_out.at[f])
    arrivals = []
    for ref, out in ((wkv_ref, wkv_out), (wq_ref, wq_out)):
        rows, width = ref.shape
        half, wide = rows // 2, width // 2
        columns = pl.ds(pl.multiple_of(core * wide, wide), wide)
        keep(ref, out.at[pl.ds(pl.multiple_of(f * rows, rows), rows)])
        for h, order in enumerate((bits_of(F), bits_of(F)[::-1])):

            def place(d, e, out=out, h=h, rows=rows, half=half, columns=columns):
                start = flip(f, e) * rows + h * half
                return out.at[pl.ds(pl.multiple_of(start, half), half), columns]

            def handed(block):
                arrivals.append(remote(block, block, {"ctx": flip(k, 1)}))

            own = ref.at[pl.ds(h * half, half), columns]
            trees.append(tree(own, place, order, f, "fsdp", handed))
    keep(place_ref, place_out.at[0])
    trees.append(tree(place_ref, lambda d, e: place_out.at[d], bits_of(C)[::-1], k, "ctx"))
    while trees:
        for one in list(trees):
            try:
                next(one)
            except StopIteration:
                trees.remove(one)
    for copy in arrivals:
        copy.wait_recv()
    for copy in started:
        copy.wait_send()
    for copy in own_copies:
        copy.wait()


def gather_head(F, C, vec, place, wkv, wq):
    copies = (F - 1) + (C - 1) + 2 * 2 * 2 * (F - 1)
    return pl.pallas_call(
        functools.partial(head_kernel, F, C),
        in_specs=[pl.BlockSpec(memory_space=pl.ANY)] * 4,
        out_specs=[pl.BlockSpec(memory_space=pl.ANY)] * 4,
        out_shape=[
            jax.ShapeDtypeStruct((F,) + vec.shape, vec.dtype),
            jax.ShapeDtypeStruct((C,) + place.shape, place.dtype),
            jax.ShapeDtypeStruct((F * wkv.shape[0], wkv.shape[1]), wkv.dtype),
            jax.ShapeDtypeStruct((F * wq.shape[0], wq.shape[1]), wq.dtype),
        ],
        scratch_shapes=[
            pltpu.SemaphoreType.DMA((copies,)),
            pltpu.SemaphoreType.DMA((copies,)),
            pltpu.SemaphoreType.DMA((4,)),
        ],
        compiler_params=pltpu.CompilerParams(collective_id=0, has_side_effects=True),
        name="gather_head",
    )(vec, place, wkv, wq)


HEAD_STEP = 2
KEY_STEP = 512


def forward_kernel(scale, q_ref, kv_ref, kplace_ref, qplace_ref, o_ref, lse_ref, bias, vt_ref, sc):
    keys = kv_ref.shape[0]

    @pl.when(pl.program_id(0) == 0)
    def _():
        fill_bias(kplace_ref, qplace_ref, bias)
        for at in range(0, keys, KEY_STEP):
            vt_ref[:, at : at + KEY_STEP] = kv_ref[at : at + KEY_STEP, HD:].T

    for h in range(HEAD_STEP):
        q = q_ref[:, h * HD : (h + 1) * HD]
        peak = None
        for at in range(0, keys, KEY_STEP):
            s = dot_t(kv_ref[at : at + KEY_STEP, :HD], q) * scale + bias[at : at + KEY_STEP]
            sc[h, at : at + KEY_STEP] = s
            top = jnp.max(s, axis=0, keepdims=True)
            peak = top if peak is None else jnp.maximum(peak, top)
        total = jnp.zeros_like(peak)
        acc = jnp.zeros((HD, q.shape[0]), F32)
        for at in range(0, keys, KEY_STEP):
            p = jnp.exp(sc[h, at : at + KEY_STEP] - peak)
            total = total + jnp.sum(p, axis=0, keepdims=True)
            acc = acc + dot(vt_ref[:, at : at + KEY_STEP], p.astype(BF16))
        o_ref[:, h * HD : (h + 1) * HD] = (acc / total).T.astype(BF16)
        lse_ref[0, h : h + 1] = peak + jnp.log(total)


def fill_bias(kplace_ref, qplace_ref, bias):
    for at in range(0, bias.shape[0], KEY_STEP):
        seg_k = kplace_ref[at : at + KEY_STEP, 0:1]
        pos_k = kplace_ref[at : at + KEY_STEP, 1:2]
        seg_q = qplace_ref[0:1]
        pos_q = qplace_ref[1:2]
        seen = (pos_k <= pos_q) & ((seg_k == 0) | (seg_k == seg_q))
        bias[at : at + KEY_STEP] = jnp.where(seen, 0.0, -1e30)


def backward_kernel(
    scale, q_ref, do_ref, o_ref, lse_ref, kv_ref, kplace_ref, qplace_ref, dq_ref, dkv_ref, bias, kt_ref
):
    keys = kv_ref.shape[0]

    @pl.when(pl.program_id(0) == 0)
    def _():
        fill_bias(kplace_ref, qplace_ref, bias)
        dkv_ref[...] = jnp.zeros_like(dkv_ref)
        for at in range(0, keys, KEY_STEP):
            kt_ref[:, at : at + KEY_STEP] = kv_ref[at : at + KEY_STEP, :HD].T

    for h in range(HEAD_STEP):
        q = q_ref[:, h * HD : (h + 1) * HD]
        do = do_ref[:, h * HD : (h + 1) * HD]
        o = o_ref[:, h * HD : (h + 1) * HD]
        inner = jnp.sum((do.astype(F32) * o.astype(F32)).T, axis=0, keepdims=True)
        lse = lse_ref[0, h : h + 1]
        dq = jnp.zeros((HD, q.shape[0]), F32)
        for at in range(0, keys, KEY_STEP):
            rows = slice(at, at + KEY_STEP)
            s = dot_t(kv_ref[rows, :HD], q) * scale + bias[rows]
            p = jnp.exp(s - lse)
            dp = dot_t(kv_ref[rows, HD:], do)
            ds = (p * (dp - inner)).astype(BF16)
            dkv_ref[rows, HD:] += dot(p.astype(BF16), do)
            dkv_ref[rows, :HD] += dot(ds, q)
            dq = dq + dot(kt_ref[:, rows], ds)
        dq_ref[:, h * HD : (h + 1) * HD] = (dq * scale).T.astype(BF16)


def attend_forward(queries, kv, kplace, qplace, scale):
    rows = queries.shape[0]
    keys = kv.shape[0]
    whole = lambda x: pl.BlockSpec(x.shape, lambda h: (0,) * x.ndim)
    heads = pl.BlockSpec((rows, HEAD_STEP * HD), lambda h: (0, h))
    return pl.pallas_call(
        functools.partial(forward_kernel, scale),
        grid=(HEADS // HEAD_STEP,),
        in_specs=[heads, whole(kv), whole(kplace), whole(qplace)],
        out_specs=[heads, pl.BlockSpec((1, HEAD_STEP, rows), lambda h: (h, 0, 0))],
        out_shape=[
            jax.ShapeDtypeStruct((rows, HEADS * HD), BF16),
            jax.ShapeDtypeStruct((HEADS // HEAD_STEP, HEAD_STEP, rows), F32),
        ],
        scratch_shapes=[
            pltpu.VMEM((keys, rows), F32),
            pltpu.VMEM((HD, keys), BF16),
            pltpu.VMEM((HEAD_STEP, keys, rows), F32),
        ],
        compiler_params=pltpu.CompilerParams(vmem_limit_bytes=32 * 1024 * 1024),
        cost_estimate=pl.CostEstimate(
            flops=8 * rows * keys * HEADS * HD,
            bytes_accessed=4 * rows * HEADS * HD,
            transcendentals=rows * keys * HEADS,
        ),
        name="attend_forward",
    )(queries, kv, kplace, qplace)


def attend_backward(queries, d_mixed, mixed, lse, kv, kplace, qplace, scale):
    rows = queries.shape[0]
    keys = kv.shape[0]
    whole = lambda x: pl.BlockSpec(x.shape, lambda h: (0,) * x.ndim)
    heads = pl.BlockSpec((rows, HEAD_STEP * HD), lambda h: (0, h))
    return pl.pallas_call(
        functools.partial(backward_kernel, scale),
        grid=(HEADS // HEAD_STEP,),
        in_specs=[
            heads,
            heads,
            heads,
            pl.BlockSpec((1, HEAD_STEP, rows), lambda h: (h, 0, 0)),
            whole(kv),
            whole(kplace),
            whole(qplace),
        ],
        out_specs=[heads, pl.BlockSpec((keys, 2 * HD), lambda h: (0, 0))],
        out_shape=[
            jax.ShapeDtypeStruct((rows, HEADS * HD), BF16),
            jax.ShapeDtypeStruct((keys, 2 * HD), F32),
        ],
        scratch_shapes=[pltpu.VMEM((keys, rows), F32), pltpu.VMEM((HD, keys), BF16)],
        compiler_params=pltpu.CompilerParams(vmem_limit_bytes=32 * 1024 * 1024),
        cost_estimate=pl.CostEstimate(
            flops=18 * rows * keys * HEADS * HD,
            bytes_accessed=8 * rows * HEADS * HD,
            transcendentals=rows * keys * HEADS,
        ),
        name="attend_backward",
    )(queries, d_mixed, mixed, lse, kv, kplace, qplace)


def build(F, C):
    Z = C // 2

    def per_device(
        hidden_in,
        segment_ids,
        positions,
        norm1_gain,
        norm1_bias,
        query_weight,
        query_bias,
        keyval_weight,
        value_bias,
        out_weight,
        out_bias,
        norm2_gain,
        norm2_bias,
        fc_weight,
        fc_bias,
        proj_weight,
        proj_bias,
        out_grad,
    ):
        micros, rows = hidden_in.shape[:2]
        tok = micros * rows
        scale = 1.0 / math.sqrt(HD)
        f = lax.axis_index("fsdp")
        k = lax.axis_index("ctx")
        core = k % 2
        quad = k % QUAD
        zi = k // 2
        hsh = D // F
        width = fc_weight.shape[1] // F // QUAD

        def pick_core(a, b):
            return jnp.where(core == 0, a, b)

        def in_order(own, other):
            return pick_core(
                jnp.concatenate([own, other], axis=1), jnp.concatenate([other, own], axis=1)
            )

        def halves(x):
            w = x.shape[1] // 2
            return pick_core(x[:, :w], x[:, w:]), pick_core(x[:, w:], x[:, :w])

        def after(x, *deps):
            return lax.optimization_barrier((x,) + deps)[0]

        def behind(x, *deps):
            zero = sum(
                jnp.minimum(jnp.abs(d[(slice(0, 1),) * d.ndim].reshape(()).astype(F32)), 0.0)
                for d in deps
            )
            return (x.astype(F32) + zero).astype(x.dtype)

        def swk(x, bit):
            return swap_k(x, bit, C)

        def gather_ctx(x):
            held = {0: x}
            for bit in bits_of(C)[1:][::-1] + [1]:
                for d in list(held):
                    held[d ^ bit] = swk(held[d], bit)
            return [held[d] for d in range(C)]

        def gather_quad(x):
            a = swk(x, 1)
            b = swk(x, 2)
            c = swk(b, 1)
            return [x, b, a, c]

        names = (
            norm1_gain, norm1_bias, query_bias, out_bias, norm2_gain, norm2_bias, proj_bias,
            fc_bias, value_bias,
        )
        sizes = [v.shape[0] for v in names]
        packed = jnp.concatenate(names)
        pad = -packed.shape[0] % 2048
        packed = jnp.pad(packed, (0, pad)).reshape(-1, 128)
        places = jnp.concatenate([segment_ids, positions], axis=0)
        vec, places, w_keyval, w_query = gather_head(
            F, C, packed, places, keyval_weight, query_weight
        )
        vec = vec.reshape(F, -1).astype(F32)
        full = []
        at = 0
        for size in sizes:
            full.append(vec[:, at : at + size])
            at += size
        gain_one, shift_one, b_query, b_out, gain_two, shift_two, b_proj = [
            v.reshape(-1) for v in full[:7]
        ]
        b_value = full[8].reshape(-1)
        b_fc = lax.dynamic_slice(
            full[7].reshape(F, QUAD, width), (0, quad, 0), (F, 1, width)
        ).reshape(-1)
        kv_bias = jnp.concatenate([jnp.zeros((HD,), F32), b_value])

        seg_all = [places[:, m].reshape(-1) for m in range(micros)]
        pos_all = [places[:, micros + m].reshape(-1) for m in range(micros)]

        wo_own = lax.all_gather(halves(out_weight)[0], "fsdp", axis=0, tiled=True)
        wo_other = swk(wo_own, 1)

        fc_piece = jnp.concatenate(
            [
                lax.dynamic_slice(fc_weight, (0, (j * QUAD + quad) * width), (hsh, width))
                for j in range(F)
            ],
            axis=1,
        )
        proj_piece = lax.dynamic_slice(proj_weight, (quad * width, 0), (width, D))
        w_fc = lax.all_gather(fc_piece, "fsdp", axis=0, tiled=True)
        w_proj = lax.all_gather(proj_piece, "fsdp", axis=0, tiled=True)

        hidden = hidden_in.reshape(tok, D).astype(F32)
        normed1 = layer_norm(hidden, gain_one, shift_one).astype(BF16)
        keyvals = (dot(normed1, w_keyval) + kv_bias).astype(BF16)
        group_kv = jnp.concatenate(
            gather_ctx(keyvals.reshape(micros, rows, 2 * HD)), axis=1
        )
        queries = (dot(normed1, w_query) + b_query).astype(BF16)
        kplace = [jnp.stack([seg_all[m], pos_all[m]], axis=1) for m in range(micros)]
        qplace = [jnp.stack([segment_ids[m], positions[m]]) for m in range(micros)]
        queries = [queries[m * rows : (m + 1) * rows] for m in range(micros)]
        mixed = []
        lse = []
        middle = []
        normed2_blocks = []
        for m in range(micros):
            mix, lse_rows = attend_forward(
                queries[m], group_kv[m], kplace[m], qplace[m], scale
            )
            mixed.append(mix)
            lse.append(lse_rows)
            mid = (
                hidden[m * rows : (m + 1) * rows]
                + in_order(dot(mix, wo_own), dot(mix, wo_other))
                + b_out
            )
            middle.append(mid)
            normed2_blocks.append(gather_quad(layer_norm(mid, gain_two, shift_two).astype(BF16)))
        all_mixed = jnp.concatenate(mixed, axis=0)
        middle = jnp.concatenate(middle, axis=0)
        normed2 = jnp.concatenate(
            [normed2_blocks[m][d] for d in range(QUAD) for m in range(micros)], axis=0
        )
        cot_own = out_grad.reshape(tok, D)
        cot = jnp.concatenate(gather_quad(after(cot_own, group_kv)), axis=0)

        active, slope = gelu_and_slope(dot(normed2, w_fc) + b_fc)
        active = active.astype(BF16)
        slope = slope.astype(BF16)

        def scatter(term):
            return lax.psum_scatter(term, "fsdp", scatter_dimension=0, tiled=True)

        def ffn_grad(left, right):
            term = t_dot(left, right).astype(BF16)
            return lax.psum_scatter(term, "fsdp", scatter_dimension=0, tiled=True), term

        proj_grad, proj_term = ffn_grad(active, cot)

        def reduce_quad(x, product):
            got = swk(product(x[2 * tok :]).astype(BF16), 1).astype(F32)
            passed = (product(x[tok : 2 * tok]) + got[tok:]).astype(BF16)
            own = product(x[:tok]) + got[:tok]
            outs = []
            for m in range(micros):
                at = slice(m * rows, (m + 1) * rows)
                outs.append(own[at] + swk(passed[at], 2).astype(F32))
            return outs

        d_before = (dot_t(after(cot, proj_term), w_proj) * slope.astype(F32)).astype(BF16)
        d_normed2 = reduce_quad(d_before, lambda x: dot_t(x, w_fc))
        fc_grad, fc_term = ffn_grad(normed2, d_before)
        fc_b_grad = jnp.sum(d_before.astype(F32), axis=0)

        d_middle, gain_two_grad, shift_two_grad = layer_norm_back(
            middle, gain_two, jnp.concatenate(d_normed2, axis=0)
        )
        d_middle = cot_own.astype(F32) + d_middle
        d_branch = d_middle.astype(BF16)
        branch_own, branch_other = halves(d_branch)
        d_mixed = (dot_t(branch_own, wo_own) + dot_t(branch_other, wo_other)).astype(BF16)
        def across_quads(x):
            for bit in bits_of(C)[2:]:
                cut = x.shape[0] // 2
                first = swk(x[:cut], bit)
                second = swk(behind(x[cut:], first), bit)
                got = jnp.concatenate([first, second])
                x = (x.astype(F32) + got.astype(F32)).astype(BF16)
            return x

        d_mixed = behind(d_mixed, proj_grad)
        proj_sum = across_quads(proj_grad)
        d_mixed = [d_mixed[m * rows : (m + 1) * rows] for m in range(micros)]
        kv_scale = jnp.concatenate([jnp.full((HD,), scale, F32), jnp.ones((HD,), F32)])
        d_queries = []
        d_keyvals = []
        for m in range(micros):
            dq, dkv = attend_backward(
                queries[m], d_mixed[m], mixed[m], lse[m], group_kv[m], kplace[m], qplace[m], scale
            )
            d_queries.append(dq)
            terms = (dkv * kv_scale).reshape(C, rows, 2 * HD)
            terms = {d: terms[d] for d in range(C)}
            for bit in [1] + bits_of(C)[1:][::-1]:
                sent = [d for d in terms if d & bit]
                got = swk(jnp.stack([terms[d] for d in sent]).astype(BF16), bit)
                for i, d in enumerate(sent):
                    terms[d ^ bit] = terms[d ^ bit] + got[i].astype(F32)
                    del terms[d]
            d_keyvals.append(terms[0].astype(BF16))
        d_queries = jnp.concatenate(d_queries, axis=0)
        d_keyvals = jnp.concatenate(d_keyvals, axis=0)
        fc_sum = across_quads(fc_grad)
        dq_own, dq_other = halves(d_queries)
        dq_pair = jnp.concatenate([dq_own, swk(dq_other, 1)], axis=0)
        normed1_pair = jnp.concatenate([normed1, swk(normed1, 1)], axis=0)
        query_term = t_dot(normed1_pair, dq_pair).astype(BF16)
        query_w_grad = scatter(query_term)
        branch_own, branch_other = halves(behind(d_branch, query_term))
        branch_pair = jnp.concatenate([branch_own, swk(branch_other, 1)], axis=0)
        mixed_pair = jnp.concatenate([all_mixed, swk(all_mixed, 1)], axis=0)
        out_term = t_dot(mixed_pair, branch_pair).astype(BF16)
        out_w_grad = scatter(out_term)
        ffn = reduce_quad(after(active, fc_term), lambda x: dot(x, w_proj))
        result = middle + jnp.concatenate(ffn, axis=0) + b_proj
        hidden_out = result.astype(BF16).reshape(micros, rows, D)
        keyval_w_grad = scatter(t_dot(normed1, d_keyvals).astype(BF16)).astype(F32)
        d_normed1 = (
            dot_t(d_queries, w_query) + dot_t(behind(d_keyvals, proj_sum), w_keyval)
        )
        d_hidden, gain_one_grad, shift_one_grad = layer_norm_back(hidden, gain_one, d_normed1)
        hidden_grad = (d_middle + d_hidden).reshape(micros, rows, D)

        def sum_z(x):
            part = x.shape[0] // Z
            blocks = x.astype(BF16).reshape(Z, part, x.shape[1])
            terms = [
                lax.dynamic_slice(blocks, (zi ^ d, 0, 0), (1,) + blocks.shape[1:])[0].astype(F32)
                for d in range(Z)
            ]
            terms = dict(enumerate(terms))
            for bit in bits_of(Z):
                sent = [d for d in terms if d & bit]
                got = swk(jnp.concatenate([terms[d] for d in sent]).astype(BF16), 2 * bit)
                for i, d in enumerate(sent):
                    terms[d ^ bit] = terms[d ^ bit] + got[i * part : (i + 1) * part].astype(F32)
                    del terms[d]
            held = terms[0].astype(BF16)
            ids = [0]
            for bit in bits_of(Z)[::-1]:
                held = jnp.concatenate([held, swk(held, 2 * bit)])
                ids = ids + [d ^ bit for d in ids]
            out = jnp.full(blocks.shape, 0.125, BF16)
            for i, d in enumerate(ids):
                block = held[i * part : (i + 1) * part]
                out = lax.dynamic_update_slice(out, block[None], (zi ^ d, 0, 0))
            own = out.reshape(x.shape)
            return in_order(own, swk(own, 1)).astype(F32)

        members = (0, 2, 1, 3)
        proj_out = jnp.full((QUAD * width, D), 1.0, F32)
        for d, part in zip(members, gather_quad(proj_sum)):
            proj_out = lax.dynamic_update_slice(proj_out, part.astype(F32), ((quad ^ d) * width, 0))
        fc_parts = jnp.full((QUAD, hsh, F * width), 0.75, BF16)
        for d, part in zip(members, gather_quad(fc_sum)):
            fc_parts = lax.dynamic_update_slice(fc_parts, part[None], (quad ^ d, 0, 0))
        fc_out = jnp.concatenate(
            [
                fc_parts[i][:, j * width : (j + 1) * width]
                for j in range(F)
                for i in range(QUAD)
            ],
            axis=1,
        ).astype(F32)
        out_out = sum_z(out_w_grad)
        query_out = sum_z(query_w_grad)
        kv_sum = keyval_w_grad
        for bit in bits_of(C):
            kv_sum = kv_sum + swk(kv_sum.astype(BF16), bit).astype(F32)

        fc_b_full = lax.dynamic_update_slice(
            jnp.zeros((F, QUAD, width), F32), fc_b_grad.reshape(F, 1, width), (0, quad, 0)
        )

        def sum_vectors(vectors):
            sizes = [v.size // F for v in vectors]
            packed = jnp.concatenate([v.reshape(F, -1) for v in vectors], axis=1)
            packed = jnp.pad(packed, ((0, 0), (0, -packed.shape[1] % 1024)))
            packed = packed.reshape(F, -1, 128)

            def one(d):
                return lax.dynamic_slice(packed, (f ^ d, 0, 0), (1,) + packed.shape[1:])[0]

            total = one(0)
            for d in range(1, F):
                total = total + swap_f(one(d), d, F)
            for bit in bits_of(C):
                total = total + swk(total, bit)
            total = total.reshape(-1)
            outs = []
            at = 0
            for size in sizes:
                outs.append(total[at : at + size])
                at += size
            return outs

        def column_sum(x):
            return jnp.sum(x.astype(F32), axis=0)

        g1, s1, bq, bv, g2, s2, bp, bo, bf = sum_vectors(
            [
                gain_one_grad,
                shift_one_grad,
                behind(column_sum(d_queries), fc_sum),
                column_sum(d_keyvals[:, HD:]),
                gain_two_grad,
                shift_two_grad,
                column_sum(cot_own),
                column_sum(d_branch),
                fc_b_full,
            ]
        )
        return (
            hidden_out, hidden_grad, g1, s1, query_out, bq, kv_sum, bv, out_out, bo, g2, s2,
            fc_out, bf, proj_out, bp,
        )

    return per_device


def solution(mesh):
    tokens = P(None, ("fsdp", "ctx"), None)
    places = P(None, ("fsdp", "ctx"))
    vec = P("fsdp")
    mat = P("fsdp", None)
    grads = (vec, vec, mat, vec, mat, vec, mat, vec, vec, vec, mat, vec, mat, vec)
    return jax.shard_map(
        build(mesh.shape["fsdp"], mesh.shape["ctx"]),
        mesh=mesh,
        in_specs=(tokens, places, places) + grads + (tokens,),
        out_specs=(tokens, tokens) + grads,
        check_vma=False,
    )
```

time: 1540 us -> 1090 us (0.71)
  matrix products: 468 us -> 244 us
  Pallas kernels: 0 us -> 166 us
  starting transfers between devices: 200 us -> 49.3 us
  other arithmetic: 191 us -> 102 us
  local copies, waits for them, and re-layouts: 188 us -> 99 us
  waiting for transfers between devices: 485 us -> 397 us
    pallas_call x0 -> x5, Pallas kernels: none -> 166 us  [the longest x1 78.6 us: gather_head(): pl.pallas_call(functools.partial(head_kernel, F, C), in_specs=[pl.BlockSp...]
    dot_general x96 -> x0, matrix products: 153 us -> none  [the longest x16 43.6 us: attend_backward(): jnp.einsum('qhd,kd->hqk', grad_block, values, preferred_element_type=F32)]
    ppermute x69 -> x3, waiting for transfers between devices: 131 us -> 0.01 us  [swap_f(): return lax.ppermute(x, 'fsdp', [(i, i ^ bit) for i in range(size)])]
    ppermute x78 -> x59, starting transfers between devices: 144 us -> 45.6 us  [swap_k(): return lax.ppermute(x, 'ctx', [(i, i ^ bit) for i in range(size)])]
    ppermute x69 -> x3, starting transfers between devices: 55.7 us -> 2.71 us  [swap_f(): return lax.ppermute(x, 'fsdp', [(i, i ^ bit) for i in range(size)])]
    dot_general x40 -> x5, matrix products: 110 us -> 64.3 us  [t_dot(): lax.dot_general(a, b, (((0,), (0,)), ((), ())), preferred_element_type=F32)]
    convert_element_type x20 -> x7, other arithmetic: 56.2 us -> 10.8 us  [the longest x2 6.66 us: reduce_quad(): got = swk(product(x[2 * tok:]).astype(BF16), 1).astype(F32)]
    dynamic_update_slice x56 -> x9, local copies, waits for them, and re-layouts: 48.4 us -> 4.14 us  [the longest x3 4.01 us: per_device(): fc_parts = lax.dynamic_update_slice(fc_parts, part[None], (quad ^ d, 0, 0))]
  transfers between devices with their start and end apart: 147 -> 70, of which waited for: 54 -> 24; matrix products, arithmetic and copies ran while one was open for 52% -> 40% of each run, Pallas kernels for 0% -> 15%
where the time goes in v2:
time: 1090 us; the launch traced here: 1080 us
  waiting for transfers between devices  397 us (36%)
  matrix products  244 us (22%)
  Pallas kernels  166 us (15%)
  other arithmetic  102 us (9%)
  local copies, waits for them, and re-layouts  99 us (9%)
  starting transfers between devices  49.3 us (5%)
  between operations  20.4 us (2%)
    ppermute x59, waiting for transfers between devices, swap_k(): return lax.ppermute(x, 'ctx', [(i, i ^ bit) for i in range(size)])  397 us
    dot_general x8, matrix products, dot_t(): lax.dot_general(a, b, (((1,), (1,)), ((), ())), preferred_element_type=F32)  91.3 us
    dot_general x10, matrix products, dot(): return jnp.dot(a, b, preferred_element_type=F32)  88.5 us
    pallas_call x1, Pallas kernels, gather_head(): pl.pallas_call(functools.partial(head_kernel, F, C), in_specs=[pl.BlockSp...  78.6 us
    dot_general x5, matrix products, t_dot(): lax.dot_general(a, b, (((0,), (0,)), ((), ())), preferred_element_type=F32)  64.3 us
    unnamed x221, local copies, waits for them, and re-layouts  50.3 us
    pallas_call x2, Pallas kernels, attend_backward(): pl.pallas_call(functools.partial(backward_kernel, scale), grid=(HEADS //...  47.8 us
    ppermute x59, starting transfers between devices, swap_k(): return lax.ppermute(x, 'ctx', [(i, i ^ bit) for i in range(size)])  45.6 us
  transfers between devices with their start and end apart: 70, of which 24 were waited for; matrix products, arithmetic and copies ran while one was open for 40% of the time, Pallas kernels for 15%

profile of v2, /device:TPU:1, one launch (start us, length us, event | category | flops | bytes accessed | tf_op | source)
XLA Modules:
  0.0 1077.6 jit_solution(16670700711351770550)
XLA Ops:
  16.8 78.6 %gather_head.1 = (bf16[4,48,128]{2,1,0:T(8,128)(2,1)}, s32[8,4,256]{2,1,0:T(4,128)}, bf16[2048,256]{1,0:T(8,128)(2,1)}, bf16[2048,2048]{1,0:T(8,128)(2,1)}) custom-call(bf16[48,128]{1,0:T(8,128)(2,1)} %pad_bitcast_fusion.1.vec_ref, s32[4,256]{1,0:T(4,128)} %pad_add_fusion.2.place_ref, bf16[512,256]{1,0:T(8,128)(2,1)} %wkv_ref.1, bf16[512,2048]{1,0:T(8,128)(2,1)} %wq_ref.1), custom_call_target="tpu_custom_call" | custom-call | tf_op jit(solution)/shard_map/gather_head/pallas_call | solution.py:187
  109.4 8.5 add_convert_fusion.6
  143.0 19.9 %attend_forward.2 = (bf16[256,2048]{1,0:T(8,128)(2,1)S(1)}, f32[8,2,256]{2,1,0:T(2,128)S(1)}) custom-call(bf16[256,2048]{1,0:T(8,128)(2,1)S(1)} %copy-done.7, bf16[2048,256]{1,0:T(8,128)(2,1)S(1)} %get-tuple-element.110.kv_ref, s32[2048,2]{1,0:T(8,128)S(1)} %copy.38.kplace_ref, s32[2,256]{1,0:T(2,128)S(1)} %get-tuple-element.160.qplace_ref), custom_call_target="tpu_custom_call" | custom-call | flops 8589934592 | bytes 2097152 | tf_op jit(solution)/shard_map/attend_forward/pallas_call | solution.py:284
  163.1 19.7 %attend_forward.3 = (bf16[256,2048]{1,0:T(8,128)(2,1)S(1)}, f32[8,2,256]{2,1,0:T(2,128)S(1)}) custom-call(bf16[256,2048]{1,0:T(8,128)(2,1)S(1)} %get-tuple-element.113.q_ref, bf16[2048,256]{1,0:T(8,128)(2,1)S(1)} %get-tuple-element.111.kv_ref, s32[2048,2]{1,0:T(8,128)S(1)} %copy.39.kplace_ref, s32[2,256]{1,0:T(2,128)S(1)} %get-tuple-element.161.qplace_ref), custom_call_target="tpu_custom_call" | custom-call | flops 8589934592 | bytes 2097152 | tf_op jit(solution)/shard_map/attend_forward/pallas_call | solution.py:284
  207.3 20.2 %collective-permute-done.8 = bf16[256,2048]{1,0:T(8,128)(2,1)S(1)} collective-permute-done((bf16[256,2048]{1,0:T(8,128)(2,1)S(1)}, bf16[256,2048]{1,0:T(8,128)(2,1)S(1)}, u32[]{:S(2)}, u32[]{:S(2)}) %collective-permute-start.8) | collective-permute-done | bytes 1048608 | tf_op jit(solution)/shard_map/ppermute | solution.py:64
  228.8 21.2 %collective-permute-done.9 = bf16[256,2048]{1,0:T(8,128)(2,1)S(1)} collective-permute-done((bf16[256,2048]{1,0:T(8,128)(2,1)S(1)}, bf16[256,2048]{1,0:T(8,128)(2,1)S(1)}, u32[]{:S(2)}, u32[]{:S(2)}) %collective-permute-start.9) | collective-permute-done | bytes 1048608 | tf_op jit(solution)/shard_map/ppermute | solution.py:64
  257.2 28.6 %multiply_convert_fusion.1 = (bf16[2048,2048]{1,0:T(8,128)(2,1)S(1)}, f32[2048,2048]{1,0:T(8,128)}) fusion(f32[2048]{0:T(1024)S(1)} %bitcast.343, bf16[2048,2048]{1,0:T(8,128)(2,1)} %constant_dynamic-update-slice_fusion.8, bf16[2048,2048]{1,0:T(8,128)(2,1)} %all-gather.6.cloned.1.call-done), kind=kOutput, calls=%fused_computation.10 | convolution fusion | flops 17221812224 | bytes 41951232 | tf_op jit(solution)/shard_map/dot_general | solution.py:48
  289.2 20.7 %convolution_convert_fusion.1 = bf16[2048,2048]{1,0:T(8,128)(2,1)} fusion(bf16[2048,2048]{1,0:T(8,128)(2,1)S(1)} %get-tuple-element.39, bf16[2048,2048]{1,0:T(8,128)(2,1)S(1)} %copy-done.47), kind=kOutput, calls=%fused_computation.13 | convolution fusion | flops 17184063488 | bytes 25165824 | tf_op jit(solution)/shard_map/dot_general | solution.py:56
  310.0 34.9 %convert_reduce_fusion = (f32[2048]{0:T(1024)S(1)}, bf16[2048,2048]{1,0:T(8,128)(2,1)}) fusion(f32[2048,2048]{1,0:T(8,128)} %get-tuple-element.156, f32[2048]{0:T(1024)S(1)} %bitcast.344, bf16[2048,2048]{1,0:T(8,128)(2,1)} %copy-done.46, bf16[2048,2048]{1,0:T(8,128)(2,1)} %all-gather.8.cloned.1.call-done), kind=kOutput, calls=%fused_computation.8 | convolution fusion | flops 17280530432 | bytes 41959424 | tf_op jit(solution)/shard_map/dot_general | solution.py:52
  344.8 14.3 %fusion.33 = bf16[1024,2048]{1,0:T(8,128)(2,1)} fusion(bf16[2048,2048]{1,0:T(8,128)(2,1)} %all-gather.6.cloned.1.call-done, bf16[2048,2048]{1,0:T(8,128)(2,1)} %get-tuple-element.159), kind=kOutput, calls=%fused_computation.68 | convolution fusion | flops 8592031744 | bytes 16777216 | tf_op jit(solution)/shard_map/dot_general | solution.py:52
  359.1 22.4 %convolution_convert_fusion = bf16[2048,2048]{1,0:T(8,128)(2,1)} fusion(bf16[2048,2048]{1,0:T(8,128)(2,1)} %constant_dynamic-update-slice_fusion.8, bf16[2048,2048]{1,0:T(8,128)(2,1)S(1)} %copy-done.80), kind=kOutput, calls=%fused_computation.12 | convolution fusion | flops 17184063488 | bytes 25165824 | tf_op jit(solution)/shard_map/dot_general | solution.py:56
  381.5 14.1 %fusion.30 = bf16[1024,2048]{1,0:T(8,128)(2,1)} fusion(bf16[2048,2048]{1,0:T(8,128)(2,1)} %all-gather.8.cloned.1.call-done, bf16[2048,2048]{1,0:T(8,128)(2,1)} %copy-done.81), kind=kOutput, calls=%fused_computation.67 | convolution fusion | flops 8592031744 | bytes 16777216 | tf_op jit(solution)/shard_map/dot_general | solution.py:48
  407.0 9.3 fusion.7
  422.4 12.0 %fusion.10 = bf16[512,2048]{1,0:T(8,128)(2,1)S(1)} fusion(f32[1024,2048]{1,0:T(8,128)S(1)} %convert_element_type.412, bf16[2048,2048]{1,0:T(8,128)(2,1)} %all-gather.8.cloned.1.call-done, bf16[2048,2048]{1,0:T(8,128)(2,1)} %copy-done.81), kind=kOutput, calls=%fused_computation.23 | convolution fusion | flops 4297064448 | bytes 16777216 | tf_op jit(solution)/shard_map/dot_general | solution.py:48
  436.8 8.0 slice_add_fusion.1
  444.8 20.1 %collective-permute-done.22 = bf16[256,2048]{1,0:T(8,128)(2,1)S(1)} collective-permute-done((bf16[256,2048]{1,0:T(8,128)(2,1)S(1)}, bf16[256,2048]{1,0:T(8,128)(2,1)S(1)}, u32[]{:S(2)}, u32[]{:S(2)}) %collective-permute-start.22) | collective-permute-done | bytes 1048608 | tf_op jit(solution)/shard_map/ppermute | solution.py:64
  469.0 4.9 fusion.122
  475.2 4.4 fusion.66
  481.4 6.5 add_convert_fusion.3
  489.5 24.0 %attend_backward.2 = (bf16[256,2048]{1,0:T(8,128)(2,1)S(1)}, f32[2048,256]{1,0:T(8,128)S(1)}) custom-call(bf16[256,2048]{1,0:T(8,128)(2,1)S(1)} %copy-done.8, bf16[256,2048]{1,0:T(8,128)(2,1)S(1)} %get-tuple-element.105.do_ref, bf16[256,2048]{1,0:T(8,128)(2,1)S(1)} %copy-done.1, f32[8,2,256]{2,1,0:T(2,128)S(1)} %get-tuple-element.40.lse_ref, ...), custom_call_target="tpu_custom_call" | custom-call | flops 19327352832 | bytes 4194304 | tf_op jit(solution)/shard_map/attend_backward/pallas_call | solution.py:313
  513.5 23.8 %attend_backward.3 = (bf16[256,2048]{1,0:T(8,128)(2,1)S(1)}, f32[2048,256]{1,0:T(8,128)S(1)}) custom-call(bf16[256,2048]{1,0:T(8,128)(2,1)S(1)} %copy-done.6, bf16[256,2048]{1,0:T(8,128)(2,1)S(1)} %get-tuple-element.104.do_ref, bf16[256,2048]{1,0:T(8,128)(2,1)S(1)} %copy-done.3, f32[8,2,256]{2,1,0:T(2,128)S(1)} %get-tuple-element.42.lse_ref, ...), custom_call_target="tpu_custom_call" | custom-call | flops 19327352832 | bytes 4194304 | tf_op jit(solution)/shard_map/attend_backward/pallas_call | solution.py:313
  545.1 15.6 %collective-permute-done.27 = bf16[2,256,256]{2,1,0:T(8,128)(2,1)S(1)} collective-permute-done((bf16[2,256,256]{2,1,0:T(8,128)(2,1)S(1)}, bf16[2,256,256]{2,1,0:T(8,128)(2,1)S(1)}, u32[]{:S(2)}, u32[]{:S(2)}) %collective-permute-start.27) | collective-permute-done | bytes 262176 | tf_op jit(solution)/shard_map/ppermute | solution.py:64
  561.4 5.0 collective-permute-done.24
  567.0 25.2 %collective-permute-done.28 = bf16[1,256,256]{2,1,0:T(8,128)(2,1)S(1)} collective-permute-done((bf16[1,256,256]{2,1,0:T(8,128)(2,1)S(1)}, bf16[1,256,256]{2,1,0:T(8,128)(2,1)S(1)}, u32[]{:S(2)}, u32[]{:S(2)}) %collective-permute-start.28) | collective-permute-done | bytes 131104 | tf_op jit(solution)/shard_map/ppermute | solution.py:64
  592.3 4.5 collective-permute-done.25
  602.1 11.8 %slice_add_fusion.3 = f32[512,2048]{1,0:T(8,128)} fusion(f32[1024,2048]{1,0:T(8,128)} %copy-done.34, bf16[2048,2048]{1,0:T(8,128)(2,1)} %all-gather.8.cloned.1.call-done, bf16[2048,2048]{1,0:T(8,128)(2,1)} %copy-done.81), kind=kOutput, calls=%fused_computation.24 | convolution fusion | flops 4296015872 | bytes 18874368 | tf_op jit(solution)/shard_map/dot_general | solution.py:48
  614.0 4.4 convert_reduce_fusion.2
  618.5 9.4 fusion.27
  642.3 9.7 fusion.139
  652.1 56.0 %collective-permute-done.29 = bf16[256,2048]{1,0:T(8,128)(2,1)} collective-permute-done((bf16[256,2048]{1,0:T(8,128)(2,1)}, bf16[256,2048]{1,0:T(8,128)(2,1)}, u32[]{:S(2)}, u32[]{:S(2)}) %collective-permute-start.29) | collective-permute-done | bytes 1048608 | tf_op jit(solution)/shard_map/ppermute | solution.py:64
  710.0 20.6 %collective-permute-done.31 = bf16[256,2048]{1,0:T(8,128)(2,1)} collective-permute-done((bf16[256,2048]{1,0:T(8,128)(2,1)}, bf16[256,2048]{1,0:T(8,128)(2,1)}, u32[]{:S(2)}, u32[]{:S(2)}) %collective-permute-start.31) | collective-permute-done | bytes 1048608 | tf_op jit(solution)/shard_map/ppermute | solution.py:64
  742.5 61.9 %collective-permute-done.32 = bf16[256,2048]{1,0:T(8,128)(2,1)S(1)} collective-permute-done((bf16[256,2048]{1,0:T(8,128)(2,1)S(1)}, bf16[256,2048]{1,0:T(8,128)(2,1)S(1)}, u32[]{:S(2)}, u32[]{:S(2)}) %collective-permute-start.32) | collective-permute-done | bytes 1048608 | tf_op jit(solution)/shard_map/ppermute | solution.py:64
  812.2 14.7 %collective-permute-done.30 = bf16[256,2048]{1,0:T(8,128)(2,1)S(1)} collective-permute-done((bf16[256,2048]{1,0:T(8,128)(2,1)S(1)}, bf16[256,2048]{1,0:T(8,128)(2,1)S(1)}, u32[]{:S(2)}, u32[]{:S(2)}) %collective-permute-start.30) | collective-permute-done | bytes 1048608 | tf_op jit(solution)/shard_map/ppermute | solution.py:64
  826.9 8.3 broadcast.176
  835.3 4.4 convert_dynamic-update-slice_fusion.3
  848.9 8.4 fusion.24
  862.0 55.8 %collective-permute-done.37 = f32[48,128]{1,0:T(8,128)S(1)} collective-permute-done((f32[48,128]{1,0:T(8,128)S(1)}, f32[48,128]{1,0:T(8,128)S(1)}, u32[]{:S(2)}, u32[]{:S(2)}) %collective-permute-start.37) | collective-permute-done | bytes 24608 | tf_op jit(solution)/shard_map/ppermute | solution.py:64
  919.1 5.7 multiply_add_fusion.1
  930.0 10.9 %collective-permute-done.48 = bf16[512,256]{1,0:T(8,128)(2,1)S(1)} collective-permute-done((bf16[512,256]{1,0:T(8,128)(2,1)S(1)}, bf16[512,256]{1,0:T(8,128)(2,1)S(1)}, u32[]{:S(2)}, u32[]{:S(2)}) %collective-permute-start.48) | collective-permute-done | bytes 262176 | tf_op jit(solution)/shard_map/ppermute | solution.py:64
  969.2 7.3 collective-permute-done.41
  984.8 8.3 collective-permute-done.42
  993.4 7.0 collective-permute-done.51
  1002.6 10.5 collective-permute-done.43
  1013.2 5.5 collective-permute-done.52
  1021.0 7.4 collective-permute-done.53
  1031.9 4.3 collective-permute-done.44
  1037.0 9.1 collective-permute-done.54
  1049.0 11.7 %convert_element_type.510 = f32[512,8192]{1,0:T(8,128)} convert(bf16[512,8192]{1,0:T(8,128)(2,1)} %slice_dynamic-update-slice_fusion) | non-fusion elementwise | flops 4194304 | bytes 25165824 | tf_op jit(solution)/shard_map/convert_element_type | solution.py:619
  (506 shorter events, 237.5 us)
Async XLA Ops:
  7.2 113.4 %all-gather.4.cloned.1.call-start = ((), (), s32[]{:S(2)}) async-start(), calls=%async_computation.5 | async-start | bytes 5242880 | tf_op jit(solution)/shard_map/all_gather | solution.py:443
  9.9 247.3 %all-gather.6.cloned.1.call-start = ((), (), s32[]{:S(2)}) async-start(), calls=%async_computation.6 | async-start | bytes 10485760 | tf_op jit(solution)/shard_map/all_gather | solution.py:454
  13.4 296.5 %all-gather.8.cloned.1.call-start = ((), (), s32[]{:S(2)}) async-start(), calls=%async_computation.7 | async-start | bytes 10485760 | tf_op jit(solution)/shard_map/all_gather | solution.py:455
  103.5 27.1 %collective-permute-start = (bf16[2,256,256]{2,1,0:T(8,128)(2,1)}, bf16[2,256,256]{2,1,0:T(8,128)(2,1)}, u32[]{:S(2)}, u32[]{:S(2)}) collective-permute-start(bf16[2,256,256]{2,1,0:T(8,128)(2,1)} %bitcast.3), channel_id=1, source_target_pairs={{0,1},{1,0},{2,3},{3,2},{4,5},{5,4},{6,7},{7,6},{8,9},{9,8},{10,11... | collective-permute-start | bytes 786440 | tf_op jit(solution)/shard_map/ppermute | solution.py:64
  103.6 20.9 %collective-permute-start.1 = (bf16[2,256,256]{2,1,0:T(8,128)(2,1)}, bf16[2,256,256]{2,1,0:T(8,128)(2,1)}, u32[]{:S(2)}, u32[]{:S(2)}) collective-permute-start(bf16[2,256,256]{2,1,0:T(8,128)(2,1)} %bitcast.3), channel_id=1, source_target_pairs={{0,2},{1,3},{2,0},{3,1},{4,6},{5,7},{6,4},{7,5},{8,10},{9,11},{10,... | collective-permute-start | bytes 786440 | tf_op jit(solution)/shard_map/ppermute | solution.py:64
  108.8 370.8 %reduce-scatter.6.cloned.1.call-start = ((), (), s32[]{:S(2)}) async-start(), calls=%async_computation.8 | async-start | bytes 10485760 | tf_op jit(solution)/shard_map/reduce_scatter | solution.py:501
  120.5 69.9 %collective-permute-start.7 = (bf16[2048,1024]{1,0:T(8,128)(2,1)}, bf16[2048,1024]{1,0:T(8,128)(2,1)}, u32[]{:S(2)}, u32[]{:S(2)}) collective-permute-start(bf16[2048,1024]{1,0:T(8,128)(2,1)} %all-gather.4.cloned.1.call-done), channel_id=1, source_target_pairs={{0,1},{1,0},{2,3},{3,2},{4,5},{5,4},{6,7},{7,6},{8,9},{9,8},{10,11... | collective-permute-start | bytes 12582920 | tf_op jit(solution)/shard_map/ppermute | solution.py:64
  139.6 47.0 %collective-permute-start.14 = (bf16[512,2048]{1,0:T(8,128)(2,1)}, bf16[512,2048]{1,0:T(8,128)(2,1)S(1)}, u32[]{:S(2)}, u32[]{:S(2)}) collective-permute-start(bf16[512,2048]{1,0:T(8,128)(2,1)} %bitcast.294), channel_id=1, source_target_pairs={{0,2},{1,3},{2,0},{3,1},{4,6},{5,7},{6,4},{7,5},{8,10},{9,11},{10,... | collective-permute-start | bytes 6291464 | tf_op jit(solution)/shard_map/ppermute | solution.py:64
  140.6 66.4 %collective-permute-start.15 = (bf16[512,2048]{1,0:T(8,128)(2,1)}, bf16[512,2048]{1,0:T(8,128)(2,1)S(1)}, u32[]{:S(2)}, u32[]{:S(2)}) collective-permute-start(bf16[512,2048]{1,0:T(8,128)(2,1)} %bitcast.295), channel_id=1, source_target_pairs={{0,1},{1,0},{2,3},{3,2},{4,5},{5,4},{6,7},{7,6},{8,9},{9,8},{10,11... | collective-permute-start | bytes 6291464 | tf_op jit(solution)/shard_map/ppermute | solution.py:64
  186.6 42.0 %collective-permute-start.16 = (bf16[512,2048]{1,0:T(8,128)(2,1)S(1)}, bf16[512,2048]{1,0:T(8,128)(2,1)S(1)}, u32[]{:S(2)}, u32[]{:S(2)}) collective-permute-start(bf16[512,2048]{1,0:T(8,128)(2,1)S(1)} %collective-permute-done.14), channel_id=1, source_target_pairs={{0,1},{1,0},{2,3},{3,2},{4,5},{5,4},{6,7},{7,6},{8,9},{9,8},{10,11... | collective-permute-start | bytes 6291464 | tf_op jit(solution)/shard_map/ppermute | solution.py:64
  202.7 24.8 %collective-permute-start.8 = (bf16[256,2048]{1,0:T(8,128)(2,1)S(1)}, bf16[256,2048]{1,0:T(8,128)(2,1)S(1)}, u32[]{:S(2)}, u32[]{:S(2)}) collective-permute-start(bf16[256,2048]{1,0:T(8,128)(2,1)S(1)} %get-tuple-element.74), channel_id=1, source_target_pairs={{0,2},{1,3},{2,0},{3,1},{4,6},{5,7},{6,4},{7,5},{8,10},{9,11},{10,... | collective-permute-start | bytes 3145736 | tf_op jit(solution)/shard_map/ppermute | solution.py:64
  205.6 44.4 %collective-permute-start.9 = (bf16[256,2048]{1,0:T(8,128)(2,1)S(1)}, bf16[256,2048]{1,0:T(8,128)(2,1)S(1)}, u32[]{:S(2)}, u32[]{:S(2)}) collective-permute-start(bf16[256,2048]{1,0:T(8,128)(2,1)S(1)} %get-tuple-element.70), channel_id=1, source_target_pairs={{0,2},{1,3},{2,0},{3,1},{4,6},{5,7},{6,4},{7,5},{8,10},{9,11},{10,... | collective-permute-start | bytes 3145736 | tf_op jit(solution)/shard_map/ppermute | solution.py:64
  206.4 46.5 %collective-permute-start.10 = (bf16[256,2048]{1,0:T(8,128)(2,1)S(1)}, bf16[256,2048]{1,0:T(8,128)(2,1)S(1)}, u32[]{:S(2)}, u32[]{:S(2)}) collective-permute-start(bf16[256,2048]{1,0:T(8,128)(2,1)S(1)} %get-tuple-element.74), channel_id=1, source_target_pairs={{0,1},{1,0},{2,3},{3,2},{4,5},{5,4},{6,7},{7,6},{8,9},{9,8},{10,11... | collective-permute-start | bytes 3145736 | tf_op jit(solution)/shard_map/ppermute | solution.py:64
  207.0 46.9 %collective-permute-start.11 = (bf16[256,2048]{1,0:T(8,128)(2,1)S(1)}, bf16[256,2048]{1,0:T(8,128)(2,1)S(1)}, u32[]{:S(2)}, u32[]{:S(2)}) collective-permute-start(bf16[256,2048]{1,0:T(8,128)(2,1)S(1)} %get-tuple-element.70), channel_id=1, source_target_pairs={{0,1},{1,0},{2,3},{3,2},{4,5},{5,4},{6,7},{7,6},{8,9},{9,8},{10,11... | collective-permute-start | bytes 3145736 | tf_op jit(solution)/shard_map/ppermute | solution.py:64
  227.4 27.6 %collective-permute-start.12 = (bf16[256,2048]{1,0:T(8,128)(2,1)S(1)}, bf16[256,2048]{1,0:T(8,128)(2,1)S(1)}, u32[]{:S(2)}, u32[]{:S(2)}) collective-permute-start(bf16[256,2048]{1,0:T(8,128)(2,1)S(1)} %collective-permute-done.8), channel_id=1, source_target_pairs={{0,1},{1,0},{2,3},{3,2},{4,5},{5,4},{6,7},{7,6},{8,9},{9,8},{10,11... | collective-permute-start | bytes 3145736 | tf_op jit(solution)/shard_map/ppermute | solution.py:64
  309.9 329.0 %reduce-scatter.8.cloned.1.call-start = ((), (), s32[]{:S(2)}) async-start(), calls=%async_computation.9 | async-start | bytes 10485760 | tf_op jit(solution)/shard_map/reduce_scatter | solution.py:501
  359.1 44.7 %collective-permute-start.20 = (bf16[1024,2048]{1,0:T(8,128)(2,1)}, bf16[1024,2048]{1,0:T(8,128)(2,1)}, u32[]{:S(2)}, u32[]{:S(2)}) collective-permute-start(bf16[1024,2048]{1,0:T(8,128)(2,1)} %fusion.33), channel_id=1, source_target_pairs={{0,1},{1,0},{2,3},{3,2},{4,5},{5,4},{6,7},{7,6},{8,9},{9,8},{10,11... | collective-permute-start | bytes 12582920 | tf_op jit(solution)/shard_map/ppermute | solution.py:64
  395.6 23.3 %collective-permute-start.17 = (bf16[1024,2048]{1,0:T(8,128)(2,1)}, bf16[1024,2048]{1,0:T(8,128)(2,1)}, u32[]{:S(2)}, u32[]{:S(2)}) collective-permute-start(bf16[1024,2048]{1,0:T(8,128)(2,1)} %fusion.30), channel_id=1, source_target_pairs={{0,1},{1,0},{2,3},{3,2},{4,5},{5,4},{6,7},{7,6},{8,9},{9,8},{10,11... | collective-permute-start | bytes 12582920 | tf_op jit(solution)/shard_map/ppermute | solution.py:64
  396.1 222.4 %collective-permute-start.39 = (bf16[512,2048]{1,0:T(8,128)(2,1)}, bf16[512,2048]{1,0:T(8,128)(2,1)}, u32[]{:S(2)}, u32[]{:S(2)}) collective-permute-start(bf16[512,2048]{1,0:T(8,128)(2,1)} %add_convert_fusion.7), channel_id=1, source_target_pairs={{0,1},{1,0},{2,3},{3,2},{4,5},{5,4},{6,7},{7,6},{8,9},{9,8},{10,11... | collective-permute-start | bytes 6291464 | tf_op jit(solution)/shard_map/ppermute | solution.py:64
  399.1 449.2 %collective-permute-start.49 = (bf16[512,2048]{1,0:T(8,128)(2,1)}, bf16[512,2048]{1,0:T(8,128)(2,1)}, u32[]{:S(2)}, u32[]{:S(2)}) collective-permute-start(bf16[512,2048]{1,0:T(8,128)(2,1)} %pad_maximum_fusion.4), channel_id=1, source_target_pairs={{0,1},{1,0},{2,3},{3,2},{4,5},{5,4},{6,7},{7,6},{8,9},{9,8},{10,11... | collective-permute-start | bytes 6291464 | tf_op jit(solution)/shard_map/ppermute | solution.py:64
  402.7 456.7 %reduce-scatter.12.cloned.1.call-start = ((), (), s32[]{:S(2)}) async-start(), calls=%async_computation.11 | async-start | bytes 1310720 | tf_op jit(solution)/shard_map/reduce_scatter | solution.py:497
  417.5 27.3 %collective-permute-start.21 = (bf16[256,2048]{1,0:T(8,128)(2,1)}, bf16[256,2048]{1,0:T(8,128)(2,1)S(1)}, u32[]{:S(2)}, u32[]{:S(2)}) collective-permute-start(bf16[256,2048]{1,0:T(8,128)(2,1)} %get-tuple-element.106), channel_id=1, source_target_pairs={{0,2},{1,3},{2,0},{3,1},{4,6},{5,7},{6,4},{7,5},{8,10},{9,11},{10,... | collective-permute-start | bytes 3145736 | tf_op jit(solution)/shard_map/ppermute | solution.py:64
  418.5 46.4 %collective-permute-start.22 = (bf16[256,2048]{1,0:T(8,128)(2,1)S(1)}, bf16[256,2048]{1,0:T(8,128)(2,1)S(1)}, u32[]{:S(2)}, u32[]{:S(2)}) collective-permute-start(bf16[256,2048]{1,0:T(8,128)(2,1)S(1)} %get-tuple-element.107), channel_id=1, source_target_pairs={{0,2},{1,3},{2,0},{3,1},{4,6},{5,7},{6,4},{7,5},{8,10},{9,11},{10,... | collective-permute-start | bytes 3145736 | tf_op jit(solution)/shard_map/ppermute | solution.py:64
  436.0 192.2 %collective-permute-start.18 = (bf16[256,2048]{1,0:T(8,128)(2,1)}, bf16[256,2048]{1,0:T(8,128)(2,1)}, u32[]{:S(2)}, u32[]{:S(2)}) collective-permute-start(bf16[256,2048]{1,0:T(8,128)(2,1)} %get-tuple-element.108), channel_id=1, source_target_pairs={{0,2},{1,3},{2,0},{3,1},{4,6},{5,7},{6,4},{7,5},{8,10},{9,11},{10,... | collective-permute-start | bytes 3145736 | tf_op jit(solution)/shard_map/ppermute | solution.py:64
  540.9 19.8 %collective-permute-start.27 = (bf16[2,256,256]{2,1,0:T(8,128)(2,1)S(1)}, bf16[2,256,256]{2,1,0:T(8,128)(2,1)S(1)}, u32[]{:S(2)}, u32[]{:S(2)}) collective-permute-start(bf16[2,256,256]{2,1,0:T(8,128)(2,1)S(1)} %pad_maximum_fusion.13), channel_id=1, source_target_pairs={{0,4},{1,5},{2,6},{3,7},{4,0},{5,1},{6,2},{7,3},{8,12},{9,13},{10,... | collective-permute-start | bytes 786440 | tf_op jit(solution)/shard_map/ppermute | solution.py:64
  543.0 23.4 %collective-permute-start.24 = (bf16[2,256,256]{2,1,0:T(8,128)(2,1)S(1)}, bf16[2,256,256]{2,1,0:T(8,128)(2,1)S(1)}, u32[]{:S(2)}, u32[]{:S(2)}) collective-permute-start(bf16[2,256,256]{2,1,0:T(8,128)(2,1)S(1)} %pad_maximum_fusion.12), channel_id=1, source_target_pairs={{0,4},{1,5},{2,6},{3,7},{4,0},{5,1},{6,2},{7,3},{8,12},{9,13},{10,... | collective-permute-start | bytes 786440 | tf_op jit(solution)/shard_map/ppermute | solution.py:64
  560.7 67.5 %collective-permute-start.19 = (bf16[256,2048]{1,0:T(8,128)(2,1)}, bf16[256,2048]{1,0:T(8,128)(2,1)}, u32[]{:S(2)}, u32[]{:S(2)}) collective-permute-start(bf16[256,2048]{1,0:T(8,128)(2,1)} %get-tuple-element.109), channel_id=1, source_target_pairs={{0,2},{1,3},{2,0},{3,1},{4,6},{5,7},{6,4},{7,5},{8,10},{9,11},{10,... | collective-permute-start | bytes 3145736 | tf_op jit(solution)/shard_map/ppermute | solution.py:64
  566.4 25.9 %collective-permute-start.28 = (bf16[1,256,256]{2,1,0:T(8,128)(2,1)S(1)}, bf16[1,256,256]{2,1,0:T(8,128)(2,1)S(1)}, u32[]{:S(2)}, u32[]{:S(2)}) collective-permute-start(bf16[1,256,256]{2,1,0:T(8,128)(2,1)S(1)} %fusion.88), channel_id=1, source_target_pairs={{0,2},{1,3},{2,0},{3,1},{4,6},{5,7},{6,4},{7,5},{8,10},{9,11},{10,... | collective-permute-start | bytes 393224 | tf_op jit(solution)/shard_map/ppermute | solution.py:64
  596.8 21.7 %collective-permute-start.40 = (bf16[512,1024]{1,0:T(8,128)(2,1)}, bf16[512,1024]{1,0:T(8,128)(2,1)}, u32[]{:S(2)}, u32[]{:S(2)}) collective-permute-start(bf16[512,1024]{1,0:T(8,128)(2,1)} %get-tuple-element.103), channel_id=1, source_target_pairs={{0,1},{1,0},{2,3},{3,2},{4,5},{5,4},{6,7},{7,6},{8,9},{9,8},{10,11... | collective-permute-start | bytes 3145736 | tf_op jit(solution)/shard_map/ppermute | solution.py:64
  601.7 360.5 %reduce-scatter.10.cloned.1.call-start = ((), (), s32[]{:S(2)}) async-start(), calls=%async_computation.10 | async-start | bytes 5242880 | tf_op jit(solution)/shard_map/reduce_scatter | solution.py:497
  628.0 351.5 %reduce-scatter.14.cloned.1.call-start = ((), (), s32[]{:S(2)}) async-start(), calls=%async_computation.12 | async-start | bytes 5242880 | tf_op jit(solution)/shard_map/reduce_scatter | solution.py:497
  637.2 70.9 %collective-permute-start.29 = (bf16[256,2048]{1,0:T(8,128)(2,1)}, bf16[256,2048]{1,0:T(8,128)(2,1)}, u32[]{:S(2)}, u32[]{:S(2)}) collective-permute-start(bf16[256,2048]{1,0:T(8,128)(2,1)} %slice.659), channel_id=1, source_target_pairs={{0,4},{1,5},{2,6},{3,7},{4,0},{5,1},{6,2},{7,3},{8,12},{9,13},{10,... | collective-permute-start | bytes 3145736 | tf_op jit(solution)/shard_map/ppermute | solution.py:64
  641.4 89.3 %collective-permute-start.31 = (bf16[256,2048]{1,0:T(8,128)(2,1)}, bf16[256,2048]{1,0:T(8,128)(2,1)}, u32[]{:S(2)}, u32[]{:S(2)}) collective-permute-start(bf16[256,2048]{1,0:T(8,128)(2,1)} %slice.663), channel_id=1, source_target_pairs={{0,4},{1,5},{2,6},{3,7},{4,0},{5,1},{6,2},{7,3},{8,12},{9,13},{10,... | collective-permute-start | bytes 3145736 | tf_op jit(solution)/shard_map/ppermute | solution.py:64
  733.9 70.5 %collective-permute-start.32 = (bf16[256,2048]{1,0:T(8,128)(2,1)S(1)}, bf16[256,2048]{1,0:T(8,128)(2,1)S(1)}, u32[]{:S(2)}, u32[]{:S(2)}) collective-permute-start(bf16[256,2048]{1,0:T(8,128)(2,1)S(1)} %add_convert_fusion.8), channel_id=1, source_target_pairs={{0,4},{1,5},{2,6},{3,7},{4,0},{5,1},{6,2},{7,3},{8,12},{9,13},{10,... | collective-permute-start | bytes 3145736 | tf_op jit(solution)/shard_map/ppermute | solution.py:64
  736.6 90.3 %collective-permute-start.30 = (bf16[256,2048]{1,0:T(8,128)(2,1)S(1)}, bf16[256,2048]{1,0:T(8,128)(2,1)S(1)}, u32[]{:S(2)}, u32[]{:S(2)}) collective-permute-start(bf16[256,2048]{1,0:T(8,128)(2,1)S(1)} %add_convert_fusion.9), channel_id=1, source_target_pairs={{0,4},{1,5},{2,6},{3,7},{4,0},{5,1},{6,2},{7,3},{8,12},{9,13},{10,... | collective-permute-start | bytes 3145736 | tf_op jit(solution)/shard_map/ppermute | solution.py:64
  741.1 107.4 %collective-permute-start.50 = (bf16[512,1024]{1,0:T(8,128)(2,1)}, bf16[512,1024]{1,0:T(8,128)(2,1)}, u32[]{:S(2)}, u32[]{:S(2)}) collective-permute-start(bf16[512,1024]{1,0:T(8,128)(2,1)} %get-tuple-element.101), channel_id=1, source_target_pairs={{0,1},{1,0},{2,3},{3,2},{4,5},{5,4},{6,7},{7,6},{8,9},{9,8},{10,11... | collective-permute-start | bytes 3145736 | tf_op jit(solution)/shard_map/ppermute | solution.py:64
  810.6 131.3 %collective-permute-start.56 = (bf16[512,2048]{1,0:T(8,128)(2,1)}, bf16[512,2048]{1,0:T(8,128)(2,1)}, u32[]{:S(2)}, u32[]{:S(2)}) collective-permute-start(bf16[512,2048]{1,0:T(8,128)(2,1)} %get-tuple-element.58), channel_id=1, source_target_pairs={{0,2},{1,3},{2,0},{3,1},{4,6},{5,7},{6,4},{7,5},{8,10},{9,11},{10,... | collective-permute-start | bytes 6291464 | tf_op jit(solution)/shard_map/ppermute | solution.py:64
  810.6 133.7 %collective-permute-start.57 = (bf16[512,2048]{1,0:T(8,128)(2,1)}, bf16[512,2048]{1,0:T(8,128)(2,1)}, u32[]{:S(2)}, u32[]{:S(2)}) collective-permute-start(bf16[512,2048]{1,0:T(8,128)(2,1)} %get-tuple-element.58), channel_id=1, source_target_pairs={{0,1},{1,0},{2,3},{3,2},{4,5},{5,4},{6,7},{7,6},{8,9},{9,8},{10,11... | collective-permute-start | bytes 6291464 | tf_op jit(solution)/shard_map/ppermute | solution.py:64
  857.4 85.0 %collective-permute-start.59 = (bf16[512,2048]{1,0:T(8,128)(2,1)}, bf16[512,2048]{1,0:T(8,128)(2,1)}, u32[]{:S(2)}, u32[]{:S(2)}) collective-permute-start(bf16[512,2048]{1,0:T(8,128)(2,1)} %copy-done.42), channel_id=1, source_target_pairs={{0,2},{1,3},{2,0},{3,1},{4,6},{5,7},{6,4},{7,5},{8,10},{9,11},{10,... | collective-permute-start | bytes 6291464 | tf_op jit(solution)/shard_map/ppermute | solution.py:64
  859.4 58.4 %collective-permute-start.46 = (bf16[512,256]{1,0:T(8,128)(2,1)}, bf16[512,256]{1,0:T(8,128)(2,1)S(1)}, u32[]{:S(2)}, u32[]{:S(2)}) collective-permute-start(bf16[512,256]{1,0:T(8,128)(2,1)} %reduce-scatter.12.cloned.1.call-done), channel_id=1, source_target_pairs={{0,1},{1,0},{2,3},{3,2},{4,5},{5,4},{6,7},{7,6},{8,9},{9,8},{10,11... | collective-permute-start | bytes 786440 | tf_op jit(solution)/shard_map/ppermute | solution.py:64
  860.3 57.5 %collective-permute-start.37 = (f32[48,128]{1,0:T(8,128)S(1)}, f32[48,128]{1,0:T(8,128)S(1)}, u32[]{:S(2)}, u32[]{:S(2)}) collective-permute-start(f32[48,128]{1,0:T(8,128)S(1)} %add.507), channel_id=1, source_target_pairs={{0,2},{1,3},{2,0},{3,1},{4,6},{5,7},{6,4},{7,5},{8,10},{9,11},{10,... | collective-permute-start | bytes 73736 | tf_op jit(solution)/shard_map/ppermute | solution.py:64
  924.9 25.5 %collective-permute-start.60 = (bf16[512,2048]{1,0:T(8,128)(2,1)S(1)}, bf16[512,2048]{1,0:T(8,128)(2,1)S(1)}, u32[]{:S(2)}, u32[]{:S(2)}) collective-permute-start(bf16[512,2048]{1,0:T(8,128)(2,1)S(1)} %copy-done.43), channel_id=1, source_target_pairs={{0,1},{1,0},{2,3},{3,2},{4,5},{5,4},{6,7},{7,6},{8,9},{9,8},{10,11... | collective-permute-start | bytes 6291464 | tf_op jit(solution)/shard_map/ppermute | solution.py:64
  942.3 118.4 %collective-permute-start.61 = (bf16[512,2048]{1,0:T(8,128)(2,1)}, bf16[512,2048]{1,0:T(8,128)(2,1)}, u32[]{:S(2)}, u32[]{:S(2)}) collective-permute-start(bf16[512,2048]{1,0:T(8,128)(2,1)} %collective-permute-done.59), channel_id=1, source_target_pairs={{0,1},{1,0},{2,3},{3,2},{4,5},{5,4},{6,7},{7,6},{8,9},{9,8},{10,11... | collective-permute-start | bytes 6291464 | tf_op jit(solution)/shard_map/ppermute | solution.py:64
  980.8 19.7 %collective-permute-start.51 = (bf16[256,1024]{1,0:T(8,128)(2,1)S(1)}, bf16[256,1024]{1,0:T(8,128)(2,1)S(1)}, u32[]{:S(2)}, u32[]{:S(2)}) collective-permute-start(bf16[256,1024]{1,0:T(8,128)(2,1)S(1)} %pad_maximum_fusion.9), channel_id=1, source_target_pairs={{0,2},{1,3},{2,0},{3,1},{4,6},{5,7},{6,4},{7,5},{8,10},{9,11},{10,... | collective-permute-start | bytes 1572872 | tf_op jit(solution)/shard_map/ppermute | solution.py:64
  993.3 19.8 %collective-permute-start.43 = (bf16[128,1024]{1,0:T(8,128)(2,1)S(1)}, bf16[128,1024]{1,0:T(8,128)(2,1)S(1)}, u32[]{:S(2)}, u32[]{:S(2)}) collective-permute-start(bf16[128,1024]{1,0:T(8,128)(2,1)S(1)} %get-tuple-element.62), channel_id=1, source_target_pairs={{0,4},{1,5},{2,6},{3,7},{4,0},{5,1},{6,2},{7,3},{8,12},{9,13},{10,... | collective-permute-start | bytes 786440 | tf_op jit(solution)/shard_map/ppermute | solution.py:64
  1013.1 23.1 %collective-permute-start.44 = (bf16[256,1024]{1,0:T(8,128)(2,1)S(1)}, bf16[256,1024]{1,0:T(8,128)(2,1)S(1)}, u32[]{:S(2)}, u32[]{:S(2)}) collective-permute-start(bf16[256,1024]{1,0:T(8,128)(2,1)S(1)} %pad_maximum_fusion.8), channel_id=1, source_target_pairs={{0,2},{1,3},{2,0},{3,1},{4,6},{5,7},{6,4},{7,5},{8,10},{9,11},{10,... | collective-permute-start | bytes 1572872 | tf_op jit(solution)/shard_map/ppermute | solution.py:64
  1036.3 28.6 %collective-permute-start.45 = (bf16[512,1024]{1,0:T(8,128)(2,1)S(1)}, bf16[512,1024]{1,0:T(8,128)(2,1)S(1)}, u32[]{:S(2)}, u32[]{:S(2)}) collective-permute-start(bf16[512,1024]{1,0:T(8,128)(2,1)S(1)} %bitcast.301), channel_id=1, source_target_pairs={{0,1},{1,0},{2,3},{3,2},{4,5},{5,4},{6,7},{7,6},{8,9},{9,8},{10,11... | collective-permute-start | bytes 3145736 | tf_op jit(solution)/shard_map/ppermute | solution.py:64
  1046.1 21.5 %collective-permute-start.55 = (bf16[512,1024]{1,0:T(8,128)(2,1)S(1)}, bf16[512,1024]{1,0:T(8,128)(2,1)S(1)}, u32[]{:S(2)}, u32[]{:S(2)}) collective-permute-start(bf16[512,1024]{1,0:T(8,128)(2,1)S(1)} %bitcast.299), channel_id=1, source_target_pairs={{0,1},{1,0},{2,3},{3,2},{4,5},{5,4},{6,7},{7,6},{8,9},{9,8},{10,11... | collective-permute-start | bytes 3145736 | tf_op jit(solution)/shard_map/ppermute | solution.py:64
  (106 other events, 1474.3 us)
Sparse Core Ops, SparseCore 0:
  10.4 84.6 all-gather.3
  97.5 86.5 all-gather.5
  186.0 87.6 all-gather.7
  310.0 85.7 reduce-scatter.5
  402.8 85.7 reduce-scatter.7
  601.8 26.9 reduce-scatter.11
  632.1 52.6 reduce-scatter.9
  862.1 51.1 reduce-scatter.13

commit v3 on v2

--- a/solution.py
+++ b/solution.py
@@ -480,7 +480,10 @@
                 + b_out
             )
             middle.append(mid)
-            normed2_blocks.append(gather_quad(layer_norm(mid, gain_two, shift_two).astype(BF16)))
+            normed2_own = layer_norm(mid, gain_two, shift_two).astype(BF16)
+            normed2_blocks.append(gather_quad(normed2_own))
+            if m + 1 < micros:
+                queries[m + 1] = behind(queries[m + 1], normed2_own)
         all_mixed = jnp.concatenate(mixed, axis=0)
         middle = jnp.concatenate(middle, axis=0)
         normed2 = jnp.concatenate(
@@ -506,57 +509,49 @@
             got = swk(product(x[2 * tok :]).astype(BF16), 1).astype(F32)
             passed = (product(x[tok : 2 * tok]) + got[tok:]).astype(BF16)
             own = product(x[:tok]) + got[:tok]
+            return [swk(passed[m * rows : (m + 1) * rows], 2) for m in range(micros)], passed, own
+
+        d_before = (dot_t(after(cot, proj_term), w_proj) * slope.astype(F32)).astype(BF16)
+        came, passed, own = reduce_quad(d_before, lambda x: dot_t(x, w_fc))
+        d_normed2 = own + jnp.concatenate(came).astype(F32)
+        fc_grad, fc_term = ffn_grad(after(normed2, passed), d_before)
+        fc_b_grad = jnp.sum(d_before.astype(F32), axis=0)
+
+        def across_quads(x, parts):
+            size = x.shape[0] // parts
             outs = []
-            for m in range(micros):
-                at = slice(m * rows, (m + 1) * rows)
-                outs.append(own[at] + swk(passed[at], 2).astype(F32))
+            for i in range(parts):
+                block = x[i * size : (i + 1) * size]
+                if i:
+                    block = behind(block, outs[-1])
+                for bit in bits_of(C)[2:]:
+                    block = (block.astype(F32) + swk(block, bit).astype(F32)).astype(BF16)
+                outs.append(block)
             return outs
 
-        d_before = (dot_t(after(cot, proj_term), w_proj) * slope.astype(F32)).astype(BF16)
-        d_normed2 = reduce_quad(d_before, lambda x: dot_t(x, w_fc))
-        fc_grad, fc_term = ffn_grad(normed2, d_before)
-        fc_b_grad = jnp.sum(d_before.astype(F32), axis=0)
+        proj_sums = across_quads(proj_grad, 4)
+        ffn, ffn_passed, ffn_own = reduce_quad(after(active, fc_term), lambda x: dot(x, w_proj))
 
         d_middle, gain_two_grad, shift_two_grad = layer_norm_back(
-            middle, gain_two, jnp.concatenate(d_normed2, axis=0)
+            behind(middle, proj_sums[0], ffn_passed, ffn_own), gain_two, d_normed2
         )
         d_middle = cot_own.astype(F32) + d_middle
         d_branch = d_middle.astype(BF16)
         branch_own, branch_other = halves(d_branch)
         d_mixed = (dot_t(branch_own, wo_own) + dot_t(branch_other, wo_other)).astype(BF16)
-        def across_quads(x):
-            for bit in bits_of(C)[2:]:
-                cut = x.shape[0] // 2
-                first = swk(x[:cut], bit)
-                second = swk(behind(x[cut:], first), bit)
-                got = jnp.concatenate([first, second])
-                x = (x.astype(F32) + got.astype(F32)).astype(BF16)
-            return x
-
-        d_mixed = behind(d_mixed, proj_grad)
-        proj_sum = across_quads(proj_grad)
         d_mixed = [d_mixed[m * rows : (m + 1) * rows] for m in range(micros)]
         kv_scale = jnp.concatenate([jnp.full((HD,), scale, F32), jnp.ones((HD,), F32)])
         d_queries = []
-        d_keyvals = []
+        kv_terms = []
         for m in range(micros):
+            d_mixed[m] = behind(d_mixed[m], proj_sums[m + 1], *d_queries)
             dq, dkv = attend_backward(
                 queries[m], d_mixed[m], mixed[m], lse[m], group_kv[m], kplace[m], qplace[m], scale
             )
             d_queries.append(dq)
-            terms = (dkv * kv_scale).reshape(C, rows, 2 * HD)
-            terms = {d: terms[d] for d in range(C)}
-            for bit in [1] + bits_of(C)[1:][::-1]:
-                sent = [d for d in terms if d & bit]
-                got = swk(jnp.stack([terms[d] for d in sent]).astype(BF16), bit)
-                for i, d in enumerate(sent):
-                    terms[d ^ bit] = terms[d ^ bit] + got[i].astype(F32)
-                    del terms[d]
-            d_keyvals.append(terms[0].astype(BF16))
+            kv_terms.append(dkv)
         d_queries = jnp.concatenate(d_queries, axis=0)
-        d_keyvals = jnp.concatenate(d_keyvals, axis=0)
-        fc_sum = across_quads(fc_grad)
-        dq_own, dq_other = halves(d_queries)
+        dq_own, dq_other = halves(behind(d_queries, proj_sums[3]))
         dq_pair = jnp.concatenate([dq_own, swk(dq_other, 1)], axis=0)
         normed1_pair = jnp.concatenate([normed1, swk(normed1, 1)], axis=0)
         query_term = t_dot(normed1_pair, dq_pair).astype(BF16)
@@ -565,18 +560,36 @@
         branch_pair = jnp.concatenate([branch_own, swk(branch_other, 1)], axis=0)
         mixed_pair = jnp.concatenate([all_mixed, swk(all_mixed, 1)], axis=0)
         out_term = t_dot(mixed_pair, branch_pair).astype(BF16)
-        out_w_grad = scatter(out_term)
-        ffn = reduce_quad(after(active, fc_term), lambda x: dot(x, w_proj))
-        result = middle + jnp.concatenate(ffn, axis=0) + b_proj
-        hidden_out = result.astype(BF16).reshape(micros, rows, D)
-        keyval_w_grad = scatter(t_dot(normed1, d_keyvals).astype(BF16)).astype(F32)
+        terms = jnp.stack(kv_terms) * behind(kv_scale, out_term)
+        terms = terms.reshape(micros, C, rows, 2 * HD)
+        terms = {d: terms[:, d] for d in range(C)}
+        for bit in [1] + bits_of(C)[1:][::-1]:
+            sent = [d for d in terms if d & bit]
+            got = swk(jnp.stack([terms[d] for d in sent]).astype(BF16), bit)
+            for i, d in enumerate(sent):
+                terms[d ^ bit] = terms[d ^ bit] + got[i].astype(F32)
+                del terms[d]
+        d_keyvals = terms[0].astype(BF16).reshape(tok, 2 * HD)
+        fc_came = swk(behind(fc_grad, d_keyvals), QUAD)
+        dkv_own, dkv_other = halves(d_keyvals)
+        dkv_pair = jnp.concatenate([dkv_own, swk(dkv_other, 1)], axis=0)
+        keyval_term = t_dot(normed1_pair, dkv_pair).astype(BF16)
+        out_w_grad = scatter(jnp.concatenate([out_term, keyval_term], axis=1))
         d_normed1 = (
-            dot_t(d_queries, w_query) + dot_t(behind(d_keyvals, proj_sum), w_keyval)
+            dot_t(d_queries, w_query) + dot_t(d_keyvals, w_keyval)
         )
         d_hidden, gain_one_grad, shift_one_grad = layer_norm_back(hidden, gain_one, d_normed1)
         hidden_grad = (d_middle + d_hidden).reshape(micros, rows, D)
 
-        def sum_z(x):
+        ffn = jnp.concatenate([behind(x, hidden_grad) for x in ffn]).astype(F32)
+        result = middle + ffn_own + ffn + b_proj
+        hidden_out = result.astype(BF16).reshape(micros, rows, D)
+
+        fc_sum = (behind(fc_grad, hidden_grad, query_w_grad).astype(F32) + fc_came.astype(F32)).astype(BF16)
+        for bit in bits_of(C)[3:]:
+            fc_sum = (fc_sum.astype(F32) + swk(fc_sum, bit).astype(F32)).astype(BF16)
+
+        def reduce_z(x):
             part = x.shape[0] // Z
             blocks = x.astype(BF16).reshape(Z, part, x.shape[1])
             terms = [
@@ -590,24 +603,31 @@
                 for i, d in enumerate(sent):
                     terms[d ^ bit] = terms[d ^ bit] + got[i * part : (i + 1) * part].astype(F32)
                     del terms[d]
-            held = terms[0].astype(BF16)
+            return terms[0].astype(BF16)
+
+        def expand_z(held):
+            part, n = held.shape
             ids = [0]
             for bit in bits_of(Z)[::-1]:
                 held = jnp.concatenate([held, swk(held, 2 * bit)])
                 ids = ids + [d ^ bit for d in ids]
-            out = jnp.full(blocks.shape, 0.125, BF16)
+            out = jnp.full((Z, part, n), 0.125, BF16)
             for i, d in enumerate(ids):
                 block = held[i * part : (i + 1) * part]
                 out = lax.dynamic_update_slice(out, block[None], (zi ^ d, 0, 0))
-            own = out.reshape(x.shape)
-            return in_order(own, swk(own, 1)).astype(F32)
+            own = out.reshape(Z * part, n)
+            return own, swk(own, 1)
+
+        query_block = reduce_z(query_w_grad)
+        out_block = reduce_z(out_w_grad)
 
         members = (0, 2, 1, 3)
         proj_out = jnp.full((QUAD * width, D), 1.0, F32)
-        for d, part in zip(members, gather_quad(proj_sum)):
+        for d, part in zip(members, gather_quad(behind(jnp.concatenate(proj_sums), d_keyvals))):
             proj_out = lax.dynamic_update_slice(proj_out, part.astype(F32), ((quad ^ d) * width, 0))
         fc_parts = jnp.full((QUAD, hsh, F * width), 0.75, BF16)
-        for d, part in zip(members, gather_quad(fc_sum)):
+        fc_blocks = gather_quad(behind(fc_sum, query_block, out_block))
+        for d, part in zip(members, fc_blocks):
             fc_parts = lax.dynamic_update_slice(fc_parts, part[None], (quad ^ d, 0, 0))
         fc_out = jnp.concatenate(
             [
@@ -617,11 +637,11 @@
             ],
             axis=1,
         ).astype(F32)
-        out_out = sum_z(out_w_grad)
-        query_out = sum_z(query_w_grad)
-        kv_sum = keyval_w_grad
-        for bit in bits_of(C):
-            kv_sum = kv_sum + swk(kv_sum.astype(BF16), bit).astype(F32)
+        query_out = in_order(*expand_z(query_block)).astype(F32)
+        own, other = expand_z(out_block)
+        half = D // 2
+        out_out = in_order(own[:, :half], other[:, :half]).astype(F32)
+        kv_sum = in_order(own[:, half:], other[:, half:]).astype(F32)
 
         fc_b_full = lax.dynamic_update_slice(
             jnp.zeros((F, QUAD, width), F32), fc_b_grad.reshape(F, 1, width), (0, quad, 0)
@@ -656,7 +676,7 @@
             [
                 gain_one_grad,
                 shift_one_grad,
-                behind(column_sum(d_queries), fc_sum),
+                behind(column_sum(d_queries), fc_blocks[1]),
                 column_sum(d_keyvals[:, HD:]),
                 gain_two_grad,
                 shift_two_grad,

time: 1090 us -> 993 us (0.911)
  waiting for transfers between devices: 397 us -> 298 us
    ppermute x59 -> x55, waiting for transfers between devices: 397 us -> 298 us  [swap_k(): return lax.ppermute(x, 'ctx', [(i, i ^ bit) for i in range(size)])]
    ppermute x59 -> x55, starting transfers between devices: 45.6 us -> 39.1 us  [swap_k(): return lax.ppermute(x, 'ctx', [(i, i ^ bit) for i in range(size)])]
    unnamed x221 -> x229, local copies, waits for them, and re-layouts: 50.3 us -> 47 us
  transfers between devices with their start and end apart: 70 -> 65, of which waited for: 24 -> 25; matrix products, arithmetic and copies ran while one was open for 40% -> 40% of each run, Pallas kernels for 15% -> 17%
where the time goes in v3:
time: 993 us; the launch traced here: 981 us
  waiting for transfers between devices  298 us (30%)
  matrix products  234 us (24%)
  Pallas kernels  167 us (17%)
  local copies, waits for them, and re-layouts  108 us (11%)
  other arithmetic  104 us (10%)
  starting transfers between devices  42.3 us (4%)
  between operations  27 us (3%)
    ppermute x55, waiting for transfers between devices, swap_k(): return lax.ppermute(x, 'ctx', [(i, i ^ bit) for i in range(size)])  298 us
    dot_general x8, matrix products, dot_t(): lax.dot_general(a, b, (((1,), (1,)), ((), ())), preferred_element_type=F32)  87.4 us
    dot_general x10, matrix products, dot(): return jnp.dot(a, b, preferred_element_type=F32)  85.3 us
    pallas_call x1, Pallas kernels, gather_head(): pl.pallas_call(functools.partial(head_kernel, F, C), in_specs=[pl.BlockSp...  78.6 us
    dot_general x5, matrix products, t_dot(): lax.dot_general(a, b, (((0,), (0,)), ((), ())), preferred_element_type=F32)  61.7 us
    pallas_call x2, Pallas kernels, attend_backward(): pl.pallas_call(functools.partial(backward_kernel, scale), grid=(HEADS //...  47.7 us
    unnamed x229, local copies, waits for them, and re-layouts  47 us
    pallas_call x2, Pallas kernels, attend_forward(): pl.pallas_call(functools.partial(forward_kernel, scale), grid=(HEADS // H...  40.6 us
  transfers between devices with their start and end apart: 65, of which 25 were waited for; matrix products, arithmetic and copies ran while one was open for 40% of the time, Pallas kernels for 17%

profile of v3, /device:TPU:1, one launch (start us, length us, event | category | flops | bytes accessed | tf_op | source)
XLA Modules:
  0.0 980.6 jit_solution(985118806062181414)
XLA Ops:
  16.8 78.6 %gather_head.1 = (bf16[4,48,128]{2,1,0:T(8,128)(2,1)}, s32[8,4,256]{2,1,0:T(4,128)}, bf16[2048,256]{1,0:T(8,128)(2,1)}, bf16[2048,2048]{1,0:T(8,128)(2,1)}) custom-call(bf16[48,128]{1,0:T(8,128)(2,1)} %pad_bitcast_fusion.1.vec_ref, s32[4,256]{1,0:T(4,128)} %pad_add_fusion.2.place_ref, bf16[512,256]{1,0:T(8,128)(2,1)} %wkv_ref.1, bf16[512,2048]{1,0:T(8,128)(2,1)} %wq_ref.1), custom_call_target="tpu_custom_call" | custom-call | tf_op jit(solution)/shard_map/gather_head/pallas_call | solution.py:187
  109.2 9.8 %add_convert_fusion.5 = bf16[512,2048]{1,0:T(8,128)(2,1)} fusion(bf16[512,2048]{1,0:T(8,128)(2,1)} %add_convert_fusion.6, bf16[2048,2048]{1,0:T(8,128)(2,1)} %get-tuple-element.33, f32[2048]{0:T(1024)S(1)} %bitcast.316), kind=kOutput, calls=%fused_computation.64 | convolution fusion | flops 4297064448 | bytes 12591104 | tf_op jit(solution)/shard_map/dot_general | solution.py:48
  122.5 4.3 collective-permute-done.5
  139.6 20.5 %attend_forward.2 = (bf16[256,2048]{1,0:T(8,128)(2,1)S(1)}, f32[8,2,256]{2,1,0:T(2,128)S(1)}) custom-call(bf16[256,2048]{1,0:T(8,128)(2,1)S(1)} %slice.553.q_ref, bf16[2048,256]{1,0:T(8,128)(2,1)S(1)} %get-tuple-element.101.kv_ref, s32[2048,2]{1,0:T(8,128)S(1)} %copy.48.kplace_ref, s32[2,256]{1,0:T(2,128)S(1)} %get-tuple-element.140.qplace_ref), custom_call_target="tpu_custom_call" | custom-call | flops 8589934592 | bytes 2097152 | tf_op jit(solution)/shard_map/attend_forward/pallas_call | solution.py:284
  160.1 19.1 %collective-permute-done.14 = bf16[512,2048]{1,0:T(8,128)(2,1)} collective-permute-done((bf16[512,2048]{1,0:T(8,128)(2,1)}, bf16[512,2048]{1,0:T(8,128)(2,1)}, u32[]{:S(2)}, u32[]{:S(2)}) %collective-permute-start.14) | collective-permute-done | bytes 2097184 | tf_op jit(solution)/shard_map/ppermute | solution.py:64
  181.3 3.6 fusion.113
  189.2 20.1 %attend_forward.3 = (bf16[256,2048]{1,0:T(8,128)(2,1)S(1)}, f32[8,2,256]{2,1,0:T(2,128)S(1)}) custom-call(bf16[256,2048]{1,0:T(8,128)(2,1)S(1)} %add_convert_fusion.12.q_ref, bf16[2048,256]{1,0:T(8,128)(2,1)S(1)} %get-tuple-element.100.kv_ref, s32[2048,2]{1,0:T(8,128)S(1)} %copy.49.kplace_ref, s32[2,256]{1,0:T(2,128)S(1)} %get-tuple-element.141.qplace_ref), custom_call_target="tpu_custom_call" | custom-call | flops 8589934592 | bytes 2097152 | tf_op jit(solution)/shard_map/attend_forward/pallas_call | solution.py:284
  209.4 3.8 fusion.115
  223.2 18.3 %collective-permute-done.9 = bf16[256,2048]{1,0:T(8,128)(2,1)S(1)} collective-permute-done((bf16[256,2048]{1,0:T(8,128)(2,1)S(1)}, bf16[256,2048]{1,0:T(8,128)(2,1)S(1)}, u32[]{:S(2)}, u32[]{:S(2)}) %collective-permute-start.9) | collective-permute-done | bytes 1048608 | tf_op jit(solution)/shard_map/ppermute | solution.py:64
  249.0 28.7 %multiply_convert_fusion.1 = (bf16[2048,2048]{1,0:T(8,128)(2,1)S(1)}, f32[2048,2048]{1,0:T(8,128)}) fusion(f32[2048]{0:T(1024)S(1)} %bitcast.314, bf16[2048,2048]{1,0:T(8,128)(2,1)} %constant_dynamic-update-slice_fusion.8, bf16[2048,2048]{1,0:T(8,128)(2,1)} %all-gather.6.cloned.1.call-done), kind=kOutput, calls=%fused_computation.10 | convolution fusion | flops 17221812224 | bytes 41951232 | tf_op jit(solution)/shard_map/dot_general | solution.py:48
  281.0 20.7 %convolution_convert_fusion.1 = bf16[2048,2048]{1,0:T(8,128)(2,1)} fusion(bf16[2048,2048]{1,0:T(8,128)(2,1)S(1)} %get-tuple-element.41, bf16[2048,2048]{1,0:T(8,128)(2,1)S(1)} %copy-done.58), kind=kOutput, calls=%fused_computation.13 | convolution fusion | flops 17184063488 | bytes 25165824 | tf_op jit(solution)/shard_map/dot_general | solution.py:56
  301.7 35.4 %convert_reduce_fusion = (f32[2048]{0:T(1024)}, bf16[2048,2048]{1,0:T(8,128)(2,1)}) fusion(f32[2048,2048]{1,0:T(8,128)} %get-tuple-element.136, f32[2048]{0:T(1024)S(1)} %bitcast.315, bf16[2048,2048]{1,0:T(8,128)(2,1)} %copy-done.57, bf16[2048,2048]{1,0:T(8,128)(2,1)} %all-gather.8.cloned.1.call-done), kind=kOutput, calls=%fused_computation.8 | convolution fusion | flops 17280530432 | bytes 41959424 | tf_op jit(solution)/shard_map/dot_general | solution.py:52
  337.1 13.0 %fusion.30 = bf16[1024,2048]{1,0:T(8,128)(2,1)S(1)} fusion(bf16[2048,2048]{1,0:T(8,128)(2,1)} %all-gather.6.cloned.1.call-done, bf16[2048,2048]{1,0:T(8,128)(2,1)} %get-tuple-element.139), kind=kOutput, calls=%fused_computation.70 | convolution fusion | flops 8592031744 | bytes 16777216 | tf_op jit(solution)/shard_map/dot_general | solution.py:52
  350.2 7.1 collective-permute-done.17
  358.5 11.7 %fusion.12 = bf16[512,2048]{1,0:T(8,128)(2,1)S(1)} fusion(f32[1024,2048]{1,0:T(8,128)S(1)} %convert_element_type.457, bf16[2048,2048]{1,0:T(8,128)(2,1)} %all-gather.6.cloned.1.call-done, bf16[2048,2048]{1,0:T(8,128)(2,1)} %get-tuple-element.139), kind=kOutput, calls=%fused_computation.31 | convolution fusion | flops 4297064448 | bytes 16777216 | tf_op jit(solution)/shard_map/dot_general | solution.py:52
  370.2 24.2 %convolution_convert_fusion = bf16[2048,2048]{1,0:T(8,128)(2,1)} fusion(bf16[2048,2048]{1,0:T(8,128)(2,1)} %constant_dynamic-update-slice_fusion.8, bf16[2048,2048]{1,0:T(8,128)(2,1)} %get-tuple-element.139), kind=kOutput, calls=%fused_computation.12 | convolution fusion | flops 17184063488 | bytes 25165824 | tf_op jit(solution)/shard_map/dot_general | solution.py:56
  394.4 14.0 %fusion.27 = bf16[1024,2048]{1,0:T(8,128)(2,1)} fusion(bf16[2048,2048]{1,0:T(8,128)(2,1)} %all-gather.8.cloned.1.call-done, bf16[2048,2048]{1,0:T(8,128)(2,1)} %copy-done.87), kind=kOutput, calls=%fused_computation.69 | convolution fusion | flops 8592031744 | bytes 16777216 | tf_op jit(solution)/shard_map/dot_general | solution.py:48
  411.9 4.0 collective-permute-done.18
  422.6 10.2 %fusion.11 = bf16[512,2048]{1,0:T(8,128)(2,1)} fusion(f32[1024,2048]{1,0:T(8,128)S(1)} %convert_element_type.461, bf16[2048,2048]{1,0:T(8,128)(2,1)} %all-gather.8.cloned.1.call-done, bf16[2048,2048]{1,0:T(8,128)(2,1)} %copy-done.87), kind=kOutput, calls=%fused_computation.28 | convolution fusion | flops 4297064448 | bytes 16777216 | tf_op jit(solution)/shard_map/dot_general | solution.py:48
  436.0 10.1 %slice_add_fusion.2 = f32[512,2048]{1,0:T(8,128)S(1)} fusion(f32[1024,2048]{1,0:T(8,128)} %copy-done.34, bf16[2048,2048]{1,0:T(8,128)(2,1)} %all-gather.8.cloned.1.call-done, bf16[2048,2048]{1,0:T(8,128)(2,1)} %copy-done.87), kind=kOutput, calls=%fused_computation.29 | convolution fusion | flops 4296015872 | bytes 18874368 | tf_op jit(solution)/shard_map/dot_general | solution.py:48
  449.6 18.4 %collective-permute-done.20 = bf16[128,2048]{1,0:T(8,128)(2,1)S(1)} collective-permute-done((bf16[128,2048]{1,0:T(8,128)(2,1)S(1)}, bf16[128,2048]{1,0:T(8,128)(2,1)S(1)}, u32[]{:S(2)}, u32[]{:S(2)}) %collective-permute-start.20) | collective-permute-done | bytes 524320 | tf_op jit(solution)/shard_map/ppermute | solution.py:64
  476.3 10.8 %multiply_reduce_fusion = (f32[2048]{0:T(1024)S(1)}, f32[512]{0:T(512)S(1)}, f32[512]{0:T(512)S(1)}, f32[2048]{0:T(1024)S(1)}, f32[512,2048]{1,0:T(8,128)S(1)}) fusion(f32[512]{0:T(512)S(1)} %add_rsqrt_fusion, f32[512]{0:T(512)S(1)} %broadcast_multiply_fusion.4, f32[]{:T(128)S(6)} %add.503, f32[256,2048]{1,0:T(8,128)S(1)} %copy-done.26, ...), kind=kOutput, calls=%fused_computation.51 | convolution fusion | flops 4312787968 | bytes 25198596 | tf_op jit(solution)/shard_map/dot_general | solution.py:52
  487.1 5.5 convert_reduce_fusion.2
  495.1 4.9 add_convert_fusion.4
  503.6 23.9 %attend_backward.2 = (bf16[256,2048]{1,0:T(8,128)(2,1)S(1)}, f32[2048,256]{1,0:T(8,128)S(1)}) custom-call(bf16[256,2048]{1,0:T(8,128)(2,1)S(1)} %copy-done.7, bf16[256,2048]{1,0:T(8,128)(2,1)S(1)} %add_convert_fusion.10.do_ref, bf16[256,2048]{1,0:T(8,128)(2,1)S(1)} %copy-done.9, f32[8,2,256]{2,1,0:T(2,128)S(1)} %get-tuple-element.42.lse_ref, ...), custom_call_target="tpu_custom_call" | custom-call | flops 19327352832 | bytes 4194304 | tf_op jit(solution)/shard_map/attend_backward/pallas_call | solution.py:313
  539.6 23.8 %attend_backward.3 = (bf16[256,2048]{1,0:T(8,128)(2,1)S(1)}, f32[2048,256]{1,0:T(8,128)S(1)}) custom-call(bf16[256,2048]{1,0:T(8,128)(2,1)S(1)} %copy-done.3, bf16[256,2048]{1,0:T(8,128)(2,1)S(1)} %add_convert_fusion.9.do_ref, bf16[256,2048]{1,0:T(8,128)(2,1)S(1)} %copy-done.12, f32[8,2,256]{2,1,0:T(2,128)S(1)} %get-tuple-element.44.lse_ref, ...), custom_call_target="tpu_custom_call" | custom-call | flops 19327352832 | bytes 4194304 | tf_op jit(solution)/shard_map/attend_backward/pallas_call | solution.py:313
  571.8 8.5 convolution_convert_fusion.2
  588.8 4.8 fusion.24
  598.6 25.3 %collective-permute-done.31 = bf16[2,2,256,256]{3,2,1,0:T(8,128)(2,1)S(1)} collective-permute-done((bf16[2,2,256,256]{3,2,1,0:T(8,128)(2,1)S(1)}, bf16[2,2,256,256]{3,2,1,0:T(8,128)(2,1)S(1)}, u32[]{:S(2)}, u32[]{:S(2)}) %collective-permute-start.31) | collective-permute-done | bytes 524320 | tf_op jit(solution)/shard_map/ppermute | solution.py:64
  624.2 7.2 collective-permute-done.32
  650.1 7.2 fusion.116
  658.5 8.3 broadcast.148
  687.8 51.2 %collective-permute-done.33 = bf16[256,2048]{1,0:T(8,128)(2,1)} collective-permute-done((bf16[256,2048]{1,0:T(8,128)(2,1)}, bf16[256,2048]{1,0:T(8,128)(2,1)}, u32[]{:S(2)}, u32[]{:S(2)}) %collective-permute-start.33) | collective-permute-done | bytes 1048608 | tf_op jit(solution)/shard_map/ppermute | solution.py:64
  742.6 4.8 add_convert_fusion.3
  747.4 36.5 %collective-permute-done.55 = bf16[512,2048]{1,0:T(8,128)(2,1)} collective-permute-done((bf16[512,2048]{1,0:T(8,128)(2,1)}, bf16[512,2048]{1,0:T(8,128)(2,1)}, u32[]{:S(2)}, u32[]{:S(2)}) %collective-permute-start.55) | collective-permute-done | bytes 2097184 | tf_op jit(solution)/shard_map/ppermute | solution.py:64
  785.9 9.1 collective-permute-done.35
  801.0 4.2 convert_dynamic-update-slice_fusion.2
  807.0 5.3 collective-permute-done.36
  814.8 4.9 collective-permute-done.38
  821.4 13.3 %collective-permute-done.47 = bf16[128,1024]{1,0:T(8,128)(2,1)S(1)} collective-permute-done((bf16[128,1024]{1,0:T(8,128)(2,1)S(1)}, bf16[128,1024]{1,0:T(8,128)(2,1)S(1)}, u32[]{:S(2)}, u32[]{:S(2)}) %collective-permute-start.47) | collective-permute-done | bytes 262176 | tf_op jit(solution)/shard_map/ppermute | solution.py:64
  834.9 6.2 collective-permute-done.39
  842.4 16.6 %collective-permute-done.48 = bf16[256,1024]{1,0:T(8,128)(2,1)S(1)} collective-permute-done((bf16[256,1024]{1,0:T(8,128)(2,1)S(1)}, bf16[256,1024]{1,0:T(8,128)(2,1)S(1)}, u32[]{:S(2)}, u32[]{:S(2)}) %collective-permute-start.48) | collective-permute-done | bytes 524320 | tf_op jit(solution)/shard_map/ppermute | solution.py:64
  862.5 3.9 bitcast_dynamic-update-slice_fusion.3
  867.9 7.9 collective-permute-done.51
  877.2 4.1 convert_dynamic-update-slice_fusion.1
  887.0 33.8 %collective-permute-done.40 = bf16[512,2048]{1,0:T(8,128)(2,1)S(1)} collective-permute-done((bf16[512,2048]{1,0:T(8,128)(2,1)}, bf16[512,2048]{1,0:T(8,128)(2,1)S(1)}, u32[]{:S(2)}, u32[]{:S(2)}) %collective-permute-start.40) | collective-permute-done | bytes 2097184 | tf_op jit(solution)/shard_map/ppermute | solution.py:64
  943.6 4.0 slice_bitcast_fusion
  961.8 11.7 %convert_element_type.563 = f32[512,8192]{1,0:T(8,128)} convert(bf16[512,8192]{1,0:T(8,128)(2,1)} %slice_dynamic-update-slice_fusion) | non-fusion elementwise | flops 4194304 | bytes 25165824 | tf_op jit(solution)/shard_map/convert_element_type | solution.py:639
  (515 shorter events, 230.1 us)
Async XLA Ops:
  7.2 101.1 %all-gather.4.cloned.1.call-start = ((), (), s32[]{:S(2)}) async-start(), calls=%async_computation.4 | async-start | bytes 5242880 | tf_op jit(solution)/shard_map/all_gather | solution.py:443
  9.9 239.1 %all-gather.6.cloned.1.call-start = ((), (), s32[]{:S(2)}) async-start(), calls=%async_computation.5 | async-start | bytes 10485760 | tf_op jit(solution)/shard_map/all_gather | solution.py:454
  13.5 288.2 %all-gather.8.cloned.1.call-start = ((), (), s32[]{:S(2)}) async-start(), calls=%async_computation.6 | async-start | bytes 10485760 | tf_op jit(solution)/shard_map/all_gather | solution.py:455
  102.9 18.2 %collective-permute-start = (bf16[2,256,256]{2,1,0:T(8,128)(2,1)S(1)}, bf16[2,256,256]{2,1,0:T(8,128)(2,1)S(1)}, u32[]{:S(2)}, u32[]{:S(2)}) collective-permute-start(bf16[2,256,256]{2,1,0:T(8,128)(2,1)S(1)} %bitcast.281), channel_id=1, source_target_pairs={{0,1},{1,0},{2,3},{3,2},{4,5},{5,4},{6,7},{7,6},{8,9},{9,8},{10,11... | collective-permute-start | bytes 786440 | tf_op jit(solution)/shard_map/ppermute | solution.py:64
  103.0 16.1 %collective-permute-start.1 = (bf16[2,256,256]{2,1,0:T(8,128)(2,1)S(1)}, bf16[2,256,256]{2,1,0:T(8,128)(2,1)S(1)}, u32[]{:S(2)}, u32[]{:S(2)}) collective-permute-start(bf16[2,256,256]{2,1,0:T(8,128)(2,1)S(1)} %bitcast.282), channel_id=1, source_target_pairs={{0,2},{1,3},{2,0},{3,1},{4,6},{5,7},{6,4},{7,5},{8,10},{9,11},{10,... | collective-permute-start | bytes 786440 | tf_op jit(solution)/shard_map/ppermute | solution.py:64
  104.3 14.9 %collective-permute-start.3 = (bf16[2,256,256]{2,1,0:T(8,128)(2,1)S(1)}, bf16[2,256,256]{2,1,0:T(8,128)(2,1)S(1)}, u32[]{:S(2)}, u32[]{:S(2)}) collective-permute-start(bf16[2,256,256]{2,1,0:T(8,128)(2,1)S(1)} %bitcast.283), channel_id=1, source_target_pairs={{0,4},{1,5},{2,6},{3,7},{4,0},{5,1},{6,2},{7,3},{8,12},{9,13},{10,... | collective-permute-start | bytes 786440 | tf_op jit(solution)/shard_map/ppermute | solution.py:64
  108.2 324.5 %reduce-scatter.5.cloned.1.call-start = ((), (), s32[]{:S(2)}) async-start(), calls=%async_computation.7 | async-start | bytes 10485760 | tf_op jit(solution)/shard_map/reduce_scatter | solution.py:504
  108.3 73.0 %collective-permute-start.7 = (bf16[2048,1024]{1,0:T(8,128)(2,1)}, bf16[2048,1024]{1,0:T(8,128)(2,1)}, u32[]{:S(2)}, u32[]{:S(2)}) collective-permute-start(bf16[2048,1024]{1,0:T(8,128)(2,1)} %all-gather.4.cloned.1.call-done), channel_id=1, source_target_pairs={{0,1},{1,0},{2,3},{3,2},{4,5},{5,4},{6,7},{7,6},{8,9},{9,8},{10,11... | collective-permute-start | bytes 12582920 | tf_op jit(solution)/shard_map/ppermute | solution.py:64
  119.1 8.9 collective-permute-start.2
  120.4 9.0 collective-permute-start.4
  131.6 47.6 %collective-permute-start.14 = (bf16[512,2048]{1,0:T(8,128)(2,1)}, bf16[512,2048]{1,0:T(8,128)(2,1)}, u32[]{:S(2)}, u32[]{:S(2)}) collective-permute-start(bf16[512,2048]{1,0:T(8,128)(2,1)} %bitcast.13), channel_id=1, source_target_pairs={{0,2},{1,3},{2,0},{3,1},{4,6},{5,7},{6,4},{7,5},{8,10},{9,11},{10,... | collective-permute-start | bytes 6291464 | tf_op jit(solution)/shard_map/ppermute | solution.py:64
  136.8 85.3 %collective-permute-start.15 = (bf16[512,2048]{1,0:T(8,128)(2,1)}, bf16[512,2048]{1,0:T(8,128)(2,1)S(1)}, u32[]{:S(2)}, u32[]{:S(2)}) collective-permute-start(bf16[512,2048]{1,0:T(8,128)(2,1)} %bitcast.13), channel_id=1, source_target_pairs={{0,1},{1,0},{2,3},{3,2},{4,5},{5,4},{6,7},{7,6},{8,9},{9,8},{10,11... | collective-permute-start | bytes 6291464 | tf_op jit(solution)/shard_map/ppermute | solution.py:64
  179.2 43.8 %collective-permute-start.16 = (bf16[512,2048]{1,0:T(8,128)(2,1)}, bf16[512,2048]{1,0:T(8,128)(2,1)S(1)}, u32[]{:S(2)}, u32[]{:S(2)}) collective-permute-start(bf16[512,2048]{1,0:T(8,128)(2,1)} %collective-permute-done.14), channel_id=1, source_target_pairs={{0,1},{1,0},{2,3},{3,2},{4,5},{5,4},{6,7},{7,6},{8,9},{9,8},{10,11... | collective-permute-start | bytes 6291464 | tf_op jit(solution)/shard_map/ppermute | solution.py:64
  187.9 34.6 %collective-permute-start.8 = (bf16[256,2048]{1,0:T(8,128)(2,1)S(1)}, bf16[256,2048]{1,0:T(8,128)(2,1)S(1)}, u32[]{:S(2)}, u32[]{:S(2)}) collective-permute-start(bf16[256,2048]{1,0:T(8,128)(2,1)S(1)} %get-tuple-element.73), channel_id=1, source_target_pairs={{0,2},{1,3},{2,0},{3,1},{4,6},{5,7},{6,4},{7,5},{8,10},{9,11},{10,... | collective-permute-start | bytes 3145736 | tf_op jit(solution)/shard_map/ppermute | solution.py:64
  216.9 24.6 %collective-permute-start.9 = (bf16[256,2048]{1,0:T(8,128)(2,1)S(1)}, bf16[256,2048]{1,0:T(8,128)(2,1)S(1)}, u32[]{:S(2)}, u32[]{:S(2)}) collective-permute-start(bf16[256,2048]{1,0:T(8,128)(2,1)S(1)} %get-tuple-element.69), channel_id=1, source_target_pairs={{0,2},{1,3},{2,0},{3,1},{4,6},{5,7},{6,4},{7,5},{8,10},{9,11},{10,... | collective-permute-start | bytes 3145736 | tf_op jit(solution)/shard_map/ppermute | solution.py:64
  221.5 23.2 %collective-permute-start.10 = (bf16[256,2048]{1,0:T(8,128)(2,1)S(1)}, bf16[256,2048]{1,0:T(8,128)(2,1)S(1)}, u32[]{:S(2)}, u32[]{:S(2)}) collective-permute-start(bf16[256,2048]{1,0:T(8,128)(2,1)S(1)} %get-tuple-element.73), channel_id=1, source_target_pairs={{0,1},{1,0},{2,3},{3,2},{4,5},{5,4},{6,7},{7,6},{8,9},{9,8},{10,11... | collective-permute-start | bytes 3145736 | tf_op jit(solution)/shard_map/ppermute | solution.py:64
  222.1 23.6 %collective-permute-start.11 = (bf16[256,2048]{1,0:T(8,128)(2,1)S(1)}, bf16[256,2048]{1,0:T(8,128)(2,1)S(1)}, u32[]{:S(2)}, u32[]{:S(2)}) collective-permute-start(bf16[256,2048]{1,0:T(8,128)(2,1)S(1)} %get-tuple-element.69), channel_id=1, source_target_pairs={{0,1},{1,0},{2,3},{3,2},{4,5},{5,4},{6,7},{7,6},{8,9},{9,8},{10,11... | collective-permute-start | bytes 3145736 | tf_op jit(solution)/shard_map/ppermute | solution.py:64
  222.5 24.4 %collective-permute-start.12 = (bf16[256,2048]{1,0:T(8,128)(2,1)S(1)}, bf16[256,2048]{1,0:T(8,128)(2,1)S(1)}, u32[]{:S(2)}, u32[]{:S(2)}) collective-permute-start(bf16[256,2048]{1,0:T(8,128)(2,1)S(1)} %collective-permute-done.8), channel_id=1, source_target_pairs={{0,1},{1,0},{2,3},{3,2},{4,5},{5,4},{6,7},{7,6},{8,9},{9,8},{10,11... | collective-permute-start | bytes 3145736 | tf_op jit(solution)/shard_map/ppermute | solution.py:64
  301.7 374.8 %reduce-scatter.7.cloned.1.call-start = ((), (), s32[]{:S(2)}) async-start(), calls=%async_computation.8 | async-start | bytes 10485760 | tf_op jit(solution)/shard_map/reduce_scatter | solution.py:504
  408.4 161.1 %collective-permute-start.26 = (bf16[512,2048]{1,0:T(8,128)(2,1)}, bf16[512,2048]{1,0:T(8,128)(2,1)}, u32[]{:S(2)}, u32[]{:S(2)}) collective-permute-start(bf16[512,2048]{1,0:T(8,128)(2,1)} %add_convert_fusion.6), channel_id=1, source_target_pairs={{0,1},{1,0},{2,3},{3,2},{4,5},{5,4},{6,7},{7,6},{8,9},{9,8},{10,11... | collective-permute-start | bytes 6291464 | tf_op jit(solution)/shard_map/ppermute | solution.py:64
  410.3 65.9 %collective-permute-start.21 = (bf16[256,2048]{1,0:T(8,128)(2,1)}, bf16[256,2048]{1,0:T(8,128)(2,1)}, u32[]{:S(2)}, u32[]{:S(2)}) collective-permute-start(bf16[256,2048]{1,0:T(8,128)(2,1)} %get-tuple-element.98), channel_id=1, source_target_pairs={{0,2},{1,3},{2,0},{3,1},{4,6},{5,7},{6,4},{7,5},{8,10},{9,11},{10,... | collective-permute-start | bytes 3145736 | tf_op jit(solution)/shard_map/ppermute | solution.py:64
  411.5 64.8 %collective-permute-start.22 = (bf16[256,2048]{1,0:T(8,128)(2,1)}, bf16[256,2048]{1,0:T(8,128)(2,1)}, u32[]{:S(2)}, u32[]{:S(2)}) collective-permute-start(bf16[256,2048]{1,0:T(8,128)(2,1)} %get-tuple-element.99), channel_id=1, source_target_pairs={{0,2},{1,3},{2,0},{3,1},{4,6},{5,7},{6,4},{7,5},{8,10},{9,11},{10,... | collective-permute-start | bytes 3145736 | tf_op jit(solution)/shard_map/ppermute | solution.py:64
  411.9 329.5 %reduce-scatter.9.cloned.1.call-start = ((), (), s32[]{:S(2)}) async-start(), calls=%async_computation.9 | async-start | bytes 5242880 | tf_op jit(solution)/shard_map/reduce_scatter | solution.py:500
  433.8 34.1 %collective-permute-start.20 = (bf16[128,2048]{1,0:T(8,128)(2,1)S(1)}, bf16[128,2048]{1,0:T(8,128)(2,1)S(1)}, u32[]{:S(2)}, u32[]{:S(2)}) collective-permute-start(bf16[128,2048]{1,0:T(8,128)(2,1)S(1)} %slice.570), channel_id=1, source_target_pairs={{0,4},{1,5},{2,6},{3,7},{4,0},{5,1},{6,2},{7,3},{8,12},{9,13},{10,... | collective-permute-start | bytes 1572872 | tf_op jit(solution)/shard_map/ppermute | solution.py:64
  470.2 29.8 %collective-permute-start.23 = (bf16[128,2048]{1,0:T(8,128)(2,1)}, bf16[128,2048]{1,0:T(8,128)(2,1)}, u32[]{:S(2)}, u32[]{:S(2)}) collective-permute-start(bf16[128,2048]{1,0:T(8,128)(2,1)} %add_convert_fusion.19), channel_id=1, source_target_pairs={{0,4},{1,5},{2,6},{3,7},{4,0},{5,1},{6,2},{7,3},{8,12},{9,13},{10,... | collective-permute-start | bytes 1572872 | tf_op jit(solution)/shard_map/ppermute | solution.py:64
  503.2 26.6 %collective-permute-start.24 = (bf16[128,2048]{1,0:T(8,128)(2,1)S(1)}, bf16[128,2048]{1,0:T(8,128)(2,1)S(1)}, u32[]{:S(2)}, u32[]{:S(2)}) collective-permute-start(bf16[128,2048]{1,0:T(8,128)(2,1)S(1)} %add_convert_fusion.17), channel_id=1, source_target_pairs={{0,4},{1,5},{2,6},{3,7},{4,0},{5,1},{6,2},{7,3},{8,12},{9,13},{10,... | collective-permute-start | bytes 1572872 | tf_op jit(solution)/shard_map/ppermute | solution.py:64
  532.1 31.4 %collective-permute-start.27 = (bf16[128,2048]{1,0:T(8,128)(2,1)}, bf16[128,2048]{1,0:T(8,128)(2,1)}, u32[]{:S(2)}, u32[]{:S(2)}) collective-permute-start(bf16[128,2048]{1,0:T(8,128)(2,1)} %add_convert_fusion.15), channel_id=1, source_target_pairs={{0,4},{1,5},{2,6},{3,7},{4,0},{5,1},{6,2},{7,3},{8,12},{9,13},{10,... | collective-permute-start | bytes 1572872 | tf_op jit(solution)/shard_map/ppermute | solution.py:64
  580.3 217.3 %reduce-scatter.11.cloned.1.call-start = ((), (), s32[]{:S(2)}) async-start(), calls=%async_computation.10 | async-start | bytes 5898240 | tf_op jit(solution)/shard_map/reduce_scatter | solution.py:500
  598.0 25.9 %collective-permute-start.31 = (bf16[2,2,256,256]{3,2,1,0:T(8,128)(2,1)S(1)}, bf16[2,2,256,256]{3,2,1,0:T(8,128)(2,1)S(1)}, u32[]{:S(2)}, u32[]{:S(2)}) collective-permute-start(bf16[2,2,256,256]{3,2,1,0:T(8,128)(2,1)S(1)} %pad_maximum_fusion.12), channel_id=1, source_target_pairs={{0,4},{1,5},{2,6},{3,7},{4,0},{5,1},{6,2},{7,3},{8,12},{9,13},{10,... | collective-permute-start | bytes 1572872 | tf_op jit(solution)/shard_map/ppermute | solution.py:64
  646.9 38.5 %collective-permute-start.19 = (bf16[256,2048]{1,0:T(8,128)(2,1)}, bf16[256,2048]{1,0:T(8,128)(2,1)S(1)}, u32[]{:S(2)}, u32[]{:S(2)}) collective-permute-start(bf16[256,2048]{1,0:T(8,128)(2,1)} %get-tuple-element.88), channel_id=1, source_target_pairs={{0,2},{1,3},{2,0},{3,1},{4,6},{5,7},{6,4},{7,5},{8,10},{9,11},{10,... | collective-permute-start | bytes 3145736 | tf_op jit(solution)/shard_map/ppermute | solution.py:64
  646.9 92.1 %collective-permute-start.33 = (bf16[256,2048]{1,0:T(8,128)(2,1)}, bf16[256,2048]{1,0:T(8,128)(2,1)}, u32[]{:S(2)}, u32[]{:S(2)}) collective-permute-start(bf16[256,2048]{1,0:T(8,128)(2,1)} %get-tuple-element.89), channel_id=1, source_target_pairs={{0,2},{1,3},{2,0},{3,1},{4,6},{5,7},{6,4},{7,5},{8,10},{9,11},{10,... | collective-permute-start | bytes 3145736 | tf_op jit(solution)/shard_map/ppermute | solution.py:64
  670.3 113.6 %collective-permute-start.55 = (bf16[512,2048]{1,0:T(8,128)(2,1)}, bf16[512,2048]{1,0:T(8,128)(2,1)}, u32[]{:S(2)}, u32[]{:S(2)}) collective-permute-start(bf16[512,2048]{1,0:T(8,128)(2,1)} %get-tuple-element.57), channel_id=1, source_target_pairs={{0,2},{1,3},{2,0},{3,1},{4,6},{5,7},{6,4},{7,5},{8,10},{9,11},{10,... | collective-permute-start | bytes 6291464 | tf_op jit(solution)/shard_map/ppermute | solution.py:64
  670.3 206.9 %collective-permute-start.56 = (bf16[512,2048]{1,0:T(8,128)(2,1)}, bf16[512,2048]{1,0:T(8,128)(2,1)}, u32[]{:S(2)}, u32[]{:S(2)}) collective-permute-start(bf16[512,2048]{1,0:T(8,128)(2,1)} %get-tuple-element.57), channel_id=1, source_target_pairs={{0,1},{1,0},{2,3},{3,2},{4,5},{5,4},{6,7},{7,6},{8,9},{9,8},{10,11... | collective-permute-start | bytes 6291464 | tf_op jit(solution)/shard_map/ppermute | solution.py:64
  681.9 179.0 %collective-permute-start.34 = (bf16[512,2048]{1,0:T(8,128)(2,1)}, bf16[512,2048]{1,0:T(8,128)(2,1)}, u32[]{:S(2)}, u32[]{:S(2)}) collective-permute-start(bf16[512,2048]{1,0:T(8,128)(2,1)} %fusion.9), channel_id=1, source_target_pairs={{0,4},{1,5},{2,6},{3,7},{4,0},{5,1},{6,2},{7,3},{8,12},{9,13},{10,... | collective-permute-start | bytes 6291464 | tf_op jit(solution)/shard_map/ppermute | solution.py:64
  742.5 52.5 %collective-permute-start.35 = (bf16[256,1024]{1,0:T(8,128)(2,1)S(1)}, bf16[256,1024]{1,0:T(8,128)(2,1)S(1)}, u32[]{:S(2)}, u32[]{:S(2)}) collective-permute-start(bf16[256,1024]{1,0:T(8,128)(2,1)S(1)} %pad_maximum_fusion.13), channel_id=1, source_target_pairs={{0,2},{1,3},{2,0},{3,1},{4,6},{5,7},{6,4},{7,5},{8,10},{9,11},{10,... | collective-permute-start | bytes 1572872 | tf_op jit(solution)/shard_map/ppermute | solution.py:64
  783.9 97.4 %collective-permute-start.57 = (bf16[512,2048]{1,0:T(8,128)(2,1)}, bf16[512,2048]{1,0:T(8,128)(2,1)S(1)}, u32[]{:S(2)}, u32[]{:S(2)}) collective-permute-start(bf16[512,2048]{1,0:T(8,128)(2,1)} %collective-permute-done.55), channel_id=1, source_target_pairs={{0,1},{1,0},{2,3},{3,2},{4,5},{5,4},{6,7},{7,6},{8,9},{9,8},{10,11... | collective-permute-start | bytes 6291464 | tf_op jit(solution)/shard_map/ppermute | solution.py:64
  797.6 14.7 %collective-permute-start.36 = (bf16[128,1024]{1,0:T(8,128)(2,1)}, bf16[128,1024]{1,0:T(8,128)(2,1)S(1)}, u32[]{:S(2)}, u32[]{:S(2)}) collective-permute-start(bf16[128,1024]{1,0:T(8,128)(2,1)} %fusion.81), channel_id=1, source_target_pairs={{0,4},{1,5},{2,6},{3,7},{4,0},{5,1},{6,2},{7,3},{8,12},{9,13},{10,... | collective-permute-start | bytes 786440 | tf_op jit(solution)/shard_map/ppermute | solution.py:64
  799.5 20.1 %collective-permute-start.38 = (bf16[256,1152]{1,0:T(8,128)(2,1)}, bf16[256,1152]{1,0:T(8,128)(2,1)}, u32[]{:S(2)}, u32[]{:S(2)}) collective-permute-start(bf16[256,1152]{1,0:T(8,128)(2,1)} %pad_maximum_fusion.10), channel_id=1, source_target_pairs={{0,2},{1,3},{2,0},{3,1},{4,6},{5,7},{6,4},{7,5},{8,10},{9,11},{10,... | collective-permute-start | bytes 1769480 | tf_op jit(solution)/shard_map/ppermute | solution.py:64
  814.1 20.6 %collective-permute-start.47 = (bf16[128,1024]{1,0:T(8,128)(2,1)S(1)}, bf16[128,1024]{1,0:T(8,128)(2,1)S(1)}, u32[]{:S(2)}, u32[]{:S(2)}) collective-permute-start(bf16[128,1024]{1,0:T(8,128)(2,1)S(1)} %get-tuple-element.63), channel_id=1, source_target_pairs={{0,4},{1,5},{2,6},{3,7},{4,0},{5,1},{6,2},{7,3},{8,12},{9,13},{10,... | collective-permute-start | bytes 786440 | tf_op jit(solution)/shard_map/ppermute | solution.py:64
  820.7 20.4 %collective-permute-start.39 = (bf16[128,1152]{1,0:T(8,128)(2,1)S(1)}, bf16[128,1152]{1,0:T(8,128)(2,1)S(1)}, u32[]{:S(2)}, u32[]{:S(2)}) collective-permute-start(bf16[128,1152]{1,0:T(8,128)(2,1)S(1)} %fusion.71), channel_id=1, source_target_pairs={{0,4},{1,5},{2,6},{3,7},{4,0},{5,1},{6,2},{7,3},{8,12},{9,13},{10,... | collective-permute-start | bytes 884744 | tf_op jit(solution)/shard_map/ppermute | solution.py:64
  834.8 24.2 %collective-permute-start.48 = (bf16[256,1024]{1,0:T(8,128)(2,1)S(1)}, bf16[256,1024]{1,0:T(8,128)(2,1)S(1)}, u32[]{:S(2)}, u32[]{:S(2)}) collective-permute-start(bf16[256,1024]{1,0:T(8,128)(2,1)S(1)} %pad_maximum_fusion.14), channel_id=1, source_target_pairs={{0,2},{1,3},{2,0},{3,1},{4,6},{5,7},{6,4},{7,5},{8,10},{9,11},{10,... | collective-permute-start | bytes 1572872 | tf_op jit(solution)/shard_map/ppermute | solution.py:64
  842.3 18.5 %collective-permute-start.50 = (bf16[128,1152]{1,0:T(8,128)(2,1)S(1)}, bf16[128,1152]{1,0:T(8,128)(2,1)S(1)}, u32[]{:S(2)}, u32[]{:S(2)}) collective-permute-start(bf16[128,1152]{1,0:T(8,128)(2,1)S(1)} %get-tuple-element.61), channel_id=1, source_target_pairs={{0,4},{1,5},{2,6},{3,7},{4,0},{5,1},{6,2},{7,3},{8,12},{9,13},{10,... | collective-permute-start | bytes 884744 | tf_op jit(solution)/shard_map/ppermute | solution.py:64
  859.1 24.9 %collective-permute-start.49 = (bf16[512,1024]{1,0:T(8,128)(2,1)S(1)}, bf16[512,1024]{1,0:T(8,128)(2,1)S(1)}, u32[]{:S(2)}, u32[]{:S(2)}) collective-permute-start(bf16[512,1024]{1,0:T(8,128)(2,1)S(1)} %bitcast.265), channel_id=1, source_target_pairs={{0,1},{1,0},{2,3},{3,2},{4,5},{5,4},{6,7},{7,6},{8,9},{9,8},{10,11... | collective-permute-start | bytes 3145736 | tf_op jit(solution)/shard_map/ppermute | solution.py:64
  860.9 15.0 %collective-permute-start.51 = (bf16[256,1152]{1,0:T(8,128)(2,1)S(1)}, bf16[256,1152]{1,0:T(8,128)(2,1)S(1)}, u32[]{:S(2)}, u32[]{:S(2)}) collective-permute-start(bf16[256,1152]{1,0:T(8,128)(2,1)S(1)} %pad_maximum_fusion.11), channel_id=1, source_target_pairs={{0,2},{1,3},{2,0},{3,1},{4,6},{5,7},{6,4},{7,5},{8,10},{9,11},{10,... | collective-permute-start | bytes 1769480 | tf_op jit(solution)/shard_map/ppermute | solution.py:64
  866.5 54.4 %collective-permute-start.40 = (bf16[512,2048]{1,0:T(8,128)(2,1)}, bf16[512,2048]{1,0:T(8,128)(2,1)S(1)}, u32[]{:S(2)}, u32[]{:S(2)}) collective-permute-start(bf16[512,2048]{1,0:T(8,128)(2,1)} %get-tuple-element.59), channel_id=1, source_target_pairs={{0,2},{1,3},{2,0},{3,1},{4,6},{5,7},{6,4},{7,5},{8,10},{9,11},{10,... | collective-permute-start | bytes 6291464 | tf_op jit(solution)/shard_map/ppermute | solution.py:64
  875.9 10.9 %collective-permute-start.52 = (bf16[512,1152]{1,0:T(8,128)(2,1)S(1)}, bf16[512,1152]{1,0:T(8,128)(2,1)S(1)}, u32[]{:S(2)}, u32[]{:S(2)}) collective-permute-start(bf16[512,1152]{1,0:T(8,128)(2,1)S(1)} %bitcast.262), channel_id=1, source_target_pairs={{0,1},{1,0},{2,3},{3,2},{4,5},{5,4},{6,7},{7,6},{8,9},{9,8},{10,11... | collective-permute-start | bytes 3538952 | tf_op jit(solution)/shard_map/ppermute | solution.py:64
  881.3 55.0 %collective-permute-start.53 = (bf16[512,2048]{1,0:T(8,128)(2,1)}, bf16[512,2048]{1,0:T(8,128)(2,1)}, u32[]{:S(2)}, u32[]{:S(2)}) collective-permute-start(bf16[512,2048]{1,0:T(8,128)(2,1)} %get-tuple-element.59), channel_id=1, source_target_pairs={{0,1},{1,0},{2,3},{3,2},{4,5},{5,4},{6,7},{7,6},{8,9},{9,8},{10,11... | collective-permute-start | bytes 6291464 | tf_op jit(solution)/shard_map/ppermute | solution.py:64
  927.0 15.0 %collective-permute-start.54 = (bf16[512,2048]{1,0:T(8,128)(2,1)}, bf16[512,2048]{1,0:T(8,128)(2,1)S(1)}, u32[]{:S(2)}, u32[]{:S(2)}) collective-permute-start(bf16[512,2048]{1,0:T(8,128)(2,1)} %copy-done.53), channel_id=1, source_target_pairs={{0,1},{1,0},{2,3},{3,2},{4,5},{5,4},{6,7},{7,6},{8,9},{9,8},{10,11... | collective-permute-start | bytes 6291464 | tf_op jit(solution)/shard_map/ppermute | solution.py:64
  (105 other events, 1183.5 us)
Sparse Core Ops, SparseCore 0:
  10.4 84.6 all-gather.3
  97.0 86.5 all-gather.5
  186.0 87.6 all-gather.7
  301.8 85.7 reduce-scatter.4
  412.0 86.7 reduce-scatter.6
  580.4 52.4 reduce-scatter.8
  640.4 55.2 reduce-scatter.10

commit v4 on v3

--- a/solution.py
+++ b/solution.py
@@ -530,13 +530,13 @@
             return outs
 
         proj_sums = across_quads(proj_grad, 4)
-        ffn, ffn_passed, ffn_own = reduce_quad(after(active, fc_term), lambda x: dot(x, w_proj))
+        ffn, ffn_passed, ffn_own = reduce_quad(after(active, fc_term, came[0]), lambda x: dot(x, w_proj))
 
         d_middle, gain_two_grad, shift_two_grad = layer_norm_back(
-            behind(middle, proj_sums[0], ffn_passed, ffn_own), gain_two, d_normed2
+            behind(middle, ffn_passed, ffn_own), gain_two, d_normed2
         )
         d_middle = cot_own.astype(F32) + d_middle
-        d_branch = d_middle.astype(BF16)
+        d_branch = behind(d_middle, proj_sums[0]).astype(BF16)
         branch_own, branch_other = halves(d_branch)
         d_mixed = (dot_t(branch_own, wo_own) + dot_t(branch_other, wo_other)).astype(BF16)
         d_mixed = [d_mixed[m * rows : (m + 1) * rows] for m in range(micros)]
@@ -626,7 +626,7 @@
         for d, part in zip(members, gather_quad(behind(jnp.concatenate(proj_sums), d_keyvals))):
             proj_out = lax.dynamic_update_slice(proj_out, part.astype(F32), ((quad ^ d) * width, 0))
         fc_parts = jnp.full((QUAD, hsh, F * width), 0.75, BF16)
-        fc_blocks = gather_quad(behind(fc_sum, query_block, out_block))
+        fc_blocks = gather_quad(behind(fc_sum, query_block))
         for d, part in zip(members, fc_blocks):
             fc_parts = lax.dynamic_update_slice(fc_parts, part[None], (quad ^ d, 0, 0))
         fc_out = jnp.concatenate(

time: 993 us -> 987 us (level)
    unnamed x229 -> x243, local copies, waits for them, and re-layouts: 47 us -> 44.1 us
  transfers between devices with their start and end apart: 65 -> 65, of which waited for: 25 -> 20; matrix products, arithmetic and copies ran while one was open for 40% -> 44% of each run, Pallas kernels for 17% -> 17%
where the time goes in v4:
time: 987 us; the launch traced here: 977 us
  waiting for transfers between devices  291 us (29%)
  matrix products  235 us (24%)
  Pallas kernels  167 us (17%)
  other arithmetic  105 us (11%)
  local copies, waits for them, and re-layouts  105 us (11%)
  starting transfers between devices  47.4 us (5%)
  between operations  26.7 us (3%)
    ppermute x55, waiting for transfers between devices, swap_k(): return lax.ppermute(x, 'ctx', [(i, i ^ bit) for i in range(size)])  291 us
    dot_general x8, matrix products, dot_t(): lax.dot_general(a, b, (((1,), (1,)), ((), ())), preferred_element_type=F32)  90.1 us
    dot_general x10, matrix products, dot(): return jnp.dot(a, b, preferred_element_type=F32)  81.2 us
    pallas_call x1, Pallas kernels, gather_head(): pl.pallas_call(functools.partial(head_kernel, F, C), in_specs=[pl.BlockSp...  78.6 us
    dot_general x5, matrix products, t_dot(): lax.dot_general(a, b, (((0,), (0,)), ((), ())), preferred_element_type=F32)  63.9 us
    pallas_call x2, Pallas kernels, attend_backward(): pl.pallas_call(functools.partial(backward_kernel, scale), grid=(HEADS //...  47.9 us
    unnamed x243, local copies, waits for them, and re-layouts  44.1 us
    ppermute x55, starting transfers between devices, swap_k(): return lax.ppermute(x, 'ctx', [(i, i ^ bit) for i in range(size)])  43.2 us
  transfers between devices with their start and end apart: 65, of which 20 were waited for; matrix products, arithmetic and copies ran while one was open for 44% of the time, Pallas kernels for 17%

profile of v4, /device:TPU:1, one launch (start us, length us, event | category | flops | bytes accessed | tf_op | source)
XLA Modules:
  0.0 976.7 jit_solution(8595174844988258886)
XLA Ops:
  16.8 78.6 %gather_head.1 = (bf16[4,48,128]{2,1,0:T(8,128)(2,1)}, s32[8,4,256]{2,1,0:T(4,128)}, bf16[2048,256]{1,0:T(8,128)(2,1)}, bf16[2048,2048]{1,0:T(8,128)(2,1)}) custom-call(bf16[48,128]{1,0:T(8,128)(2,1)} %pad_bitcast_fusion.1.vec_ref, s32[4,256]{1,0:T(4,128)} %pad_add_fusion.2.place_ref, bf16[512,256]{1,0:T(8,128)(2,1)} %wkv_ref.1, bf16[512,2048]{1,0:T(8,128)(2,1)} %wq_ref.1), custom_call_target="tpu_custom_call" | custom-call | tf_op jit(solution)/shard_map/gather_head/pallas_call | solution.py:187
  109.3 9.9 %add_convert_fusion.6 = bf16[512,2048]{1,0:T(8,128)(2,1)} fusion(bf16[512,2048]{1,0:T(8,128)(2,1)} %add_convert_fusion.7, bf16[2048,2048]{1,0:T(8,128)(2,1)} %get-tuple-element.33, f32[2048]{0:T(1024)S(1)} %bitcast.315), kind=kOutput, calls=%fused_computation.65 | convolution fusion | flops 4297064448 | bytes 12591104 | tf_op jit(solution)/shard_map/dot_general | solution.py:48
  122.7 4.3 collective-permute-done.5
  139.8 20.2 %attend_forward.2 = (bf16[256,2048]{1,0:T(8,128)(2,1)S(1)}, f32[8,2,256]{2,1,0:T(2,128)S(1)}) custom-call(bf16[256,2048]{1,0:T(8,128)(2,1)S(1)} %slice.549.q_ref, bf16[2048,256]{1,0:T(8,128)(2,1)S(1)} %get-tuple-element.101.kv_ref, s32[2048,2]{1,0:T(8,128)S(1)} %copy.48.kplace_ref, s32[2,256]{1,0:T(2,128)S(1)} %get-tuple-element.140.qplace_ref), custom_call_target="tpu_custom_call" | custom-call | flops 8589934592 | bytes 2097152 | tf_op jit(solution)/shard_map/attend_forward/pallas_call | solution.py:284
  160.1 19.2 %collective-permute-done.14 = bf16[512,2048]{1,0:T(8,128)(2,1)} collective-permute-done((bf16[512,2048]{1,0:T(8,128)(2,1)}, bf16[512,2048]{1,0:T(8,128)(2,1)}, u32[]{:S(2)}, u32[]{:S(2)}) %collective-permute-start.14) | collective-permute-done | bytes 2097184 | tf_op jit(solution)/shard_map/ppermute | solution.py:64
  189.4 19.9 %attend_forward.3 = (bf16[256,2048]{1,0:T(8,128)(2,1)S(1)}, f32[8,2,256]{2,1,0:T(2,128)S(1)}) custom-call(bf16[256,2048]{1,0:T(8,128)(2,1)S(1)} %add_convert_fusion.13.q_ref, bf16[2048,256]{1,0:T(8,128)(2,1)S(1)} %get-tuple-element.100.kv_ref, s32[2048,2]{1,0:T(8,128)S(1)} %copy.49.kplace_ref, s32[2,256]{1,0:T(2,128)S(1)} %get-tuple-element.141.qplace_ref), custom_call_target="tpu_custom_call" | custom-call | flops 8589934592 | bytes 2097152 | tf_op jit(solution)/shard_map/attend_forward/pallas_call | solution.py:284
  223.1 18.4 %collective-permute-done.9 = bf16[256,2048]{1,0:T(8,128)(2,1)S(1)} collective-permute-done((bf16[256,2048]{1,0:T(8,128)(2,1)S(1)}, bf16[256,2048]{1,0:T(8,128)(2,1)S(1)}, u32[]{:S(2)}, u32[]{:S(2)}) %collective-permute-start.9) | collective-permute-done | bytes 1048608 | tf_op jit(solution)/shard_map/ppermute | solution.py:64
  249.0 28.7 %multiply_convert_fusion.1 = (bf16[2048,2048]{1,0:T(8,128)(2,1)S(1)}, f32[2048,2048]{1,0:T(8,128)}) fusion(f32[2048]{0:T(1024)S(1)} %bitcast.313, bf16[2048,2048]{1,0:T(8,128)(2,1)} %constant_dynamic-update-slice_fusion.8, bf16[2048,2048]{1,0:T(8,128)(2,1)} %all-gather.6.cloned.1.call-done), kind=kOutput, calls=%fused_computation.10 | convolution fusion | flops 17221812224 | bytes 41951232 | tf_op jit(solution)/shard_map/dot_general | solution.py:48
  281.0 20.6 %convolution_convert_fusion.1 = bf16[2048,2048]{1,0:T(8,128)(2,1)} fusion(bf16[2048,2048]{1,0:T(8,128)(2,1)S(1)} %get-tuple-element.41, bf16[2048,2048]{1,0:T(8,128)(2,1)S(1)} %copy-done.62), kind=kOutput, calls=%fused_computation.13 | convolution fusion | flops 17184063488 | bytes 25165824 | tf_op jit(solution)/shard_map/dot_general | solution.py:56
  301.7 35.3 %convert_reduce_fusion = (f32[2048]{0:T(1024)}, bf16[2048,2048]{1,0:T(8,128)(2,1)}) fusion(f32[2048,2048]{1,0:T(8,128)} %get-tuple-element.136, f32[2048]{0:T(1024)S(1)} %bitcast.314, bf16[2048,2048]{1,0:T(8,128)(2,1)} %copy-done.61, bf16[2048,2048]{1,0:T(8,128)(2,1)} %all-gather.8.cloned.1.call-done), kind=kOutput, calls=%fused_computation.8 | convolution fusion | flops 17280530432 | bytes 41959424 | tf_op jit(solution)/shard_map/dot_general | solution.py:52
  337.0 13.2 %fusion.30 = bf16[1024,2048]{1,0:T(8,128)(2,1)S(1)} fusion(bf16[2048,2048]{1,0:T(8,128)(2,1)} %all-gather.6.cloned.1.call-done, bf16[2048,2048]{1,0:T(8,128)(2,1)} %get-tuple-element.139), kind=kOutput, calls=%fused_computation.71 | convolution fusion | flops 8592031744 | bytes 16777216 | tf_op jit(solution)/shard_map/dot_general | solution.py:52
  350.3 7.1 collective-permute-done.17
  358.6 11.7 %fusion.12 = bf16[512,2048]{1,0:T(8,128)(2,1)S(1)} fusion(f32[1024,2048]{1,0:T(8,128)S(1)} %convert_element_type.453, bf16[2048,2048]{1,0:T(8,128)(2,1)} %all-gather.6.cloned.1.call-done, bf16[2048,2048]{1,0:T(8,128)(2,1)} %get-tuple-element.139), kind=kOutput, calls=%fused_computation.31 | convolution fusion | flops 4297064448 | bytes 16777216 | tf_op jit(solution)/shard_map/dot_general | solution.py:52
  372.4 24.1 %convolution_convert_fusion = bf16[2048,2048]{1,0:T(8,128)(2,1)} fusion(bf16[2048,2048]{1,0:T(8,128)(2,1)} %constant_dynamic-update-slice_fusion.8, bf16[2048,2048]{1,0:T(8,128)(2,1)} %get-tuple-element.139), kind=kOutput, calls=%fused_computation.12 | convolution fusion | flops 17184063488 | bytes 25165824 | tf_op jit(solution)/shard_map/dot_general | solution.py:56
  396.5 14.1 %fusion.27 = bf16[1024,2048]{1,0:T(8,128)(2,1)} fusion(bf16[2048,2048]{1,0:T(8,128)(2,1)} %all-gather.8.cloned.1.call-done, bf16[2048,2048]{1,0:T(8,128)(2,1)} %copy-done.92), kind=kOutput, calls=%fused_computation.70 | convolution fusion | flops 8592031744 | bytes 16777216 | tf_op jit(solution)/shard_map/dot_general | solution.py:48
  412.3 6.0 collective-permute-done.19
  418.3 4.0 convert_element_type.457
  422.3 9.0 fusion.11
  431.4 7.0 slice_add_fusion.2
  445.3 10.8 %multiply_reduce_fusion = (f32[2048]{0:T(1024)S(1)}, f32[512]{0:T(512)S(1)}, f32[512]{0:T(512)S(1)}, f32[2048]{0:T(1024)S(1)}, f32[512,2048]{1,0:T(8,128)S(1)}) fusion(f32[512]{0:T(512)S(1)} %add_rsqrt_fusion, f32[512]{0:T(512)S(1)} %broadcast_multiply_fusion.4, f32[]{:T(128)} %bitcast.14, f32[256,2048]{1,0:T(8,128)} %copy-done.25, ...), kind=kOutput, calls=%fused_computation.51 | convolution fusion | flops 4312787968 | bytes 25199104 | tf_op jit(solution)/shard_map/dot_general | solution.py:52
  456.1 12.5 %collective-permute-done.22 = bf16[128,2048]{1,0:T(8,128)(2,1)S(1)} collective-permute-done((bf16[128,2048]{1,0:T(8,128)(2,1)S(1)}, bf16[128,2048]{1,0:T(8,128)(2,1)S(1)}, u32[]{:S(2)}, u32[]{:S(2)}) %collective-permute-start.22) | collective-permute-done | bytes 524320 | tf_op jit(solution)/shard_map/ppermute | solution.py:64
  470.1 5.5 convert_reduce_fusion.2
  478.1 4.9 add_convert_fusion.4
  483.1 11.9 %collective-permute-done.23 = bf16[128,2048]{1,0:T(8,128)(2,1)S(1)} collective-permute-done((bf16[128,2048]{1,0:T(8,128)(2,1)S(1)}, bf16[128,2048]{1,0:T(8,128)(2,1)S(1)}, u32[]{:S(2)}, u32[]{:S(2)}) %collective-permute-start.23) | collective-permute-done | bytes 524320 | tf_op jit(solution)/shard_map/ppermute | solution.py:64
  496.8 24.2 %attend_backward.2 = (bf16[256,2048]{1,0:T(8,128)(2,1)S(1)}, f32[2048,256]{1,0:T(8,128)S(1)}) custom-call(bf16[256,2048]{1,0:T(8,128)(2,1)S(1)} %copy-done.7, bf16[256,2048]{1,0:T(8,128)(2,1)S(1)} %add_convert_fusion.11.do_ref, bf16[256,2048]{1,0:T(8,128)(2,1)S(1)} %copy-done.9, f32[8,2,256]{2,1,0:T(2,128)S(1)} %get-tuple-element.42.lse_ref, ...), custom_call_target="tpu_custom_call" | custom-call | flops 19327352832 | bytes 4194304 | tf_op jit(solution)/shard_map/attend_backward/pallas_call | solution.py:313
  533.0 23.7 %attend_backward.3 = (bf16[256,2048]{1,0:T(8,128)(2,1)S(1)}, f32[2048,256]{1,0:T(8,128)S(1)}) custom-call(bf16[256,2048]{1,0:T(8,128)(2,1)S(1)} %copy-done.3, bf16[256,2048]{1,0:T(8,128)(2,1)S(1)} %add_convert_fusion.10.do_ref, bf16[256,2048]{1,0:T(8,128)(2,1)S(1)} %copy-done.12, f32[8,2,256]{2,1,0:T(2,128)S(1)} %get-tuple-element.44.lse_ref, ...), custom_call_target="tpu_custom_call" | custom-call | flops 19327352832 | bytes 4194304 | tf_op jit(solution)/shard_map/attend_backward/pallas_call | solution.py:313
  565.9 8.5 convolution_convert_fusion.2
  581.3 6.9 fusion.24
  599.3 19.6 %collective-permute-done.31 = bf16[2,2,256,256]{3,2,1,0:T(8,128)(2,1)S(1)} collective-permute-done((bf16[2,2,256,256]{3,2,1,0:T(8,128)(2,1)S(1)}, bf16[2,2,256,256]{3,2,1,0:T(8,128)(2,1)S(1)}, u32[]{:S(2)}, u32[]{:S(2)}) %collective-permute-start.31) | collective-permute-done | bytes 524320 | tf_op jit(solution)/shard_map/ppermute | solution.py:64
  631.7 9.6 fusion.110
  649.0 8.5 broadcast.148
  657.6 3.9 convert_dynamic-update-slice_fusion.3
  680.4 93.8 %collective-permute-done.35 = bf16[256,1024]{1,0:T(8,128)(2,1)S(1)} collective-permute-done((bf16[256,1024]{1,0:T(8,128)(2,1)S(1)}, bf16[256,1024]{1,0:T(8,128)(2,1)S(1)}, u32[]{:S(2)}, u32[]{:S(2)}) %collective-permute-start.35) | collective-permute-done | bytes 524320 | tf_op jit(solution)/shard_map/ppermute | solution.py:64
  776.1 4.0 add_convert_fusion.3
  781.3 9.5 collective-permute-done.36
  793.3 4.5 broadcast_in_dim.76
  797.8 3.9 bitcast_dynamic-update-slice_fusion.3
  804.2 4.1 convert_dynamic-update-slice_fusion.2
  808.3 43.9 %collective-permute-done.44 = bf16[128,1024]{1,0:T(8,128)(2,1)S(1)} collective-permute-done((bf16[128,1024]{1,0:T(8,128)(2,1)}, bf16[128,1024]{1,0:T(8,128)(2,1)S(1)}, u32[]{:S(2)}, u32[]{:S(2)}) %collective-permute-start.44) | collective-permute-done | bytes 262176 | tf_op jit(solution)/shard_map/ppermute | solution.py:64
  855.3 4.1 convert_dynamic-update-slice_fusion.1
  860.8 5.6 collective-permute-done.45
  874.3 4.1 convert_dynamic-update-slice_fusion
  879.6 4.4 fusion.51
  894.5 4.8 collective-permute-done.43
  904.7 12.3 %collective-permute-done.49 = bf16[128,1152]{1,0:T(8,128)(2,1)S(1)} collective-permute-done((bf16[128,1152]{1,0:T(8,128)(2,1)S(1)}, bf16[128,1152]{1,0:T(8,128)(2,1)S(1)}, u32[]{:S(2)}, u32[]{:S(2)}) %collective-permute-start.49) | collective-permute-done | bytes 294944 | tf_op jit(solution)/shard_map/ppermute | solution.py:64
  920.5 4.0 slice_bitcast_fusion
  935.4 12.0 %collective-permute-done.51 = bf16[256,1152]{1,0:T(8,128)(2,1)S(1)} collective-permute-done((bf16[256,1152]{1,0:T(8,128)(2,1)S(1)}, bf16[256,1152]{1,0:T(8,128)(2,1)S(1)}, u32[]{:S(2)}, u32[]{:S(2)}) %collective-permute-start.51) | collective-permute-done | bytes 589856 | tf_op jit(solution)/shard_map/ppermute | solution.py:64
  953.7 11.7 %convert_element_type.558 = f32[512,8192]{1,0:T(8,128)} convert(bf16[512,8192]{1,0:T(8,128)(2,1)} %slice_dynamic-update-slice_fusion) | non-fusion elementwise | flops 4194304 | bytes 25165824 | tf_op jit(solution)/shard_map/convert_element_type | solution.py:639
  (530 shorter events, 221.3 us)
Async XLA Ops:
  7.2 101.1 %all-gather.4.cloned.1.call-start = ((), (), s32[]{:S(2)}) async-start(), calls=%async_computation.4 | async-start | bytes 5242880 | tf_op jit(solution)/shard_map/all_gather | solution.py:443
  9.9 239.1 %all-gather.6.cloned.1.call-start = ((), (), s32[]{:S(2)}) async-start(), calls=%async_computation.5 | async-start | bytes 10485760 | tf_op jit(solution)/shard_map/all_gather | solution.py:454
  13.4 288.3 %all-gather.8.cloned.1.call-start = ((), (), s32[]{:S(2)}) async-start(), calls=%async_computation.6 | async-start | bytes 10485760 | tf_op jit(solution)/shard_map/all_gather | solution.py:455
  102.8 18.4 %collective-permute-start = (bf16[2,256,256]{2,1,0:T(8,128)(2,1)S(1)}, bf16[2,256,256]{2,1,0:T(8,128)(2,1)S(1)}, u32[]{:S(2)}, u32[]{:S(2)}) collective-permute-start(bf16[2,256,256]{2,1,0:T(8,128)(2,1)S(1)} %bitcast.280), channel_id=1, source_target_pairs={{0,1},{1,0},{2,3},{3,2},{4,5},{5,4},{6,7},{7,6},{8,9},{9,8},{10,11... | collective-permute-start | bytes 786440 | tf_op jit(solution)/shard_map/ppermute | solution.py:64
  103.0 16.3 %collective-permute-start.1 = (bf16[2,256,256]{2,1,0:T(8,128)(2,1)S(1)}, bf16[2,256,256]{2,1,0:T(8,128)(2,1)S(1)}, u32[]{:S(2)}, u32[]{:S(2)}) collective-permute-start(bf16[2,256,256]{2,1,0:T(8,128)(2,1)S(1)} %bitcast.281), channel_id=1, source_target_pairs={{0,2},{1,3},{2,0},{3,1},{4,6},{5,7},{6,4},{7,5},{8,10},{9,11},{10,... | collective-permute-start | bytes 786440 | tf_op jit(solution)/shard_map/ppermute | solution.py:64
  104.3 15.0 %collective-permute-start.3 = (bf16[2,256,256]{2,1,0:T(8,128)(2,1)S(1)}, bf16[2,256,256]{2,1,0:T(8,128)(2,1)S(1)}, u32[]{:S(2)}, u32[]{:S(2)}) collective-permute-start(bf16[2,256,256]{2,1,0:T(8,128)(2,1)S(1)} %bitcast.282), channel_id=1, source_target_pairs={{0,4},{1,5},{2,6},{3,7},{4,0},{5,1},{6,2},{7,3},{8,12},{9,13},{10,... | collective-permute-start | bytes 786440 | tf_op jit(solution)/shard_map/ppermute | solution.py:64
  108.2 333.9 %reduce-scatter.5.cloned.1.call-start = ((), (), s32[]{:S(2)}) async-start(), calls=%async_computation.7 | async-start | bytes 10485760 | tf_op jit(solution)/shard_map/reduce_scatter | solution.py:504
  108.3 73.1 %collective-permute-start.7 = (bf16[2048,1024]{1,0:T(8,128)(2,1)}, bf16[2048,1024]{1,0:T(8,128)(2,1)}, u32[]{:S(2)}, u32[]{:S(2)}) collective-permute-start(bf16[2048,1024]{1,0:T(8,128)(2,1)} %all-gather.4.cloned.1.call-done), channel_id=1, source_target_pairs={{0,1},{1,0},{2,3},{3,2},{4,5},{5,4},{6,7},{7,6},{8,9},{9,8},{10,11... | collective-permute-start | bytes 12582920 | tf_op jit(solution)/shard_map/ppermute | solution.py:64
  131.7 47.6 %collective-permute-start.14 = (bf16[512,2048]{1,0:T(8,128)(2,1)}, bf16[512,2048]{1,0:T(8,128)(2,1)}, u32[]{:S(2)}, u32[]{:S(2)}) collective-permute-start(bf16[512,2048]{1,0:T(8,128)(2,1)} %bitcast.13), channel_id=1, source_target_pairs={{0,2},{1,3},{2,0},{3,1},{4,6},{5,7},{6,4},{7,5},{8,10},{9,11},{10,... | collective-permute-start | bytes 6291464 | tf_op jit(solution)/shard_map/ppermute | solution.py:64
  137.0 85.0 %collective-permute-start.15 = (bf16[512,2048]{1,0:T(8,128)(2,1)}, bf16[512,2048]{1,0:T(8,128)(2,1)S(1)}, u32[]{:S(2)}, u32[]{:S(2)}) collective-permute-start(bf16[512,2048]{1,0:T(8,128)(2,1)} %bitcast.13), channel_id=1, source_target_pairs={{0,1},{1,0},{2,3},{3,2},{4,5},{5,4},{6,7},{7,6},{8,9},{9,8},{10,11... | collective-permute-start | bytes 6291464 | tf_op jit(solution)/shard_map/ppermute | solution.py:64
  179.3 43.5 %collective-permute-start.16 = (bf16[512,2048]{1,0:T(8,128)(2,1)}, bf16[512,2048]{1,0:T(8,128)(2,1)S(1)}, u32[]{:S(2)}, u32[]{:S(2)}) collective-permute-start(bf16[512,2048]{1,0:T(8,128)(2,1)} %collective-permute-done.14), channel_id=1, source_target_pairs={{0,1},{1,0},{2,3},{3,2},{4,5},{5,4},{6,7},{7,6},{8,9},{9,8},{10,11... | collective-permute-start | bytes 6291464 | tf_op jit(solution)/shard_map/ppermute | solution.py:64
  188.0 34.3 %collective-permute-start.8 = (bf16[256,2048]{1,0:T(8,128)(2,1)S(1)}, bf16[256,2048]{1,0:T(8,128)(2,1)S(1)}, u32[]{:S(2)}, u32[]{:S(2)}) collective-permute-start(bf16[256,2048]{1,0:T(8,128)(2,1)S(1)} %get-tuple-element.73), channel_id=1, source_target_pairs={{0,2},{1,3},{2,0},{3,1},{4,6},{5,7},{6,4},{7,5},{8,10},{9,11},{10,... | collective-permute-start | bytes 3145736 | tf_op jit(solution)/shard_map/ppermute | solution.py:64
  216.9 24.6 %collective-permute-start.9 = (bf16[256,2048]{1,0:T(8,128)(2,1)S(1)}, bf16[256,2048]{1,0:T(8,128)(2,1)S(1)}, u32[]{:S(2)}, u32[]{:S(2)}) collective-permute-start(bf16[256,2048]{1,0:T(8,128)(2,1)S(1)} %get-tuple-element.69), channel_id=1, source_target_pairs={{0,2},{1,3},{2,0},{3,1},{4,6},{5,7},{6,4},{7,5},{8,10},{9,11},{10,... | collective-permute-start | bytes 3145736 | tf_op jit(solution)/shard_map/ppermute | solution.py:64
  221.4 23.3 %collective-permute-start.10 = (bf16[256,2048]{1,0:T(8,128)(2,1)S(1)}, bf16[256,2048]{1,0:T(8,128)(2,1)S(1)}, u32[]{:S(2)}, u32[]{:S(2)}) collective-permute-start(bf16[256,2048]{1,0:T(8,128)(2,1)S(1)} %get-tuple-element.73), channel_id=1, source_target_pairs={{0,1},{1,0},{2,3},{3,2},{4,5},{5,4},{6,7},{7,6},{8,9},{9,8},{10,11... | collective-permute-start | bytes 3145736 | tf_op jit(solution)/shard_map/ppermute | solution.py:64
  222.0 23.8 %collective-permute-start.11 = (bf16[256,2048]{1,0:T(8,128)(2,1)S(1)}, bf16[256,2048]{1,0:T(8,128)(2,1)S(1)}, u32[]{:S(2)}, u32[]{:S(2)}) collective-permute-start(bf16[256,2048]{1,0:T(8,128)(2,1)S(1)} %get-tuple-element.69), channel_id=1, source_target_pairs={{0,1},{1,0},{2,3},{3,2},{4,5},{5,4},{6,7},{7,6},{8,9},{9,8},{10,11... | collective-permute-start | bytes 3145736 | tf_op jit(solution)/shard_map/ppermute | solution.py:64
  222.3 24.5 %collective-permute-start.12 = (bf16[256,2048]{1,0:T(8,128)(2,1)S(1)}, bf16[256,2048]{1,0:T(8,128)(2,1)S(1)}, u32[]{:S(2)}, u32[]{:S(2)}) collective-permute-start(bf16[256,2048]{1,0:T(8,128)(2,1)S(1)} %collective-permute-done.8), channel_id=1, source_target_pairs={{0,1},{1,0},{2,3},{3,2},{4,5},{5,4},{6,7},{7,6},{8,9},{9,8},{10,11... | collective-permute-start | bytes 3145736 | tf_op jit(solution)/shard_map/ppermute | solution.py:64
  301.6 368.6 %reduce-scatter.7.cloned.1.call-start = ((), (), s32[]{:S(2)}) async-start(), calls=%async_computation.8 | async-start | bytes 10485760 | tf_op jit(solution)/shard_map/reduce_scatter | solution.py:504
  371.4 25.1 %collective-permute-start.18 = (bf16[256,2048]{1,0:T(8,128)(2,1)S(1)}, bf16[256,2048]{1,0:T(8,128)(2,1)S(1)}, u32[]{:S(2)}, u32[]{:S(2)}) collective-permute-start(bf16[256,2048]{1,0:T(8,128)(2,1)S(1)} %get-tuple-element.99), channel_id=1, source_target_pairs={{0,2},{1,3},{2,0},{3,1},{4,6},{5,7},{6,4},{7,5},{8,10},{9,11},{10,... | collective-permute-start | bytes 3145736 | tf_op jit(solution)/shard_map/ppermute | solution.py:64
  411.2 154.1 %collective-permute-start.26 = (bf16[512,2048]{1,0:T(8,128)(2,1)}, bf16[512,2048]{1,0:T(8,128)(2,1)}, u32[]{:S(2)}, u32[]{:S(2)}) collective-permute-start(bf16[512,2048]{1,0:T(8,128)(2,1)} %add_convert_fusion.7), channel_id=1, source_target_pairs={{0,1},{1,0},{2,3},{3,2},{4,5},{5,4},{6,7},{7,6},{8,9},{9,8},{10,11... | collective-permute-start | bytes 6291464 | tf_op jit(solution)/shard_map/ppermute | solution.py:64
  411.2 34.1 %collective-permute-start.21 = (bf16[256,2048]{1,0:T(8,128)(2,1)}, bf16[256,2048]{1,0:T(8,128)(2,1)}, u32[]{:S(2)}, u32[]{:S(2)}) collective-permute-start(bf16[256,2048]{1,0:T(8,128)(2,1)} %get-tuple-element.98), channel_id=1, source_target_pairs={{0,2},{1,3},{2,0},{3,1},{4,6},{5,7},{6,4},{7,5},{8,10},{9,11},{10,... | collective-permute-start | bytes 3145736 | tf_op jit(solution)/shard_map/ppermute | solution.py:64
  412.2 262.6 %reduce-scatter.9.cloned.1.call-start = ((), (), s32[]{:S(2)}) async-start(), calls=%async_computation.9 | async-start | bytes 5242880 | tf_op jit(solution)/shard_map/reduce_scatter | solution.py:500
  443.2 25.4 %collective-permute-start.22 = (bf16[128,2048]{1,0:T(8,128)(2,1)S(1)}, bf16[128,2048]{1,0:T(8,128)(2,1)S(1)}, u32[]{:S(2)}, u32[]{:S(2)}) collective-permute-start(bf16[128,2048]{1,0:T(8,128)(2,1)S(1)} %slice.572), channel_id=1, source_target_pairs={{0,4},{1,5},{2,6},{3,7},{4,0},{5,1},{6,2},{7,3},{8,12},{9,13},{10,... | collective-permute-start | bytes 1572872 | tf_op jit(solution)/shard_map/ppermute | solution.py:64
  470.0 24.9 %collective-permute-start.23 = (bf16[128,2048]{1,0:T(8,128)(2,1)S(1)}, bf16[128,2048]{1,0:T(8,128)(2,1)S(1)}, u32[]{:S(2)}, u32[]{:S(2)}) collective-permute-start(bf16[128,2048]{1,0:T(8,128)(2,1)S(1)} %add_convert_fusion.20), channel_id=1, source_target_pairs={{0,4},{1,5},{2,6},{3,7},{4,0},{5,1},{6,2},{7,3},{8,12},{9,13},{10,... | collective-permute-start | bytes 1572872 | tf_op jit(solution)/shard_map/ppermute | solution.py:64
  496.5 26.8 %collective-permute-start.24 = (bf16[128,2048]{1,0:T(8,128)(2,1)S(1)}, bf16[128,2048]{1,0:T(8,128)(2,1)S(1)}, u32[]{:S(2)}, u32[]{:S(2)}) collective-permute-start(bf16[128,2048]{1,0:T(8,128)(2,1)S(1)} %add_convert_fusion.18), channel_id=1, source_target_pairs={{0,4},{1,5},{2,6},{3,7},{4,0},{5,1},{6,2},{7,3},{8,12},{9,13},{10,... | collective-permute-start | bytes 1572872 | tf_op jit(solution)/shard_map/ppermute | solution.py:64
  525.5 31.4 %collective-permute-start.27 = (bf16[128,2048]{1,0:T(8,128)(2,1)}, bf16[128,2048]{1,0:T(8,128)(2,1)}, u32[]{:S(2)}, u32[]{:S(2)}) collective-permute-start(bf16[128,2048]{1,0:T(8,128)(2,1)} %add_convert_fusion.16), channel_id=1, source_target_pairs={{0,4},{1,5},{2,6},{3,7},{4,0},{5,1},{6,2},{7,3},{8,12},{9,13},{10,... | collective-permute-start | bytes 1572872 | tf_op jit(solution)/shard_map/ppermute | solution.py:64
  565.1 13.9 %collective-permute-start.25 = (bf16[512,2048]{1,0:T(8,128)(2,1)}, bf16[512,2048]{1,0:T(8,128)(2,1)}, u32[]{:S(2)}, u32[]{:S(2)}) collective-permute-start(bf16[512,2048]{1,0:T(8,128)(2,1)} %pad_maximum_fusion.8), channel_id=1, source_target_pairs={{0,1},{1,0},{2,3},{3,2},{4,5},{5,4},{6,7},{7,6},{8,9},{9,8},{10,11... | collective-permute-start | bytes 6291464 | tf_op jit(solution)/shard_map/ppermute | solution.py:64
  576.3 309.3 %reduce-scatter.11.cloned.1.call-start = ((), (), s32[]{:S(2)}) async-start(), calls=%async_computation.10 | async-start | bytes 5898240 | tf_op jit(solution)/shard_map/reduce_scatter | solution.py:500
  594.8 24.0 %collective-permute-start.31 = (bf16[2,2,256,256]{3,2,1,0:T(8,128)(2,1)S(1)}, bf16[2,2,256,256]{3,2,1,0:T(8,128)(2,1)S(1)}, u32[]{:S(2)}, u32[]{:S(2)}) collective-permute-start(bf16[2,2,256,256]{3,2,1,0:T(8,128)(2,1)S(1)} %pad_maximum_fusion.12), channel_id=1, source_target_pairs={{0,4},{1,5},{2,6},{3,7},{4,0},{5,1},{6,2},{7,3},{8,12},{9,13},{10,... | collective-permute-start | bytes 1572872 | tf_op jit(solution)/shard_map/ppermute | solution.py:64
  622.3 53.9 %collective-permute-start.20 = (bf16[256,2048]{1,0:T(8,128)(2,1)}, bf16[256,2048]{1,0:T(8,128)(2,1)}, u32[]{:S(2)}, u32[]{:S(2)}) collective-permute-start(bf16[256,2048]{1,0:T(8,128)(2,1)} %get-tuple-element.88), channel_id=1, source_target_pairs={{0,2},{1,3},{2,0},{3,1},{4,6},{5,7},{6,4},{7,5},{8,10},{9,11},{10,... | collective-permute-start | bytes 3145736 | tf_op jit(solution)/shard_map/ppermute | solution.py:64
  623.8 55.2 %collective-permute-start.33 = (bf16[256,2048]{1,0:T(8,128)(2,1)}, bf16[256,2048]{1,0:T(8,128)(2,1)}, u32[]{:S(2)}, u32[]{:S(2)}) collective-permute-start(bf16[256,2048]{1,0:T(8,128)(2,1)} %get-tuple-element.89), channel_id=1, source_target_pairs={{0,2},{1,3},{2,0},{3,1},{4,6},{5,7},{6,4},{7,5},{8,10},{9,11},{10,... | collective-permute-start | bytes 3145736 | tf_op jit(solution)/shard_map/ppermute | solution.py:64
  629.4 13.1 %collective-permute-start.47 = (bf16[512,128]{1,0:T(8,128)(2,1)S(1)}, bf16[512,128]{1,0:T(8,128)(2,1)S(1)}, u32[]{:S(2)}, u32[]{:S(2)}) collective-permute-start(bf16[512,128]{1,0:T(8,128)(2,1)S(1)} %get-tuple-element.107), channel_id=1, source_target_pairs={{0,1},{1,0},{2,3},{3,2},{4,5},{5,4},{6,7},{7,6},{8,9},{9,8},{10,11... | collective-permute-start | bytes 393224 | tf_op jit(solution)/shard_map/ppermute | solution.py:64
  661.4 140.5 %collective-permute-start.55 = (bf16[512,2048]{1,0:T(8,128)(2,1)}, bf16[512,2048]{1,0:T(8,128)(2,1)}, u32[]{:S(2)}, u32[]{:S(2)}) collective-permute-start(bf16[512,2048]{1,0:T(8,128)(2,1)} %get-tuple-element.57), channel_id=1, source_target_pairs={{0,2},{1,3},{2,0},{3,1},{4,6},{5,7},{6,4},{7,5},{8,10},{9,11},{10,... | collective-permute-start | bytes 6291464 | tf_op jit(solution)/shard_map/ppermute | solution.py:64
  661.5 193.8 %collective-permute-start.56 = (bf16[512,2048]{1,0:T(8,128)(2,1)}, bf16[512,2048]{1,0:T(8,128)(2,1)}, u32[]{:S(2)}, u32[]{:S(2)}) collective-permute-start(bf16[512,2048]{1,0:T(8,128)(2,1)} %get-tuple-element.57), channel_id=1, source_target_pairs={{0,1},{1,0},{2,3},{3,2},{4,5},{5,4},{6,7},{7,6},{8,9},{9,8},{10,11... | collective-permute-start | bytes 6291464 | tf_op jit(solution)/shard_map/ppermute | solution.py:64
  673.6 119.6 %collective-permute-start.34 = (bf16[512,2048]{1,0:T(8,128)(2,1)}, bf16[512,2048]{1,0:T(8,128)(2,1)}, u32[]{:S(2)}, u32[]{:S(2)}) collective-permute-start(bf16[512,2048]{1,0:T(8,128)(2,1)} %fusion.9), channel_id=1, source_target_pairs={{0,4},{1,5},{2,6},{3,7},{4,0},{5,1},{6,2},{7,3},{8,12},{9,13},{10,... | collective-permute-start | bytes 6291464 | tf_op jit(solution)/shard_map/ppermute | solution.py:64
  676.2 98.1 %collective-permute-start.35 = (bf16[256,1024]{1,0:T(8,128)(2,1)S(1)}, bf16[256,1024]{1,0:T(8,128)(2,1)S(1)}, u32[]{:S(2)}, u32[]{:S(2)}) collective-permute-start(bf16[256,1024]{1,0:T(8,128)(2,1)S(1)} %pad_maximum_fusion.13), channel_id=1, source_target_pairs={{0,2},{1,3},{2,0},{3,1},{4,6},{5,7},{6,4},{7,5},{8,10},{9,11},{10,... | collective-permute-start | bytes 1572872 | tf_op jit(solution)/shard_map/ppermute | solution.py:64
  775.8 15.0 %collective-permute-start.36 = (bf16[128,1024]{1,0:T(8,128)(2,1)}, bf16[128,1024]{1,0:T(8,128)(2,1)}, u32[]{:S(2)}, u32[]{:S(2)}) collective-permute-start(bf16[128,1024]{1,0:T(8,128)(2,1)} %fusion.75), channel_id=1, source_target_pairs={{0,4},{1,5},{2,6},{3,7},{4,0},{5,1},{6,2},{7,3},{8,12},{9,13},{10,... | collective-permute-start | bytes 786440 | tf_op jit(solution)/shard_map/ppermute | solution.py:64
  801.7 66.5 %collective-permute-start.37 = (bf16[512,2048]{1,0:T(8,128)(2,1)S(1)}, bf16[512,2048]{1,0:T(8,128)(2,1)}, u32[]{:S(2)}, u32[]{:S(2)}) collective-permute-start(bf16[512,2048]{1,0:T(8,128)(2,1)S(1)} %get-tuple-element.59), channel_id=1, source_target_pairs={{0,2},{1,3},{2,0},{3,1},{4,6},{5,7},{6,4},{7,5},{8,10},{9,11},{10,... | collective-permute-start | bytes 6291464 | tf_op jit(solution)/shard_map/ppermute | solution.py:64
  801.9 72.3 %collective-permute-start.57 = (bf16[512,2048]{1,0:T(8,128)(2,1)}, bf16[512,2048]{1,0:T(8,128)(2,1)}, u32[]{:S(2)}, u32[]{:S(2)}) collective-permute-start(bf16[512,2048]{1,0:T(8,128)(2,1)} %collective-permute-done.55), channel_id=1, source_target_pairs={{0,1},{1,0},{2,3},{3,2},{4,5},{5,4},{6,7},{7,6},{8,9},{9,8},{10,11... | collective-permute-start | bytes 6291464 | tf_op jit(solution)/shard_map/ppermute | solution.py:64
  802.5 49.7 %collective-permute-start.44 = (bf16[128,1024]{1,0:T(8,128)(2,1)}, bf16[128,1024]{1,0:T(8,128)(2,1)S(1)}, u32[]{:S(2)}, u32[]{:S(2)}) collective-permute-start(bf16[128,1024]{1,0:T(8,128)(2,1)} %copy-done.59), channel_id=1, source_target_pairs={{0,4},{1,5},{2,6},{3,7},{4,0},{5,1},{6,2},{7,3},{8,12},{9,13},{10,... | collective-permute-start | bytes 786440 | tf_op jit(solution)/shard_map/ppermute | solution.py:64
  853.2 13.2 %collective-permute-start.45 = (bf16[256,1024]{1,0:T(8,128)(2,1)S(1)}, bf16[256,1024]{1,0:T(8,128)(2,1)S(1)}, u32[]{:S(2)}, u32[]{:S(2)}) collective-permute-start(bf16[256,1024]{1,0:T(8,128)(2,1)S(1)} %pad_maximum_fusion.14), channel_id=1, source_target_pairs={{0,2},{1,3},{2,0},{3,1},{4,6},{5,7},{6,4},{7,5},{8,10},{9,11},{10,... | collective-permute-start | bytes 1572872 | tf_op jit(solution)/shard_map/ppermute | solution.py:64
  859.4 31.9 %collective-permute-start.53 = (bf16[512,2048]{1,0:T(8,128)(2,1)S(1)}, bf16[512,2048]{1,0:T(8,128)(2,1)}, u32[]{:S(2)}, u32[]{:S(2)}) collective-permute-start(bf16[512,2048]{1,0:T(8,128)(2,1)S(1)} %get-tuple-element.59), channel_id=1, source_target_pairs={{0,1},{1,0},{2,3},{3,2},{4,5},{5,4},{6,7},{7,6},{8,9},{9,8},{10,11... | collective-permute-start | bytes 6291464 | tf_op jit(solution)/shard_map/ppermute | solution.py:64
  866.5 13.2 %collective-permute-start.46 = (bf16[512,1024]{1,0:T(8,128)(2,1)S(1)}, bf16[512,1024]{1,0:T(8,128)(2,1)}, u32[]{:S(2)}, u32[]{:S(2)}) collective-permute-start(bf16[512,1024]{1,0:T(8,128)(2,1)S(1)} %bitcast.264), channel_id=1, source_target_pairs={{0,1},{1,0},{2,3},{3,2},{4,5},{5,4},{6,7},{7,6},{8,9},{9,8},{10,11... | collective-permute-start | bytes 3145736 | tf_op jit(solution)/shard_map/ppermute | solution.py:64
  884.0 33.3 %collective-permute-start.54 = (bf16[512,2048]{1,0:T(8,128)(2,1)}, bf16[512,2048]{1,0:T(8,128)(2,1)}, u32[]{:S(2)}, u32[]{:S(2)}) collective-permute-start(bf16[512,2048]{1,0:T(8,128)(2,1)} %collective-permute-done.37), channel_id=1, source_target_pairs={{0,1},{1,0},{2,3},{3,2},{4,5},{5,4},{6,7},{7,6},{8,9},{9,8},{10,11... | collective-permute-start | bytes 6291464 | tf_op jit(solution)/shard_map/ppermute | solution.py:64
  886.7 14.7 %collective-permute-start.48 = (bf16[256,1152]{1,0:T(8,128)(2,1)S(1)}, bf16[256,1152]{1,0:T(8,128)(2,1)S(1)}, u32[]{:S(2)}, u32[]{:S(2)}) collective-permute-start(bf16[256,1152]{1,0:T(8,128)(2,1)S(1)} %pad_maximum_fusion.10), channel_id=1, source_target_pairs={{0,2},{1,3},{2,0},{3,1},{4,6},{5,7},{6,4},{7,5},{8,10},{9,11},{10,... | collective-permute-start | bytes 1769480 | tf_op jit(solution)/shard_map/ppermute | solution.py:64
  901.5 15.5 %collective-permute-start.49 = (bf16[128,1152]{1,0:T(8,128)(2,1)S(1)}, bf16[128,1152]{1,0:T(8,128)(2,1)S(1)}, u32[]{:S(2)}, u32[]{:S(2)}) collective-permute-start(bf16[128,1152]{1,0:T(8,128)(2,1)S(1)} %fusion.65), channel_id=1, source_target_pairs={{0,4},{1,5},{2,6},{3,7},{4,0},{5,1},{6,2},{7,3},{8,12},{9,13},{10,... | collective-permute-start | bytes 884744 | tf_op jit(solution)/shard_map/ppermute | solution.py:64
  917.3 16.1 %collective-permute-start.50 = (bf16[128,1152]{1,0:T(8,128)(2,1)S(1)}, bf16[128,1152]{1,0:T(8,128)(2,1)S(1)}, u32[]{:S(2)}, u32[]{:S(2)}) collective-permute-start(bf16[128,1152]{1,0:T(8,128)(2,1)S(1)} %get-tuple-element.61), channel_id=1, source_target_pairs={{0,4},{1,5},{2,6},{3,7},{4,0},{5,1},{6,2},{7,3},{8,12},{9,13},{10,... | collective-permute-start | bytes 884744 | tf_op jit(solution)/shard_map/ppermute | solution.py:64
  933.4 14.0 %collective-permute-start.51 = (bf16[256,1152]{1,0:T(8,128)(2,1)S(1)}, bf16[256,1152]{1,0:T(8,128)(2,1)S(1)}, u32[]{:S(2)}, u32[]{:S(2)}) collective-permute-start(bf16[256,1152]{1,0:T(8,128)(2,1)S(1)} %pad_maximum_fusion.11), channel_id=1, source_target_pairs={{0,2},{1,3},{2,0},{3,1},{4,6},{5,7},{6,4},{7,5},{8,10},{9,11},{10,... | collective-permute-start | bytes 1769480 | tf_op jit(solution)/shard_map/ppermute | solution.py:64
  947.5 18.2 %collective-permute-start.52 = (bf16[512,1152]{1,0:T(8,128)(2,1)S(1)}, bf16[512,1152]{1,0:T(8,128)(2,1)S(1)}, u32[]{:S(2)}, u32[]{:S(2)}) collective-permute-start(bf16[512,1152]{1,0:T(8,128)(2,1)S(1)} %bitcast.261), channel_id=1, source_target_pairs={{0,1},{1,0},{2,3},{3,2},{4,5},{5,4},{6,7},{7,6},{8,9},{9,8},{10,11... | collective-permute-start | bytes 3538952 | tf_op jit(solution)/shard_map/ppermute | solution.py:64
  (113 other events, 1540.1 us)
Sparse Core Ops, SparseCore 0:
  10.4 84.6 all-gather.3
  97.5 86.5 all-gather.5
  186.6 87.5 all-gather.7
  301.8 85.7 reduce-scatter.4
  412.4 86.2 reduce-scatter.6
  576.4 51.5 reduce-scatter.8
  649.1 57.0 reduce-scatter.10

commit v5 on v4

--- a/solution.py
+++ b/solution.py
@@ -204,7 +204,7 @@
     )(vec, place, wkv, wq)
 
 
-HEAD_STEP = 2
+HEAD_STEP = 4
 KEY_STEP = 512
 
 
@@ -511,10 +511,10 @@
             own = product(x[:tok]) + got[:tok]
             return [swk(passed[m * rows : (m + 1) * rows], 2) for m in range(micros)], passed, own
 
-        d_before = (dot_t(after(cot, proj_term), w_proj) * slope.astype(F32)).astype(BF16)
+        d_before = (dot_t(cot, w_proj) * slope.astype(F32)).astype(BF16)
         came, passed, own = reduce_quad(d_before, lambda x: dot_t(x, w_fc))
         d_normed2 = own + jnp.concatenate(came).astype(F32)
-        fc_grad, fc_term = ffn_grad(after(normed2, passed), d_before)
+        fc_grad, fc_term = ffn_grad(after(normed2, passed, proj_term), d_before)
         fc_b_grad = jnp.sum(d_before.astype(F32), axis=0)
 
         def across_quads(x, parts):

time: 987 us -> 981 us (level)
  transfers between devices with their start and end apart: 65 -> 65, of which waited for: 20 -> 21; matrix products, arithmetic and copies ran while one was open for 44% -> 44% of each run, Pallas kernels for 17% -> 16%
where the time goes in v5:
time: 981 us; the launch traced here: 971 us
  waiting for transfers between devices  293 us (30%)
  matrix products  234 us (24%)
  Pallas kernels  159 us (16%)
  local copies, waits for them, and re-layouts  106 us (11%)
  other arithmetic  105 us (11%)
  starting transfers between devices  47 us (5%)
  between operations  26.5 us (3%)
    ppermute x55, waiting for transfers between devices, swap_k(): return lax.ppermute(x, 'ctx', [(i, i ^ bit) for i in range(size)])  293 us
    dot_general x8, matrix products, dot_t(): lax.dot_general(a, b, (((1,), (1,)), ((), ())), preferred_element_type=F32)  89.5 us
    dot_general x10, matrix products, dot(): return jnp.dot(a, b, preferred_element_type=F32)  80.9 us
    pallas_call x1, Pallas kernels, gather_head(): pl.pallas_call(functools.partial(head_kernel, F, C), in_specs=[pl.BlockSp...  78.6 us
    dot_general x5, matrix products, t_dot(): lax.dot_general(a, b, (((0,), (0,)), ((), ())), preferred_element_type=F32)  63.6 us
    pallas_call x2, Pallas kernels, attend_backward(): pl.pallas_call(functools.partial(backward_kernel, scale), grid=(HEADS //...  44.9 us
    unnamed x243, local copies, waits for them, and re-layouts  44.9 us
    ppermute x55, starting transfers between devices, swap_k(): return lax.ppermute(x, 'ctx', [(i, i ^ bit) for i in range(size)])  42.8 us
  transfers between devices with their start and end apart: 65, of which 21 were waited for; matrix products, arithmetic and copies ran while one was open for 44% of the time, Pallas kernels for 16%

profile of v5, /device:TPU:1, one launch (start us, length us, event | category | flops | bytes accessed | tf_op | source)
XLA Modules:
  0.0 970.9 jit_solution(1476651348380174107)
XLA Ops:
  16.8 78.6 %gather_head.1 = (bf16[4,48,128]{2,1,0:T(8,128)(2,1)}, s32[8,4,256]{2,1,0:T(4,128)}, bf16[2048,256]{1,0:T(8,128)(2,1)}, bf16[2048,2048]{1,0:T(8,128)(2,1)}) custom-call(bf16[48,128]{1,0:T(8,128)(2,1)} %pad_bitcast_fusion.1.vec_ref, s32[4,256]{1,0:T(4,128)} %pad_add_fusion.2.place_ref, bf16[512,256]{1,0:T(8,128)(2,1)} %wkv_ref.1, bf16[512,2048]{1,0:T(8,128)(2,1)} %wq_ref.1), custom_call_target="tpu_custom_call" | custom-call | tf_op jit(solution)/shard_map/gather_head/pallas_call | solution.py:187
  109.3 9.9 %add_convert_fusion.6 = bf16[512,2048]{1,0:T(8,128)(2,1)} fusion(bf16[512,2048]{1,0:T(8,128)(2,1)} %add_convert_fusion.7, bf16[2048,2048]{1,0:T(8,128)(2,1)} %get-tuple-element.32, f32[2048]{0:T(1024)S(1)} %bitcast.315), kind=kOutput, calls=%fused_computation.65 | convolution fusion | flops 4297064448 | bytes 12591104 | tf_op jit(solution)/shard_map/dot_general | solution.py:48
  122.7 4.3 collective-permute-done.5
  139.8 18.0 %attend_forward.2 = (bf16[256,2048]{1,0:T(8,128)(2,1)S(1)}, f32[4,4,256]{2,1,0:T(4,128)S(1)}) custom-call(bf16[256,2048]{1,0:T(8,128)(2,1)S(1)} %slice.549.q_ref, bf16[2048,256]{1,0:T(8,128)(2,1)S(1)} %get-tuple-element.99.kv_ref, s32[2048,2]{1,0:T(8,128)S(1)} %copy.48.kplace_ref, s32[2,256]{1,0:T(2,128)S(1)} %get-tuple-element.138.qplace_ref), custom_call_target="tpu_custom_call" | custom-call | flops 8589934592 | bytes 2097152 | tf_op jit(solution)/shard_map/attend_forward/pallas_call | solution.py:284
  157.9 21.4 %collective-permute-done.14 = bf16[512,2048]{1,0:T(8,128)(2,1)} collective-permute-done((bf16[512,2048]{1,0:T(8,128)(2,1)}, bf16[512,2048]{1,0:T(8,128)(2,1)}, u32[]{:S(2)}, u32[]{:S(2)}) %collective-permute-start.14) | collective-permute-done | bytes 2097184 | tf_op jit(solution)/shard_map/ppermute | solution.py:64
  189.4 17.7 %attend_forward.3 = (bf16[256,2048]{1,0:T(8,128)(2,1)S(1)}, f32[4,4,256]{2,1,0:T(4,128)S(1)}) custom-call(bf16[256,2048]{1,0:T(8,128)(2,1)S(1)} %add_convert_fusion.13.q_ref, bf16[2048,256]{1,0:T(8,128)(2,1)S(1)} %get-tuple-element.98.kv_ref, s32[2048,2]{1,0:T(8,128)S(1)} %copy.49.kplace_ref, s32[2,256]{1,0:T(2,128)S(1)} %get-tuple-element.139.qplace_ref), custom_call_target="tpu_custom_call" | custom-call | flops 8589934592 | bytes 2097152 | tf_op jit(solution)/shard_map/attend_forward/pallas_call | solution.py:284
  220.5 18.4 %collective-permute-done.9 = bf16[256,2048]{1,0:T(8,128)(2,1)S(1)} collective-permute-done((bf16[256,2048]{1,0:T(8,128)(2,1)S(1)}, bf16[256,2048]{1,0:T(8,128)(2,1)S(1)}, u32[]{:S(2)}, u32[]{:S(2)}) %collective-permute-start.9) | collective-permute-done | bytes 1048608 | tf_op jit(solution)/shard_map/ppermute | solution.py:64
  246.4 28.9 %multiply_convert_fusion.1 = (bf16[2048,2048]{1,0:T(8,128)(2,1)S(1)}, f32[2048,2048]{1,0:T(8,128)}) fusion(f32[2048]{0:T(1024)S(1)} %bitcast.313, bf16[2048,2048]{1,0:T(8,128)(2,1)} %constant_dynamic-update-slice_fusion.8, bf16[2048,2048]{1,0:T(8,128)(2,1)} %all-gather.6.cloned.1.call-done), kind=kOutput, calls=%fused_computation.10 | convolution fusion | flops 17221812224 | bytes 41951232 | tf_op jit(solution)/shard_map/dot_general | solution.py:48
  278.6 20.6 %convolution_convert_fusion.1 = bf16[2048,2048]{1,0:T(8,128)(2,1)} fusion(bf16[2048,2048]{1,0:T(8,128)(2,1)S(1)} %get-tuple-element.39, bf16[2048,2048]{1,0:T(8,128)(2,1)S(1)} %copy-done.62), kind=kOutput, calls=%fused_computation.13 | convolution fusion | flops 17184063488 | bytes 25165824 | tf_op jit(solution)/shard_map/dot_general | solution.py:56
  299.3 35.4 %convert_reduce_fusion = (f32[2048]{0:T(1024)}, bf16[2048,2048]{1,0:T(8,128)(2,1)}) fusion(f32[2048,2048]{1,0:T(8,128)} %get-tuple-element.134, f32[2048]{0:T(1024)S(1)} %bitcast.314, bf16[2048,2048]{1,0:T(8,128)(2,1)} %copy-done.61, bf16[2048,2048]{1,0:T(8,128)(2,1)} %all-gather.8.cloned.1.call-done), kind=kOutput, calls=%fused_computation.8 | convolution fusion | flops 17280530432 | bytes 41959424 | tf_op jit(solution)/shard_map/dot_general | solution.py:52
  334.7 13.0 %fusion.30 = bf16[1024,2048]{1,0:T(8,128)(2,1)S(1)} fusion(bf16[2048,2048]{1,0:T(8,128)(2,1)} %all-gather.6.cloned.1.call-done, bf16[2048,2048]{1,0:T(8,128)(2,1)} %get-tuple-element.137), kind=kOutput, calls=%fused_computation.71 | convolution fusion | flops 8592031744 | bytes 16777216 | tf_op jit(solution)/shard_map/dot_general | solution.py:52
  347.8 7.1 collective-permute-done.17
  356.1 11.7 %fusion.12 = bf16[512,2048]{1,0:T(8,128)(2,1)S(1)} fusion(f32[1024,2048]{1,0:T(8,128)S(1)} %convert_element_type.452, bf16[2048,2048]{1,0:T(8,128)(2,1)} %all-gather.6.cloned.1.call-done, bf16[2048,2048]{1,0:T(8,128)(2,1)} %get-tuple-element.137), kind=kOutput, calls=%fused_computation.31 | convolution fusion | flops 4297064448 | bytes 16777216 | tf_op jit(solution)/shard_map/dot_general | solution.py:52
  369.9 24.1 %convolution_convert_fusion = bf16[2048,2048]{1,0:T(8,128)(2,1)} fusion(bf16[2048,2048]{1,0:T(8,128)(2,1)} %constant_dynamic-update-slice_fusion.8, bf16[2048,2048]{1,0:T(8,128)(2,1)} %get-tuple-element.137), kind=kOutput, calls=%fused_computation.12 | convolution fusion | flops 17184063488 | bytes 25165824 | tf_op jit(solution)/shard_map/dot_general | solution.py:56
  394.0 14.1 %fusion.27 = bf16[1024,2048]{1,0:T(8,128)(2,1)} fusion(bf16[2048,2048]{1,0:T(8,128)(2,1)} %all-gather.8.cloned.1.call-done, bf16[2048,2048]{1,0:T(8,128)(2,1)} %copy-done.92), kind=kOutput, calls=%fused_computation.70 | convolution fusion | flops 8592031744 | bytes 16777216 | tf_op jit(solution)/shard_map/dot_general | solution.py:48
  409.8 6.0 collective-permute-done.19
  415.8 4.1 convert_element_type.457
  419.9 7.8 slice_add_fusion.2
  427.7 8.0 fusion.11
  442.6 10.6 %multiply_reduce_fusion = (f32[2048]{0:T(1024)S(1)}, f32[512]{0:T(512)S(1)}, f32[512]{0:T(512)S(1)}, f32[2048]{0:T(1024)S(1)}, f32[512,2048]{1,0:T(8,128)S(1)}) fusion(f32[512]{0:T(512)S(1)} %add_rsqrt_fusion, f32[512]{0:T(512)S(1)} %broadcast_multiply_fusion.4, f32[]{:T(128)} %bitcast.14, f32[256,2048]{1,0:T(8,128)} %copy-done.25, ...), kind=kOutput, calls=%fused_computation.51 | convolution fusion | flops 4312787968 | bytes 25199104 | tf_op jit(solution)/shard_map/dot_general | solution.py:52
  453.2 12.7 %collective-permute-done.22 = bf16[128,2048]{1,0:T(8,128)(2,1)S(1)} collective-permute-done((bf16[128,2048]{1,0:T(8,128)(2,1)S(1)}, bf16[128,2048]{1,0:T(8,128)(2,1)S(1)}, u32[]{:S(2)}, u32[]{:S(2)}) %collective-permute-start.22) | collective-permute-done | bytes 524320 | tf_op jit(solution)/shard_map/ppermute | solution.py:64
  467.5 6.0 convert_reduce_fusion.2
  475.9 4.9 add_convert_fusion.4
  480.8 11.6 %collective-permute-done.23 = bf16[128,2048]{1,0:T(8,128)(2,1)S(1)} collective-permute-done((bf16[128,2048]{1,0:T(8,128)(2,1)S(1)}, bf16[128,2048]{1,0:T(8,128)(2,1)S(1)}, u32[]{:S(2)}, u32[]{:S(2)}) %collective-permute-start.23) | collective-permute-done | bytes 524320 | tf_op jit(solution)/shard_map/ppermute | solution.py:64
  494.2 22.4 %attend_backward.2 = (bf16[256,2048]{1,0:T(8,128)(2,1)S(1)}, f32[2048,256]{1,0:T(8,128)S(1)}) custom-call(bf16[256,2048]{1,0:T(8,128)(2,1)S(1)} %copy-done.7, bf16[256,2048]{1,0:T(8,128)(2,1)S(1)} %add_convert_fusion.11.do_ref, bf16[256,2048]{1,0:T(8,128)(2,1)S(1)} %copy-done.9, f32[4,4,256]{2,1,0:T(4,128)S(1)} %get-tuple-element.40.lse_ref, ...), custom_call_target="tpu_custom_call" | custom-call | flops 19327352832 | bytes 4194304 | tf_op jit(solution)/shard_map/attend_backward/pallas_call | solution.py:313
  529.7 22.5 %attend_backward.3 = (bf16[256,2048]{1,0:T(8,128)(2,1)S(1)}, f32[2048,256]{1,0:T(8,128)S(1)}) custom-call(bf16[256,2048]{1,0:T(8,128)(2,1)S(1)} %copy-done.3, bf16[256,2048]{1,0:T(8,128)(2,1)S(1)} %add_convert_fusion.10.do_ref, bf16[256,2048]{1,0:T(8,128)(2,1)S(1)} %copy-done.12, f32[4,4,256]{2,1,0:T(4,128)S(1)} %get-tuple-element.42.lse_ref, ...), custom_call_target="tpu_custom_call" | custom-call | flops 19327352832 | bytes 4194304 | tf_op jit(solution)/shard_map/attend_backward/pallas_call | solution.py:313
  560.8 8.3 convolution_convert_fusion.2
  576.0 6.9 fusion.24
  594.4 19.2 %collective-permute-done.31 = bf16[2,2,256,256]{3,2,1,0:T(8,128)(2,1)S(1)} collective-permute-done((bf16[2,2,256,256]{3,2,1,0:T(8,128)(2,1)S(1)}, bf16[2,2,256,256]{3,2,1,0:T(8,128)(2,1)S(1)}, u32[]{:S(2)}, u32[]{:S(2)}) %collective-permute-start.31) | collective-permute-done | bytes 524320 | tf_op jit(solution)/shard_map/ppermute | solution.py:64
  626.4 9.4 fusion.110
  643.5 8.5 broadcast.148
  652.1 3.9 convert_dynamic-update-slice_fusion.3
  674.9 94.0 %collective-permute-done.35 = bf16[256,1024]{1,0:T(8,128)(2,1)S(1)} collective-permute-done((bf16[256,1024]{1,0:T(8,128)(2,1)S(1)}, bf16[256,1024]{1,0:T(8,128)(2,1)S(1)}, u32[]{:S(2)}, u32[]{:S(2)}) %collective-permute-start.35) | collective-permute-done | bytes 524320 | tf_op jit(solution)/shard_map/ppermute | solution.py:64
  770.7 4.0 add_convert_fusion.3
  775.9 9.6 collective-permute-done.36
  788.0 4.5 broadcast_in_dim.76
  792.5 3.9 bitcast_dynamic-update-slice_fusion.3
  798.8 4.1 convert_dynamic-update-slice_fusion.2
  803.0 43.9 %collective-permute-done.44 = bf16[128,1024]{1,0:T(8,128)(2,1)S(1)} collective-permute-done((bf16[128,1024]{1,0:T(8,128)(2,1)}, bf16[128,1024]{1,0:T(8,128)(2,1)S(1)}, u32[]{:S(2)}, u32[]{:S(2)}) %collective-permute-start.44) | collective-permute-done | bytes 262176 | tf_op jit(solution)/shard_map/ppermute | solution.py:64
  849.9 4.1 convert_dynamic-update-slice_fusion.1
  855.5 5.6 collective-permute-done.45
  869.0 4.1 convert_dynamic-update-slice_fusion
  873.8 4.4 fusion.51
  888.9 4.5 collective-permute-done.43
  898.9 12.6 %collective-permute-done.49 = bf16[128,1152]{1,0:T(8,128)(2,1)S(1)} collective-permute-done((bf16[128,1152]{1,0:T(8,128)(2,1)S(1)}, bf16[128,1152]{1,0:T(8,128)(2,1)S(1)}, u32[]{:S(2)}, u32[]{:S(2)}) %collective-permute-start.49) | collective-permute-done | bytes 294944 | tf_op jit(solution)/shard_map/ppermute | solution.py:64
  914.9 4.0 slice_bitcast_fusion
  930.2 11.6 %collective-permute-done.51 = bf16[256,1152]{1,0:T(8,128)(2,1)S(1)} collective-permute-done((bf16[256,1152]{1,0:T(8,128)(2,1)S(1)}, bf16[256,1152]{1,0:T(8,128)(2,1)S(1)}, u32[]{:S(2)}, u32[]{:S(2)}) %collective-permute-start.51) | collective-permute-done | bytes 589856 | tf_op jit(solution)/shard_map/ppermute | solution.py:64
  948.2 11.7 %convert_element_type.558 = f32[512,8192]{1,0:T(8,128)} convert(bf16[512,8192]{1,0:T(8,128)(2,1)} %slice_dynamic-update-slice_fusion) | non-fusion elementwise | flops 4194304 | bytes 25165824 | tf_op jit(solution)/shard_map/convert_element_type | solution.py:639
  (530 shorter events, 222.0 us)
Async XLA Ops:
  7.2 101.1 %all-gather.4.cloned.1.call-start = ((), (), s32[]{:S(2)}) async-start(), calls=%async_computation.4 | async-start | bytes 5242880 | tf_op jit(solution)/shard_map/all_gather | solution.py:443
  9.9 236.5 %all-gather.6.cloned.1.call-start = ((), (), s32[]{:S(2)}) async-start(), calls=%async_computation.5 | async-start | bytes 10485760 | tf_op jit(solution)/shard_map/all_gather | solution.py:454
  13.4 285.9 %all-gather.8.cloned.1.call-start = ((), (), s32[]{:S(2)}) async-start(), calls=%async_computation.6 | async-start | bytes 10485760 | tf_op jit(solution)/shard_map/all_gather | solution.py:455
  102.8 18.4 %collective-permute-start = (bf16[2,256,256]{2,1,0:T(8,128)(2,1)S(1)}, bf16[2,256,256]{2,1,0:T(8,128)(2,1)S(1)}, u32[]{:S(2)}, u32[]{:S(2)}) collective-permute-start(bf16[2,256,256]{2,1,0:T(8,128)(2,1)S(1)} %bitcast.280), channel_id=1, source_target_pairs={{0,1},{1,0},{2,3},{3,2},{4,5},{5,4},{6,7},{7,6},{8,9},{9,8},{10,11... | collective-permute-start | bytes 786440 | tf_op jit(solution)/shard_map/ppermute | solution.py:64
  103.0 16.3 %collective-permute-start.1 = (bf16[2,256,256]{2,1,0:T(8,128)(2,1)S(1)}, bf16[2,256,256]{2,1,0:T(8,128)(2,1)S(1)}, u32[]{:S(2)}, u32[]{:S(2)}) collective-permute-start(bf16[2,256,256]{2,1,0:T(8,128)(2,1)S(1)} %bitcast.281), channel_id=1, source_target_pairs={{0,2},{1,3},{2,0},{3,1},{4,6},{5,7},{6,4},{7,5},{8,10},{9,11},{10,... | collective-permute-start | bytes 786440 | tf_op jit(solution)/shard_map/ppermute | solution.py:64
  104.3 15.0 %collective-permute-start.3 = (bf16[2,256,256]{2,1,0:T(8,128)(2,1)S(1)}, bf16[2,256,256]{2,1,0:T(8,128)(2,1)S(1)}, u32[]{:S(2)}, u32[]{:S(2)}) collective-permute-start(bf16[2,256,256]{2,1,0:T(8,128)(2,1)S(1)} %bitcast.282), channel_id=1, source_target_pairs={{0,4},{1,5},{2,6},{3,7},{4,0},{5,1},{6,2},{7,3},{8,12},{9,13},{10,... | collective-permute-start | bytes 786440 | tf_op jit(solution)/shard_map/ppermute | solution.py:64
  108.2 331.1 %reduce-scatter.5.cloned.1.call-start = ((), (), s32[]{:S(2)}) async-start(), calls=%async_computation.7 | async-start | bytes 10485760 | tf_op jit(solution)/shard_map/reduce_scatter | solution.py:504
  108.3 73.1 %collective-permute-start.7 = (bf16[2048,1024]{1,0:T(8,128)(2,1)}, bf16[2048,1024]{1,0:T(8,128)(2,1)}, u32[]{:S(2)}, u32[]{:S(2)}) collective-permute-start(bf16[2048,1024]{1,0:T(8,128)(2,1)} %all-gather.4.cloned.1.call-done), channel_id=1, source_target_pairs={{0,1},{1,0},{2,3},{3,2},{4,5},{5,4},{6,7},{7,6},{8,9},{9,8},{10,11... | collective-permute-start | bytes 12582920 | tf_op jit(solution)/shard_map/ppermute | solution.py:64
  131.7 47.6 %collective-permute-start.14 = (bf16[512,2048]{1,0:T(8,128)(2,1)}, bf16[512,2048]{1,0:T(8,128)(2,1)}, u32[]{:S(2)}, u32[]{:S(2)}) collective-permute-start(bf16[512,2048]{1,0:T(8,128)(2,1)} %bitcast.13), channel_id=1, source_target_pairs={{0,2},{1,3},{2,0},{3,1},{4,6},{5,7},{6,4},{7,5},{8,10},{9,11},{10,... | collective-permute-start | bytes 6291464 | tf_op jit(solution)/shard_map/ppermute | solution.py:64
  137.0 82.4 %collective-permute-start.15 = (bf16[512,2048]{1,0:T(8,128)(2,1)}, bf16[512,2048]{1,0:T(8,128)(2,1)S(1)}, u32[]{:S(2)}, u32[]{:S(2)}) collective-permute-start(bf16[512,2048]{1,0:T(8,128)(2,1)} %bitcast.13), channel_id=1, source_target_pairs={{0,1},{1,0},{2,3},{3,2},{4,5},{5,4},{6,7},{7,6},{8,9},{9,8},{10,11... | collective-permute-start | bytes 6291464 | tf_op jit(solution)/shard_map/ppermute | solution.py:64
  179.3 40.9 %collective-permute-start.16 = (bf16[512,2048]{1,0:T(8,128)(2,1)}, bf16[512,2048]{1,0:T(8,128)(2,1)S(1)}, u32[]{:S(2)}, u32[]{:S(2)}) collective-permute-start(bf16[512,2048]{1,0:T(8,128)(2,1)} %collective-permute-done.14), channel_id=1, source_target_pairs={{0,1},{1,0},{2,3},{3,2},{4,5},{5,4},{6,7},{7,6},{8,9},{9,8},{10,11... | collective-permute-start | bytes 6291464 | tf_op jit(solution)/shard_map/ppermute | solution.py:64
  188.0 31.7 %collective-permute-start.8 = (bf16[256,2048]{1,0:T(8,128)(2,1)S(1)}, bf16[256,2048]{1,0:T(8,128)(2,1)S(1)}, u32[]{:S(2)}, u32[]{:S(2)}) collective-permute-start(bf16[256,2048]{1,0:T(8,128)(2,1)S(1)} %get-tuple-element.71), channel_id=1, source_target_pairs={{0,2},{1,3},{2,0},{3,1},{4,6},{5,7},{6,4},{7,5},{8,10},{9,11},{10,... | collective-permute-start | bytes 3145736 | tf_op jit(solution)/shard_map/ppermute | solution.py:64
  214.3 24.6 %collective-permute-start.9 = (bf16[256,2048]{1,0:T(8,128)(2,1)S(1)}, bf16[256,2048]{1,0:T(8,128)(2,1)S(1)}, u32[]{:S(2)}, u32[]{:S(2)}) collective-permute-start(bf16[256,2048]{1,0:T(8,128)(2,1)S(1)} %get-tuple-element.67), channel_id=1, source_target_pairs={{0,2},{1,3},{2,0},{3,1},{4,6},{5,7},{6,4},{7,5},{8,10},{9,11},{10,... | collective-permute-start | bytes 3145736 | tf_op jit(solution)/shard_map/ppermute | solution.py:64
  218.8 23.3 %collective-permute-start.10 = (bf16[256,2048]{1,0:T(8,128)(2,1)S(1)}, bf16[256,2048]{1,0:T(8,128)(2,1)S(1)}, u32[]{:S(2)}, u32[]{:S(2)}) collective-permute-start(bf16[256,2048]{1,0:T(8,128)(2,1)S(1)} %get-tuple-element.71), channel_id=1, source_target_pairs={{0,1},{1,0},{2,3},{3,2},{4,5},{5,4},{6,7},{7,6},{8,9},{9,8},{10,11... | collective-permute-start | bytes 3145736 | tf_op jit(solution)/shard_map/ppermute | solution.py:64
  219.4 23.8 %collective-permute-start.11 = (bf16[256,2048]{1,0:T(8,128)(2,1)S(1)}, bf16[256,2048]{1,0:T(8,128)(2,1)S(1)}, u32[]{:S(2)}, u32[]{:S(2)}) collective-permute-start(bf16[256,2048]{1,0:T(8,128)(2,1)S(1)} %get-tuple-element.67), channel_id=1, source_target_pairs={{0,1},{1,0},{2,3},{3,2},{4,5},{5,4},{6,7},{7,6},{8,9},{9,8},{10,11... | collective-permute-start | bytes 3145736 | tf_op jit(solution)/shard_map/ppermute | solution.py:64
  219.7 24.5 %collective-permute-start.12 = (bf16[256,2048]{1,0:T(8,128)(2,1)S(1)}, bf16[256,2048]{1,0:T(8,128)(2,1)S(1)}, u32[]{:S(2)}, u32[]{:S(2)}) collective-permute-start(bf16[256,2048]{1,0:T(8,128)(2,1)S(1)} %collective-permute-done.8), channel_id=1, source_target_pairs={{0,1},{1,0},{2,3},{3,2},{4,5},{5,4},{6,7},{7,6},{8,9},{9,8},{10,11... | collective-permute-start | bytes 3145736 | tf_op jit(solution)/shard_map/ppermute | solution.py:64
  299.2 365.5 %reduce-scatter.7.cloned.1.call-start = ((), (), s32[]{:S(2)}) async-start(), calls=%async_computation.8 | async-start | bytes 10485760 | tf_op jit(solution)/shard_map/reduce_scatter | solution.py:504
  368.9 25.1 %collective-permute-start.18 = (bf16[256,2048]{1,0:T(8,128)(2,1)S(1)}, bf16[256,2048]{1,0:T(8,128)(2,1)S(1)}, u32[]{:S(2)}, u32[]{:S(2)}) collective-permute-start(bf16[256,2048]{1,0:T(8,128)(2,1)S(1)} %get-tuple-element.97), channel_id=1, source_target_pairs={{0,2},{1,3},{2,0},{3,1},{4,6},{5,7},{6,4},{7,5},{8,10},{9,11},{10,... | collective-permute-start | bytes 3145736 | tf_op jit(solution)/shard_map/ppermute | solution.py:64
  408.6 151.5 %collective-permute-start.26 = (bf16[512,2048]{1,0:T(8,128)(2,1)}, bf16[512,2048]{1,0:T(8,128)(2,1)}, u32[]{:S(2)}, u32[]{:S(2)}) collective-permute-start(bf16[512,2048]{1,0:T(8,128)(2,1)} %add_convert_fusion.7), channel_id=1, source_target_pairs={{0,1},{1,0},{2,3},{3,2},{4,5},{5,4},{6,7},{7,6},{8,9},{9,8},{10,11... | collective-permute-start | bytes 6291464 | tf_op jit(solution)/shard_map/ppermute | solution.py:64
  408.7 33.9 %collective-permute-start.21 = (bf16[256,2048]{1,0:T(8,128)(2,1)}, bf16[256,2048]{1,0:T(8,128)(2,1)}, u32[]{:S(2)}, u32[]{:S(2)}) collective-permute-start(bf16[256,2048]{1,0:T(8,128)(2,1)} %get-tuple-element.96), channel_id=1, source_target_pairs={{0,2},{1,3},{2,0},{3,1},{4,6},{5,7},{6,4},{7,5},{8,10},{9,11},{10,... | collective-permute-start | bytes 3145736 | tf_op jit(solution)/shard_map/ppermute | solution.py:64
  409.8 259.6 %reduce-scatter.9.cloned.1.call-start = ((), (), s32[]{:S(2)}) async-start(), calls=%async_computation.9 | async-start | bytes 5242880 | tf_op jit(solution)/shard_map/reduce_scatter | solution.py:500
  440.5 25.5 %collective-permute-start.22 = (bf16[128,2048]{1,0:T(8,128)(2,1)S(1)}, bf16[128,2048]{1,0:T(8,128)(2,1)S(1)}, u32[]{:S(2)}, u32[]{:S(2)}) collective-permute-start(bf16[128,2048]{1,0:T(8,128)(2,1)S(1)} %slice.572), channel_id=1, source_target_pairs={{0,4},{1,5},{2,6},{3,7},{4,0},{5,1},{6,2},{7,3},{8,12},{9,13},{10,... | collective-permute-start | bytes 1572872 | tf_op jit(solution)/shard_map/ppermute | solution.py:64
  467.4 25.0 %collective-permute-start.23 = (bf16[128,2048]{1,0:T(8,128)(2,1)S(1)}, bf16[128,2048]{1,0:T(8,128)(2,1)S(1)}, u32[]{:S(2)}, u32[]{:S(2)}) collective-permute-start(bf16[128,2048]{1,0:T(8,128)(2,1)S(1)} %add_convert_fusion.20), channel_id=1, source_target_pairs={{0,4},{1,5},{2,6},{3,7},{4,0},{5,1},{6,2},{7,3},{8,12},{9,13},{10,... | collective-permute-start | bytes 1572872 | tf_op jit(solution)/shard_map/ppermute | solution.py:64
  493.9 25.6 %collective-permute-start.24 = (bf16[128,2048]{1,0:T(8,128)(2,1)S(1)}, bf16[128,2048]{1,0:T(8,128)(2,1)S(1)}, u32[]{:S(2)}, u32[]{:S(2)}) collective-permute-start(bf16[128,2048]{1,0:T(8,128)(2,1)S(1)} %add_convert_fusion.18), channel_id=1, source_target_pairs={{0,4},{1,5},{2,6},{3,7},{4,0},{5,1},{6,2},{7,3},{8,12},{9,13},{10,... | collective-permute-start | bytes 1572872 | tf_op jit(solution)/shard_map/ppermute | solution.py:64
  522.8 29.6 %collective-permute-start.27 = (bf16[128,2048]{1,0:T(8,128)(2,1)S(1)}, bf16[128,2048]{1,0:T(8,128)(2,1)S(1)}, u32[]{:S(2)}, u32[]{:S(2)}) collective-permute-start(bf16[128,2048]{1,0:T(8,128)(2,1)S(1)} %add_convert_fusion.16), channel_id=1, source_target_pairs={{0,4},{1,5},{2,6},{3,7},{4,0},{5,1},{6,2},{7,3},{8,12},{9,13},{10,... | collective-permute-start | bytes 1572872 | tf_op jit(solution)/shard_map/ppermute | solution.py:64
  560.0 13.7 %collective-permute-start.25 = (bf16[512,2048]{1,0:T(8,128)(2,1)}, bf16[512,2048]{1,0:T(8,128)(2,1)}, u32[]{:S(2)}, u32[]{:S(2)}) collective-permute-start(bf16[512,2048]{1,0:T(8,128)(2,1)} %pad_maximum_fusion.8), channel_id=1, source_target_pairs={{0,1},{1,0},{2,3},{3,2},{4,5},{5,4},{6,7},{7,6},{8,9},{9,8},{10,11... | collective-permute-start | bytes 6291464 | tf_op jit(solution)/shard_map/ppermute | solution.py:64
  571.0 308.7 %reduce-scatter.11.cloned.1.call-start = ((), (), s32[]{:S(2)}) async-start(), calls=%async_computation.10 | async-start | bytes 5898240 | tf_op jit(solution)/shard_map/reduce_scatter | solution.py:500
  589.5 24.0 %collective-permute-start.31 = (bf16[2,2,256,256]{3,2,1,0:T(8,128)(2,1)S(1)}, bf16[2,2,256,256]{3,2,1,0:T(8,128)(2,1)S(1)}, u32[]{:S(2)}, u32[]{:S(2)}) collective-permute-start(bf16[2,2,256,256]{3,2,1,0:T(8,128)(2,1)S(1)} %pad_maximum_fusion.12), channel_id=1, source_target_pairs={{0,4},{1,5},{2,6},{3,7},{4,0},{5,1},{6,2},{7,3},{8,12},{9,13},{10,... | collective-permute-start | bytes 1572872 | tf_op jit(solution)/shard_map/ppermute | solution.py:64
  617.0 53.7 %collective-permute-start.33 = (bf16[256,2048]{1,0:T(8,128)(2,1)}, bf16[256,2048]{1,0:T(8,128)(2,1)}, u32[]{:S(2)}, u32[]{:S(2)}) collective-permute-start(bf16[256,2048]{1,0:T(8,128)(2,1)} %get-tuple-element.87), channel_id=1, source_target_pairs={{0,2},{1,3},{2,0},{3,1},{4,6},{5,7},{6,4},{7,5},{8,10},{9,11},{10,... | collective-permute-start | bytes 3145736 | tf_op jit(solution)/shard_map/ppermute | solution.py:64
  618.4 55.1 %collective-permute-start.20 = (bf16[256,2048]{1,0:T(8,128)(2,1)}, bf16[256,2048]{1,0:T(8,128)(2,1)}, u32[]{:S(2)}, u32[]{:S(2)}) collective-permute-start(bf16[256,2048]{1,0:T(8,128)(2,1)} %get-tuple-element.86), channel_id=1, source_target_pairs={{0,2},{1,3},{2,0},{3,1},{4,6},{5,7},{6,4},{7,5},{8,10},{9,11},{10,... | collective-permute-start | bytes 3145736 | tf_op jit(solution)/shard_map/ppermute | solution.py:64
  624.1 12.9 %collective-permute-start.47 = (bf16[512,128]{1,0:T(8,128)(2,1)S(1)}, bf16[512,128]{1,0:T(8,128)(2,1)S(1)}, u32[]{:S(2)}, u32[]{:S(2)}) collective-permute-start(bf16[512,128]{1,0:T(8,128)(2,1)S(1)} %get-tuple-element.105), channel_id=1, source_target_pairs={{0,1},{1,0},{2,3},{3,2},{4,5},{5,4},{6,7},{7,6},{8,9},{9,8},{10,11... | collective-permute-start | bytes 393224 | tf_op jit(solution)/shard_map/ppermute | solution.py:64
  655.9 140.6 %collective-permute-start.55 = (bf16[512,2048]{1,0:T(8,128)(2,1)}, bf16[512,2048]{1,0:T(8,128)(2,1)}, u32[]{:S(2)}, u32[]{:S(2)}) collective-permute-start(bf16[512,2048]{1,0:T(8,128)(2,1)} %get-tuple-element.55), channel_id=1, source_target_pairs={{0,2},{1,3},{2,0},{3,1},{4,6},{5,7},{6,4},{7,5},{8,10},{9,11},{10,... | collective-permute-start | bytes 6291464 | tf_op jit(solution)/shard_map/ppermute | solution.py:64
  655.9 194.0 %collective-permute-start.56 = (bf16[512,2048]{1,0:T(8,128)(2,1)}, bf16[512,2048]{1,0:T(8,128)(2,1)}, u32[]{:S(2)}, u32[]{:S(2)}) collective-permute-start(bf16[512,2048]{1,0:T(8,128)(2,1)} %get-tuple-element.55), channel_id=1, source_target_pairs={{0,1},{1,0},{2,3},{3,2},{4,5},{5,4},{6,7},{7,6},{8,9},{9,8},{10,11... | collective-permute-start | bytes 6291464 | tf_op jit(solution)/shard_map/ppermute | solution.py:64
  668.2 119.8 %collective-permute-start.34 = (bf16[512,2048]{1,0:T(8,128)(2,1)}, bf16[512,2048]{1,0:T(8,128)(2,1)}, u32[]{:S(2)}, u32[]{:S(2)}) collective-permute-start(bf16[512,2048]{1,0:T(8,128)(2,1)} %fusion.9), channel_id=1, source_target_pairs={{0,4},{1,5},{2,6},{3,7},{4,0},{5,1},{6,2},{7,3},{8,12},{9,13},{10,... | collective-permute-start | bytes 6291464 | tf_op jit(solution)/shard_map/ppermute | solution.py:64
  670.6 98.3 %collective-permute-start.35 = (bf16[256,1024]{1,0:T(8,128)(2,1)S(1)}, bf16[256,1024]{1,0:T(8,128)(2,1)S(1)}, u32[]{:S(2)}, u32[]{:S(2)}) collective-permute-start(bf16[256,1024]{1,0:T(8,128)(2,1)S(1)} %pad_maximum_fusion.13), channel_id=1, source_target_pairs={{0,2},{1,3},{2,0},{3,1},{4,6},{5,7},{6,4},{7,5},{8,10},{9,11},{10,... | collective-permute-start | bytes 1572872 | tf_op jit(solution)/shard_map/ppermute | solution.py:64
  770.5 15.0 %collective-permute-start.36 = (bf16[128,1024]{1,0:T(8,128)(2,1)}, bf16[128,1024]{1,0:T(8,128)(2,1)}, u32[]{:S(2)}, u32[]{:S(2)}) collective-permute-start(bf16[128,1024]{1,0:T(8,128)(2,1)} %fusion.75), channel_id=1, source_target_pairs={{0,4},{1,5},{2,6},{3,7},{4,0},{5,1},{6,2},{7,3},{8,12},{9,13},{10,... | collective-permute-start | bytes 786440 | tf_op jit(solution)/shard_map/ppermute | solution.py:64
  796.4 66.5 %collective-permute-start.37 = (bf16[512,2048]{1,0:T(8,128)(2,1)S(1)}, bf16[512,2048]{1,0:T(8,128)(2,1)}, u32[]{:S(2)}, u32[]{:S(2)}) collective-permute-start(bf16[512,2048]{1,0:T(8,128)(2,1)S(1)} %get-tuple-element.57), channel_id=1, source_target_pairs={{0,2},{1,3},{2,0},{3,1},{4,6},{5,7},{6,4},{7,5},{8,10},{9,11},{10,... | collective-permute-start | bytes 6291464 | tf_op jit(solution)/shard_map/ppermute | solution.py:64
  796.6 72.0 %collective-permute-start.57 = (bf16[512,2048]{1,0:T(8,128)(2,1)}, bf16[512,2048]{1,0:T(8,128)(2,1)}, u32[]{:S(2)}, u32[]{:S(2)}) collective-permute-start(bf16[512,2048]{1,0:T(8,128)(2,1)} %collective-permute-done.55), channel_id=1, source_target_pairs={{0,1},{1,0},{2,3},{3,2},{4,5},{5,4},{6,7},{7,6},{8,9},{9,8},{10,11... | collective-permute-start | bytes 6291464 | tf_op jit(solution)/shard_map/ppermute | solution.py:64
  797.2 49.7 %collective-permute-start.44 = (bf16[128,1024]{1,0:T(8,128)(2,1)}, bf16[128,1024]{1,0:T(8,128)(2,1)S(1)}, u32[]{:S(2)}, u32[]{:S(2)}) collective-permute-start(bf16[128,1024]{1,0:T(8,128)(2,1)} %copy-done.59), channel_id=1, source_target_pairs={{0,4},{1,5},{2,6},{3,7},{4,0},{5,1},{6,2},{7,3},{8,12},{9,13},{10,... | collective-permute-start | bytes 786440 | tf_op jit(solution)/shard_map/ppermute | solution.py:64
  847.8 13.2 %collective-permute-start.45 = (bf16[256,1024]{1,0:T(8,128)(2,1)S(1)}, bf16[256,1024]{1,0:T(8,128)(2,1)S(1)}, u32[]{:S(2)}, u32[]{:S(2)}) collective-permute-start(bf16[256,1024]{1,0:T(8,128)(2,1)S(1)} %pad_maximum_fusion.14), channel_id=1, source_target_pairs={{0,2},{1,3},{2,0},{3,1},{4,6},{5,7},{6,4},{7,5},{8,10},{9,11},{10,... | collective-permute-start | bytes 1572872 | tf_op jit(solution)/shard_map/ppermute | solution.py:64
  854.0 31.7 %collective-permute-start.53 = (bf16[512,2048]{1,0:T(8,128)(2,1)S(1)}, bf16[512,2048]{1,0:T(8,128)(2,1)}, u32[]{:S(2)}, u32[]{:S(2)}) collective-permute-start(bf16[512,2048]{1,0:T(8,128)(2,1)S(1)} %get-tuple-element.57), channel_id=1, source_target_pairs={{0,1},{1,0},{2,3},{3,2},{4,5},{5,4},{6,7},{7,6},{8,9},{9,8},{10,11... | collective-permute-start | bytes 6291464 | tf_op jit(solution)/shard_map/ppermute | solution.py:64
  861.1 12.7 %collective-permute-start.46 = (bf16[512,1024]{1,0:T(8,128)(2,1)S(1)}, bf16[512,1024]{1,0:T(8,128)(2,1)}, u32[]{:S(2)}, u32[]{:S(2)}) collective-permute-start(bf16[512,1024]{1,0:T(8,128)(2,1)S(1)} %bitcast.264), channel_id=1, source_target_pairs={{0,1},{1,0},{2,3},{3,2},{4,5},{5,4},{6,7},{7,6},{8,9},{9,8},{10,11... | collective-permute-start | bytes 3145736 | tf_op jit(solution)/shard_map/ppermute | solution.py:64
  878.2 33.6 %collective-permute-start.54 = (bf16[512,2048]{1,0:T(8,128)(2,1)}, bf16[512,2048]{1,0:T(8,128)(2,1)}, u32[]{:S(2)}, u32[]{:S(2)}) collective-permute-start(bf16[512,2048]{1,0:T(8,128)(2,1)} %collective-permute-done.37), channel_id=1, source_target_pairs={{0,1},{1,0},{2,3},{3,2},{4,5},{5,4},{6,7},{7,6},{8,9},{9,8},{10,11... | collective-permute-start | bytes 6291464 | tf_op jit(solution)/shard_map/ppermute | solution.py:64
  880.9 14.7 %collective-permute-start.48 = (bf16[256,1152]{1,0:T(8,128)(2,1)S(1)}, bf16[256,1152]{1,0:T(8,128)(2,1)S(1)}, u32[]{:S(2)}, u32[]{:S(2)}) collective-permute-start(bf16[256,1152]{1,0:T(8,128)(2,1)S(1)} %pad_maximum_fusion.10), channel_id=1, source_target_pairs={{0,2},{1,3},{2,0},{3,1},{4,6},{5,7},{6,4},{7,5},{8,10},{9,11},{10,... | collective-permute-start | bytes 1769480 | tf_op jit(solution)/shard_map/ppermute | solution.py:64
  895.6 15.8 %collective-permute-start.49 = (bf16[128,1152]{1,0:T(8,128)(2,1)S(1)}, bf16[128,1152]{1,0:T(8,128)(2,1)S(1)}, u32[]{:S(2)}, u32[]{:S(2)}) collective-permute-start(bf16[128,1152]{1,0:T(8,128)(2,1)S(1)} %fusion.65), channel_id=1, source_target_pairs={{0,4},{1,5},{2,6},{3,7},{4,0},{5,1},{6,2},{7,3},{8,12},{9,13},{10,... | collective-permute-start | bytes 884744 | tf_op jit(solution)/shard_map/ppermute | solution.py:64
  911.7 16.1 %collective-permute-start.50 = (bf16[128,1152]{1,0:T(8,128)(2,1)S(1)}, bf16[128,1152]{1,0:T(8,128)(2,1)S(1)}, u32[]{:S(2)}, u32[]{:S(2)}) collective-permute-start(bf16[128,1152]{1,0:T(8,128)(2,1)S(1)} %get-tuple-element.59), channel_id=1, source_target_pairs={{0,4},{1,5},{2,6},{3,7},{4,0},{5,1},{6,2},{7,3},{8,12},{9,13},{10,... | collective-permute-start | bytes 884744 | tf_op jit(solution)/shard_map/ppermute | solution.py:64
  927.8 14.0 %collective-permute-start.51 = (bf16[256,1152]{1,0:T(8,128)(2,1)S(1)}, bf16[256,1152]{1,0:T(8,128)(2,1)S(1)}, u32[]{:S(2)}, u32[]{:S(2)}) collective-permute-start(bf16[256,1152]{1,0:T(8,128)(2,1)S(1)} %pad_maximum_fusion.11), channel_id=1, source_target_pairs={{0,2},{1,3},{2,0},{3,1},{4,6},{5,7},{6,4},{7,5},{8,10},{9,11},{10,... | collective-permute-start | bytes 1769480 | tf_op jit(solution)/shard_map/ppermute | solution.py:64
  941.8 18.2 %collective-permute-start.52 = (bf16[512,1152]{1,0:T(8,128)(2,1)S(1)}, bf16[512,1152]{1,0:T(8,128)(2,1)S(1)}, u32[]{:S(2)}, u32[]{:S(2)}) collective-permute-start(bf16[512,1152]{1,0:T(8,128)(2,1)S(1)} %bitcast.261), channel_id=1, source_target_pairs={{0,1},{1,0},{2,3},{3,2},{4,5},{5,4},{6,7},{7,6},{8,9},{9,8},{10,11... | collective-permute-start | bytes 3538952 | tf_op jit(solution)/shard_map/ppermute | solution.py:64
  (113 other events, 1523.0 us)
Sparse Core Ops, SparseCore 0:
  10.4 84.6 all-gather.3
  97.5 86.5 all-gather.5
  186.5 87.5 all-gather.7
  299.4 85.7 reduce-scatter.4
  409.9 86.2 reduce-scatter.6
  571.1 51.6 reduce-scatter.8
  643.6 56.9 reduce-scatter.10
